TPU v7x, 32 devices: a whole 2x2x4 slice. The times are simulated.
32 devices in a mesh: lat: 4 (over y, x), lon: 8 (over z, core).
Axes of the slice: x: 2, y: 2, z: 4, core: 2. Of those that a mesh axis runs over, the one named last changes fastest.
Arguments:
- features: bfloat16 [4, 24, 96, 192], P(None, 'lat', 'lon'), may hold values from -6 to 6
- norm_gain: float32 [192], replicated, may hold values from 0.5 to 1.5
- norm_shift: float32 [192], replicated, may hold values from -3 to 3
- w_qkv: bfloat16 [192, 576], replicated, may hold values from -0.4375 to 0.4375
- w_out: bfloat16 [192, 192], replicated, may hold values from -0.4375 to 0.4375
- bias_table: float32 [2, 4, 6, 3312], P(None, 'lat'), may hold values from -3 to 400
- index_table: int32 [144, 144], replicated, may hold values from 0 to 3311, as said below
- cotangent: bfloat16 [4, 24, 96, 192], P(None, 'lat', 'lon'), may hold values from -6 to 6
Outputs:
- outputs: bfloat16 [4, 24, 96, 192], P(None, 'lat', 'lon')
- grad_features: bfloat16 [4, 24, 96, 192], P(None, 'lat', 'lon')
- grad_gain: float32 [192], replicated
- grad_shift: float32 [192], replicated
- grad_wqkv: float32 [192, 576], replicated
- grad_wout: float32 [192, 192], replicated
- grad_table: float32 [2, 4, 6, 3312], P(None, 'lat')
Inputs may be any that keep to these rules, and one draw needn't show every extreme that they name: `index_table`: entry (i, j) labels the bias of tokens i and j of a window; two pairs share a label exactly when they have the same two levels, the same two rows and the same column difference.
All inputs are finite; a program needn't handle non-finite values.
Results may differ from a plain program's by a relative error of at most 0.018.
Values may be sent and summed in bfloat16 or wider, within the bound.
No kernel may reach another device: no remote copies, remote signals or barrier semaphores. Data moves between devices by JAX's collectives and lax.ppermute only.
A program may use at most 128 MiB of HBM per device.

v0:
```python
import jax
import jax.numpy as jnp
from jax import lax
from jax.sharding import PartitionSpec as P

HEADS = 6
WZ = 2
WH = 6
WW = 12
WIN = 144
POS = 3312


epsilon = 1e-05


def from_behind(value, axis, steps):
    count = lax.axis_size(axis)
    pairs = [(source, (source + steps) % count) for source in range(count)]
    return lax.ppermute(value, axis, pairs)


def normalize(features, norm_gain, norm_shift):
    values = features.astype(jnp.float32)
    center = values - jnp.mean(values, -1, keepdims=True)
    inv_std = lax.rsqrt(jnp.mean(center * center, -1, keepdims=True) + epsilon)
    x_hat = center * inv_std
    normed = (x_hat * norm_gain + norm_shift).astype(jnp.bfloat16)
    return (x_hat, inv_std, normed)


def norm_backward(grad_normed, x_hat, inv_std, norm_gain, cotangent):
    upstream = grad_normed.astype(jnp.float32)
    gain_part = jnp.sum(upstream * x_hat, (0, 1, 2))
    shift_part = jnp.sum(upstream, (0, 1, 2))
    g_hat = upstream * norm_gain
    centred = (
        g_hat
        - jnp.mean(g_hat, -1, keepdims=True)
        - x_hat * jnp.mean(g_hat * x_hat, -1, keepdims=True)
    )
    grad_features = (cotangent.astype(jnp.float32) + inv_std * centred).astype(jnp.bfloat16)
    return (grad_features, gain_part, shift_part)


def roll_cells(volume, direction):
    level_cut, lat_cut, lon_cut = (WZ // 2, WH // 2, WW // 2)
    levels, lat_rows, lon_cols = (volume.shape[0], volume.shape[1], volume.shape[2])
    if direction < 0:
        volume = jnp.concatenate((volume[level_cut:], volume[:level_cut]), 0)
        remain, edge_rows = (volume[:, lat_cut:], volume[:, :lat_cut])
    else:
        remain, edge_rows = (volume[:, : lat_rows - lat_cut], volume[:, lat_rows - lat_cut :])
    arrived = from_behind(edge_rows, "lat", direction)
    volume = jnp.concatenate((remain, arrived) if direction < 0 else (arrived, remain), 1)
    if direction < 0:
        remain, edge_cols = (volume[:, :, lon_cut:], volume[:, :, :lon_cut])
    else:
        remain, edge_cols = (volume[:, :, : lon_cols - lon_cut], volume[:, :, lon_cols - lon_cut :])
    arrived = from_behind(edge_cols, "lon", direction)
    volume = jnp.concatenate((remain, arrived) if direction < 0 else (arrived, remain), 2)
    if direction > 0:
        volume = jnp.concatenate((volume[levels - level_cut :], volume[: levels - level_cut]), 0)
    return volume


def blocks_of(volume, level_win, lat_win, lon_win):
    channels = volume.shape[-1]
    volume = volume.reshape(level_win, WZ, lat_win, WH, lon_win, WW, channels)
    volume = volume.transpose(2, 0, 4, 1, 3, 5, 6)
    return volume.reshape(lat_win, level_win * lon_win, WIN, channels)


def unblock(blocks, level_win, lat_win, lon_win):
    channels = blocks.shape[-1]
    blocks = blocks.reshape(lat_win, level_win, lon_win, WZ, WH, WW, channels)
    blocks = blocks.transpose(1, 3, 0, 4, 2, 5, 6)
    return blocks.reshape(level_win * WZ, lat_win * WH, lon_win * WW, channels)


def window_mask(lat_key, level_key, level_win, lat_win):
    grid_shape = (level_win, lat_win, WZ, WH, WW)
    per_level = jnp.broadcast_to(level_key.reshape(level_win, 1, WZ, 1, 1), grid_shape).reshape(
        level_win, lat_win, WIN
    )
    per_lat = jnp.broadcast_to(lat_key.reshape(1, lat_win, 1, WH, 1), grid_shape).reshape(
        level_win, lat_win, WIN
    )
    same_level = per_level[..., :, None] == per_level[..., None, :]
    same_lat = per_lat[..., :, None] == per_lat[..., None, :]
    return jnp.logical_and(same_level, same_lat)


def label_places(index_table):
    spans = 2 * WW - 1
    canon = jnp.arange(POS, dtype=jnp.int32)
    offset = canon % spans - (WW - 1)
    block = canon // spans
    lat_second = block % WH
    lat_first = block // WH % WH
    level_second = block // (WH * WH) % WZ
    level_first = block // (WH * WH * WZ)
    lon_first = jnp.maximum(offset, 0)
    lon_second = lon_first - offset
    token_first = (level_first * WH + lat_first) * WW + lon_first
    token_second = (level_second * WH + lat_second) * WW + lon_second
    return index_table[token_first, token_second]


def skew_table():
    first = jnp.arange(WW * WW, dtype=jnp.int32) // WW
    second = jnp.arange(WW * WW, dtype=jnp.int32) % WW
    target = first - second + WW - 1
    return (target[:, None] == jnp.arange(2 * WW - 1, dtype=jnp.int32)[None, :]).astype(jnp.float32)


def table_grad(score_grad, places, skew):
    groups = score_grad.shape[0]
    sixfold = score_grad.reshape(groups * HEADS, WZ, WH, WW, WZ, WH, WW).transpose(
        0, 1, 4, 2, 5, 3, 6
    )
    flat = sixfold.reshape(groups * HEADS * WZ * WZ * WH * WH, WW * WW)
    canonical = jnp.dot(
        flat, skew, preferred_element_type=jnp.float32, precision=lax.Precision.HIGHEST
    )
    canonical = canonical.reshape(groups * HEADS, POS)
    placed = jnp.zeros((groups * HEADS, POS), jnp.float32).at[:, places].set(canonical)
    return placed.reshape(groups, HEADS, POS)


def window_pass(inputs_win, grad_win, pos_bias, allowed, w_qkv, w_out):
    win_count, win_len, channels = inputs_win.shape
    level_win = pos_bias.shape[0]
    head_size = channels // HEADS
    scaling = head_size ** (-0.5)
    flat_in = inputs_win.reshape(win_count * win_len, channels)
    projected = jnp.dot(flat_in, w_qkv, preferred_element_type=jnp.float32)
    projected = projected.astype(jnp.bfloat16).reshape(win_count, win_len, 3, HEADS, head_size)
    query_part, key_part, value_part = (projected[:, :, 0], projected[:, :, 1], projected[:, :, 2])
    logits = (
        jnp.einsum("bihe,bjhe->bhij", query_part, key_part, preferred_element_type=jnp.float32)
        * scaling
    )
    logits = (
        logits.reshape(level_win, win_count // level_win, HEADS, win_len, win_len)
        + pos_bias[:, None]
    )
    logits = jnp.where(allowed[:, None, None], logits, -jnp.inf)
    row_max = jnp.max(logits, -1, keepdims=True)
    raised = jnp.exp(logits - row_max)
    weights_f32 = (raised / jnp.sum(raised, -1, keepdims=True)).reshape(
        win_count, HEADS, win_len, win_len
    )
    weights_bf = weights_f32.astype(jnp.bfloat16)
    mixed = jnp.einsum(
        "bhij,bjhe->bihe", weights_bf, value_part, preferred_element_type=jnp.float32
    )
    mixed = mixed.astype(jnp.bfloat16).reshape(win_count * win_len, channels)
    attn_out = jnp.dot(mixed, w_out, preferred_element_type=jnp.float32).astype(jnp.bfloat16)
    grad_flat = grad_win.reshape(win_count * win_len, channels)
    grad_wout = jnp.dot(mixed.T, grad_flat, preferred_element_type=jnp.float32)
    grad_heads = jnp.dot(grad_flat, w_out.T, preferred_element_type=jnp.float32).astype(
        jnp.bfloat16
    )
    grad_heads = grad_heads.reshape(win_count, win_len, HEADS, head_size)
    grad_weights = jnp.einsum(
        "bihe,bjhe->bhij", grad_heads, value_part, preferred_element_type=jnp.float32
    )
    grad_value = jnp.einsum(
        "bhij,bihe->bjhe", weights_bf, grad_heads, preferred_element_type=jnp.float32
    ).astype(jnp.bfloat16)
    grad_logits = weights_f32 * (
        grad_weights - jnp.sum(weights_f32 * grad_weights, -1, keepdims=True)
    )
    logit_bf = grad_logits.astype(jnp.bfloat16)
    grad_query = (
        jnp.einsum("bhij,bjhe->bihe", logit_bf, key_part, preferred_element_type=jnp.float32)
        * scaling
    ).astype(jnp.bfloat16)
    grad_key = (
        jnp.einsum("bhij,bihe->bjhe", logit_bf, query_part, preferred_element_type=jnp.float32)
        * scaling
    ).astype(jnp.bfloat16)
    grad_proj = jnp.stack((grad_query, grad_key, grad_value), 2).reshape(
        win_count * win_len, 3 * channels
    )
    grad_wqkv = jnp.dot(flat_in.T, grad_proj, preferred_element_type=jnp.float32)
    grad_input = jnp.dot(grad_proj, w_qkv.T, preferred_element_type=jnp.float32).astype(
        jnp.bfloat16
    )
    return (
        attn_out.reshape(win_count, win_len, channels),
        grad_input.reshape(win_count, win_len, channels),
        grad_wqkv,
        grad_wout,
        grad_logits,
    )


def on_device(features, norm_gain, norm_shift, w_qkv, w_out, bias_table, index_table, cotangent):
    levels, lat_rows, lon_cols, channels = features.shape
    level_win, lat_win, lon_win = (levels // WZ, lat_rows // WH, lon_cols // WW)
    x_hat, inv_std, normed = normalize(features, norm_gain, norm_shift)
    shifted = roll_cells(normed, -1)
    grad_blocks = blocks_of(roll_cells(cotangent, -1), level_win, lat_win, lon_win)
    lat_total = lat_rows * lax.axis_size("lat")
    lat_index = lax.axis_index("lat") * lat_rows + jnp.arange(lat_rows, dtype=jnp.int32)
    lat_key = (lat_index >= lat_total - WH // 2).astype(jnp.int32)
    level_key = (jnp.arange(levels, dtype=jnp.int32) >= levels - WZ // 2).astype(jnp.int32)
    allowed = window_mask(lat_key, level_key, level_win, lat_win).transpose(1, 0, 2, 3)
    pos_bias = jnp.take(bias_table, index_table, axis=3).transpose(1, 0, 2, 3, 4)
    input_blocks = blocks_of(shifted, level_win, lat_win, lon_win)
    places = label_places(index_table)
    skew = skew_table()

    def window_row(inputs):
        attn_out, grad_input, grad_wqkv, grad_wout, grad_logits = window_pass(
            inputs[0], inputs[1], inputs[2], inputs[3], w_qkv, w_out
        )
        summed = jnp.sum(grad_logits.reshape(level_win, lon_win, HEADS, WIN, WIN), 1)
        return (attn_out, grad_input, grad_wqkv, grad_wout, table_grad(summed, places, skew))

    attn_blocks, grad_input, wqkv_rows, wout_rows, table_rows = lax.map(
        window_row, (input_blocks, grad_blocks, pos_bias, allowed)
    )
    attn = roll_cells(unblock(attn_blocks, level_win, lat_win, lon_win), 1)
    outputs = (features.astype(jnp.float32) + attn.astype(jnp.float32)).astype(jnp.bfloat16)
    grad_normed = roll_cells(unblock(grad_input, level_win, lat_win, lon_win), 1)
    grad_features, grad_gain, grad_shift = norm_backward(
        grad_normed, x_hat, inv_std, norm_gain, cotangent
    )
    grad_wqkv = jnp.sum(wqkv_rows, 0)
    grad_wout = jnp.sum(wout_rows, 0)
    grad_table = table_rows.transpose(1, 0, 2, 3)
    grad_table, grad_wqkv, grad_wout, grad_gain, grad_shift = (
        lax.psum(grad_table.astype(jnp.bfloat16), "lon").astype(jnp.float32),
        lax.psum(grad_wqkv.astype(jnp.bfloat16), "lon").astype(jnp.float32),
        lax.psum(grad_wout.astype(jnp.bfloat16), "lon").astype(jnp.float32),
        lax.psum(grad_gain.astype(jnp.bfloat16), "lon").astype(jnp.float32),
        lax.psum(grad_shift.astype(jnp.bfloat16), "lon").astype(jnp.float32),
    )
    grad_wqkv, grad_wout, grad_gain, grad_shift = (
        lax.psum(grad_wqkv.astype(jnp.bfloat16), "lat").astype(jnp.float32),
        lax.psum(grad_wout.astype(jnp.bfloat16), "lat").astype(jnp.float32),
        lax.psum(grad_gain.astype(jnp.bfloat16), "lat").astype(jnp.float32),
        lax.psum(grad_shift.astype(jnp.bfloat16), "lat").astype(jnp.float32),
    )
    factor = (levels * lat_total * lon_cols * lax.axis_size("lon")) ** (-0.5)
    return (
        outputs,
        grad_features,
        grad_gain * factor,
        grad_shift * factor,
        grad_wqkv * factor,
        grad_wout * factor,
        grad_table * factor,
    )


def solution(mesh):
    placed = (
        P(None, "lat", "lon", None),
        P(),
        P(),
        P(),
        P(),
        P(None, "lat", None, None),
        P(),
        P(None, "lat", "lon", None),
    )
    return jax.shard_map(
        on_device,
        mesh=mesh,
        in_specs=placed,
        out_specs=(
            P(None, "lat", "lon", None),
            P(None, "lat", "lon", None),
            P(),
            P(),
            P(),
            P(),
            P(None, "lat", None, None),
        ),
        check_vma=False,
    )
```

profile of v0, /device:TPU:0, one launch (start us, length us, event | category | flops | bytes accessed | tf_op | source)
XLA Modules:
  0.0 348.5 jit_solution(8264107106497406919)
XLA Ops:
  7.2 1.1 slice.99
  8.4 1.0 slice.100
  9.5 3.9 %collective-permute-start.4 = (bf16[4,3,12,192]{3,0,2,1:T(4,128)(2,1)S(1)}, bf16[4,3,12,192]{3,0,2,1:T(4,128)(2,1)S(1)}, u32[]{:S(2)}, u32[]{:S(2)}) collective-permute-start(bf16[4,3,12,192]{3,0,2,1:T(4,128)(2,1)S(1)} %get-tuple-element.83), channel_id=1, source_target_pairs={{0,24},{8,0},{16,8},{24,16},{1,25},{9,1},{17,9},{25,17},{2,26},{10... | collective-permute-start | bytes 165896 | tf_op jit(solution)/shard_map/ppermute | solution.py:20
  13.5 1.0 convert_reduce_fusion
  14.5 1.1 fusion.27
  15.7 1.1 fusion.22
  16.9 0.6 collective-permute-start
  17.5 0.6 fusion.57
  18.6 0.8 compare_and_fusion
  19.4 0.5 fusion.53
  19.9 3.5 copy.93
  23.3 58.9 %gather_fusion = f32[20736,2,6]{2,1,0:T(2,128)} fusion(f32[2,6,3312]{1,0,2:T(2,128)} %bitcast.65, s32[21504]{0:T(1024)S(1)} %pad_clamp_fusion), kind=kCustom, calls=%fused_computation | custom fusion | bytes 2073600 | tf_op jit(solution)/shard_map/jit(_take)/gather | solution.py:211
  82.2 30.0 %copy.68 = f32[144,144,2,6]{0,1,3,2:T(8,128)S(1)} copy(f32[144,144,2,6]{3,2,1,0:T(2,128)} %bitcast.64) | data formatting | bytes 1990656 | tf_op jit(solution)/shard_map/jit(_take)/gather | solution.py:211
  112.2 0.7 copy.64
  113.0 41.2 %gather_fusion.1 = s32[3312]{0:T(1024)S(1)} fusion(s32[144,144]{1,0:T(8,128)S(1)} %copy-done.2, s32[3312]{0:T(1024)S(1)} %fusion.53), kind=kCustom, calls=%fused_computation.1 | custom fusion | bytes 52992 | tf_op jit(solution)/shard_map/gather | solution.py:107
  154.4 2.5 collective-permute-start.5
  157.0 1.5 collective-permute-start.1
  158.5 0.5 collective-permute-done.5
  159.5 0.8 reshape.445
  160.3 0.4 collective-permute-done.1
  160.9 0.3 convolution_convert_fusion
  161.1 0.2 copy.60
  161.6 1.2 fusion.60
  162.8 0.6 fusion.1
  163.4 1.8 fusion.63
  165.2 3.2 fusion.5
  168.4 0.5 multiply_reduce_fusion
  168.9 1.9 subtract_multiply_fusion
  170.8 0.4 fusion.6
  171.2 0.3 fusion.7
  171.5 3.3 fusion.4
  174.9 0.6 copy.79
  175.5 0.3 reshape.446
  175.8 0.3 convolution_convert_fusion.4
  176.2 1.1 convolution_convert_fusion.1
  177.6 0.2 convolution_convert_fusion.6
  177.8 0.8 convolution_convert_fusion.7
  178.7 1.9 copy.80
  180.7 1.5 collective-permute-start.6
  182.3 0.8 collective-permute-start.2
  183.1 10.1 %reshape.447 = f32[12,2,6,12,2,6,12]{6,5,4,3,2,1,0:T(8,128)} reshape(f32[2,6,144,144]{3,2,1,0:T(8,128)} %copy.80) | data formatting | bytes 1990656 | tf_op jit(solution)/shard_map/while/body/eval_jaxpr/reshape | solution.py:119
  193.2 14.1 %copy.81 = f32[12,2,2,6,6,12,12]{6,5,4,3,2,1,0:T(8,128)} copy(f32[12,2,2,6,6,12,12]{6,4,2,5,3,1,0:T(8,128)} %bitcast.63) | data formatting | bytes 1990656 | tf_op jit(solution)/shard_map/while/body/eval_jaxpr/transpose | solution.py:119
  207.3 9.3 %reshape.448 = f32[1728,144]{1,0:T(8,128)S(1)} reshape(f32[12,2,2,6,6,12,12]{6,5,4,3,2,1,0:T(8,128)} %copy.81) | data formatting | bytes 1990656 | tf_op jit(solution)/shard_map/while/body/eval_jaxpr/reshape | solution.py:122
  216.6 1.0 fusion.41
  217.6 0.4 reshape.467
  218.0 1.7 copy.83
  219.7 13.9 %scatter_custom_fusion = f32[12,3312]{0,1:T(8,128)S(1)} fusion(s32[3312]{0:T(1024)S(1)} %fusion.46, f32[3312,12]{1,0:T(8,128)} %copy.83, f32[]{:T(128)} %constant.144.clone.1), kind=kCustom, calls=%fused_computation.26 | custom fusion | bytes 159488 | tf_op jit(solution)/shard_map/while/body/eval_jaxpr/scatter | solution.py:127
  233.7 0.5 copy.84
  234.2 0.7 convert_element_type.167
  235.2 5.7 %collective-permute-done.7 = bf16[4,6,6,192]{3,2,1,0:T(8,128)(2,1)S(1)} collective-permute-done((bf16[4,6,6,192]{3,2,1,0:T(8,128)(2,1)S(1)}, bf16[4,6,6,192]{3,2,1,0:T(8,128)(2,1)S(1)}, u32[]{:S(2)}, u32[]{:S(2)}) %collective-permute-start.7) | collective-permute-done | bytes 55328 | tf_op jit(solution)/shard_map/ppermute | solution.py:20
  241.1 0.4 fusion.29
  241.5 0.5 collective-permute-done.3
  242.0 0.3 fusion.26
  242.3 0.8 copy.85
  243.1 0.8 copy.86
  243.9 13.7 %all-reduce = (bf16[192]{0:T(256)(128)(2,1)S(1)}, bf16[192]{0:T(256)(128)(2,1)S(1)}) all-reduce(bf16[192]{0:T(256)(128)(2,1)S(1)} %get-tuple-element.63, bf16[192]{0:T(256)(128)(2,1)S(1)} %reduce_sum.107), channel_id=1, replica_groups=mesh['lat'=4,'lon'=8] {'lon'}, use_global_device_ids=true, to_apply=%region_8.9 | all-reduce | flops 384 | bytes 1536 | tf_op jit(solution)/shard_map/psum | solution.py:239
  257.5 9.8 %all-reduce.2 = (bf16[192]{0:T(256)(128)(2,1)S(1)}, bf16[192]{0:T(256)(128)(2,1)S(1)}) all-reduce(bf16[192]{0:T(256)(128)(2,1)S(1)} %get-tuple-element.66, bf16[192]{0:T(256)(128)(2,1)S(1)} %get-tuple-element.67), channel_id=1, replica_groups=mesh['lat'=4,'lon'=8] {'lat'}, use_global_device_ids=true, to_apply=%region_9.10 | all-reduce | flops 384 | bytes 1536 | tf_op jit(solution)/shard_map/psum | solution.py:245
  267.4 0.6 convert_multiply_fusion.5
  267.9 23.9 %all-reduce.7.cloned.1.call-done = (bf16[192,576]{1,0:T(8,128)(2,1)}, bf16[192,192]{1,0:T(8,128)(2,1)}, bf16[2,1,6,3312]{3,2,0,1:T(8,128)(2,1)}) async-done(((bf16[192,576]{1,0:T(8,128)(2,1)}, bf16[192,192]{1,0:T(8,128)(2,1)}, bf16[2,1,6,3312]{3,2,0,1:T(8,128)(2,1)}), (bf16[192,576]{1,0:T(8,128)(2,1)}, bf16[192,192]{1,0:T(8,128)(2,1)}, bf16[2,1,6,3312]{3,2,0,1:T(8,128)(2,1)})) %all-reduce.7.cloned.1.call-update) | async-done | bytes 374416 | tf_op jit(solution)/shard_map/psum | solution.py:237
  291.9 0.9 convert_multiply_fusion.3
  292.8 0.8 copy.87
  293.6 44.6 %all-reduce.9.cloned.1.call-done = (bf16[192,576]{1,0:T(8,128)(2,1)}, bf16[192,192]{1,0:T(8,128)(2,1)}) async-done(((bf16[192,576]{1,0:T(8,128)(2,1)}, bf16[192,192]{1,0:T(8,128)(2,1)}), (bf16[192,576]{1,0:T(8,128)(2,1)}, bf16[192,192]{1,0:T(8,128)(2,1)})) %all-reduce.9.cloned.1.call-update) | async-done | bytes 294928 | tf_op jit(solution)/shard_map/psum | solution.py:243
  338.3 1.8 convert_multiply_fusion
  340.1 1.6 convert_multiply_fusion.4
  (84 shorter events, 3.1 us)
Async XLA Ops:
  7.2 153.7 %copy-start = (bf16[192,576]{1,0:T(8,128)(2,1)S(1)}, bf16[192,576]{1,0:T(8,128)(2,1)}, u32[]{:S(2)}) copy-start(bf16[192,576]{1,0:T(8,128)(2,1)} %param.11) | copy-start | bytes 663556
  7.2 10.3 %copy-start.2 = (s32[144,144]{1,0:T(8,128)S(1)}, s32[144,144]{1,0:T(8,128)}, u32[]{:S(2)}) copy-start(s32[144,144]{1,0:T(8,128)} %param.14) | copy-start | bytes 248836
  7.2 12.7 %copy-start.13 = (f32[2,1,6,3312]{3,1,2,0:T(1,128)S(1)}, f32[2,1,6,3312]{3,1,2,0:T(1,128)}, u32[]{:S(2)}) copy-start(f32[2,1,6,3312]{3,1,2,0:T(1,128)} %param.13) | copy-start | bytes 476932
  7.2 284.7 %all-reduce.7.cloned.1.call-start = ((), (), s32[]{:S(2)}) async-start(), calls=%async_computation | async-start | bytes 901120 | tf_op jit(solution)/shard_map/psum | solution.py:237
  9.5 144.8 %collective-permute-start.4 = (bf16[4,3,12,192]{3,0,2,1:T(4,128)(2,1)S(1)}, bf16[4,3,12,192]{3,0,2,1:T(4,128)(2,1)S(1)}, u32[]{:S(2)}, u32[]{:S(2)}) collective-permute-start(bf16[4,3,12,192]{3,0,2,1:T(4,128)(2,1)S(1)} %get-tuple-element.83), channel_id=1, source_target_pairs={{0,24},{8,0},{16,8},{24,16},{1,25},{9,1},{17,9},{25,17},{2,26},{10... | collective-permute-start | bytes 165896 | tf_op jit(solution)/shard_map/ppermute | solution.py:20
  16.9 140.1 %collective-permute-start = (bf16[4,3,12,192]{3,2,1,0:T(8,128)(2,1)S(1)}, bf16[4,3,12,192]{3,2,1,0:T(8,128)(2,1)S(1)}, u32[]{:S(2)}, u32[]{:S(2)}) collective-permute-start(bf16[4,3,12,192]{3,2,1,0:T(8,128)(2,1)S(1)} %get-tuple-element.91), channel_id=1, source_target_pairs={{0,24},{8,0},{16,8},{24,16},{1,25},{9,1},{17,9},{25,17},{2,26},{10... | collective-permute-start | bytes 165896 | tf_op jit(solution)/shard_map/ppermute | solution.py:20
  154.2 4.9 %copy-start.7 = (bf16[192,192]{1,0:T(8,128)(2,1)S(1)}, bf16[192,192]{1,0:T(8,128)(2,1)}, u32[]{:S(2)}) copy-start(bf16[192,192]{1,0:T(8,128)(2,1)} %param.12) | copy-start | bytes 221188
  154.4 4.5 %collective-permute-start.5 = (bf16[4,6,6,192]{3,0,2,1:T(4,128)(2,1)S(1)}, bf16[4,6,6,192]{3,0,2,1:T(4,128)(2,1)S(1)}, u32[]{:S(2)}, u32[]{:S(2)}) collective-permute-start(bf16[4,6,6,192]{3,0,2,1:T(4,128)(2,1)S(1)} %get-tuple-element.95), channel_id=1, source_target_pairs={{0,7},{1,0},{2,1},{3,2},{4,3},{5,4},{6,5},{7,6},{8,15},{9,8},{10,9... | collective-permute-start | bytes 165896 | tf_op jit(solution)/shard_map/ppermute | solution.py:20
  157.0 3.7 %collective-permute-start.1 = (bf16[4,6,6,192]{3,2,1,0:T(8,128)(2,1)S(1)}, bf16[4,6,6,192]{3,2,1,0:T(8,128)(2,1)S(1)}, u32[]{:S(2)}, u32[]{:S(2)}) collective-permute-start(bf16[4,6,6,192]{3,2,1,0:T(8,128)(2,1)S(1)} %get-tuple-element.89), channel_id=1, source_target_pairs={{0,7},{1,0},{2,1},{3,2},{4,3},{5,4},{6,5},{7,6},{8,15},{9,8},{10,9... | collective-permute-start | bytes 165896 | tf_op jit(solution)/shard_map/ppermute | solution.py:20
  160.8 2.0 copy-start.9
  160.9 2.0 copy-start.14
  163.4 1.8 copy-start.3
  163.4 1.8 copy-start.12
  165.2 3.2 copy-start.4
  165.2 3.2 copy-start.10
  175.5 2.1 copy-start.8
  175.8 1.4 copy-start.11
  180.7 54.3 %collective-permute-start.6 = (bf16[4,3,12,192]{3,2,1,0:T(8,128)(2,1)S(1)}, bf16[4,3,12,192]{3,2,1,0:T(8,128)(2,1)S(1)}, u32[]{:S(2)}, u32[]{:S(2)}) collective-permute-start(bf16[4,3,12,192]{3,2,1,0:T(8,128)(2,1)S(1)} %get-tuple-element.84), channel_id=1, source_target_pairs={{0,8},{8,16},{16,24},{24,0},{1,9},{9,17},{17,25},{25,1},{2,10},{10... | collective-permute-start | bytes 165896 | tf_op jit(solution)/shard_map/ppermute | solution.py:20
  182.3 52.8 %collective-permute-start.2 = (bf16[4,3,12,192]{3,2,1,0:T(8,128)(2,1)S(1)}, bf16[4,3,12,192]{3,2,1,0:T(8,128)(2,1)S(1)}, u32[]{:S(2)}, u32[]{:S(2)}) collective-permute-start(bf16[4,3,12,192]{3,2,1,0:T(8,128)(2,1)S(1)} %get-tuple-element.87), channel_id=1, source_target_pairs={{0,8},{8,16},{16,24},{24,0},{1,9},{9,17},{17,25},{25,1},{2,10},{10... | collective-permute-start | bytes 165896 | tf_op jit(solution)/shard_map/ppermute | solution.py:20
  207.3 9.3 %copy-start.16 = (s32[144]{0:T(256)S(1)}, s32[144]{0:T(256)}, u32[]{:S(2)}) copy-start(s32[144]{0:T(256)} %fusion.57) | copy-start | bytes 1732
  233.6 7.4 %copy-start.5 = (bf16[4,6,12,192]{3,0,2,1:T(4,128)(2,1)S(1)}, bf16[4,6,12,192]{3,0,2,1:T(4,128)(2,1)}, u32[]{:S(2)}) copy-start(bf16[4,6,12,192]{3,0,2,1:T(4,128)(2,1)} %param.8) | copy-start | bytes 331780
  233.6 7.4 %copy-start.15 = (f32[192]{0:T(256)S(1)}, f32[192]{0:T(256)}, u32[]{:S(2)}) copy-start(f32[192]{0:T(256)} %param.9) | copy-start | bytes 2308
  233.7 8.3 %copy-start.6 = (bf16[4,6,12,192]{3,0,2,1:T(4,128)(2,1)S(1)}, bf16[4,6,12,192]{3,0,2,1:T(4,128)(2,1)}, u32[]{:S(2)}) copy-start(bf16[4,6,12,192]{3,0,2,1:T(4,128)(2,1)} %param.15) | copy-start | bytes 331780
  234.9 103.4 %all-reduce.9.cloned.1.call-start = ((), (), s32[]{:S(2)}) async-start(), calls=%async_computation.1 | async-start | bytes 688128 | tf_op jit(solution)/shard_map/psum | solution.py:243
  235.0 5.9 %collective-permute-start.7 = (bf16[4,6,6,192]{3,2,1,0:T(8,128)(2,1)S(1)}, bf16[4,6,6,192]{3,2,1,0:T(8,128)(2,1)S(1)}, u32[]{:S(2)}, u32[]{:S(2)}) collective-permute-start(bf16[4,6,6,192]{3,2,1,0:T(8,128)(2,1)S(1)} %fusion.35), channel_id=1, source_target_pairs={{0,1},{1,2},{2,3},{3,4},{4,5},{5,6},{6,7},{7,0},{8,9},{9,10},{10,1... | collective-permute-start | bytes 165896 | tf_op jit(solution)/shard_map/ppermute | solution.py:20
  235.2 6.8 %collective-permute-start.3 = (bf16[4,6,6,192]{3,2,1,0:T(8,128)(2,1)S(1)}, bf16[4,6,6,192]{3,2,1,0:T(8,128)(2,1)S(1)}, u32[]{:S(2)}, u32[]{:S(2)}) collective-permute-start(bf16[4,6,6,192]{3,2,1,0:T(8,128)(2,1)S(1)} %fusion.36), channel_id=1, source_target_pairs={{0,1},{1,2},{2,3},{3,4},{4,5},{5,6},{6,7},{7,0},{8,9},{9,10},{10,1... | collective-permute-start | bytes 165896 | tf_op jit(solution)/shard_map/ppermute | solution.py:20
  242.0 99.7 %copy-start.1 = (bf16[192,576]{1,0:T(8,128)(2,1)S(1)}, bf16[192,576]{1,0:T(8,128)(2,1)}, u32[]{:S(2)}) copy-start(bf16[192,576]{1,0:T(8,128)(2,1)} %param.11) | copy-start | bytes 663556
Sparse Core Ops, SparseCore 0:
  235.0 56.7 all-reduce.6
  295.2 43.0 all-reduce.8
where the time goes:
time: 350 us; the launch traced here: 348 us
  local copies, waits for them, and re-layouts  196 us (56%)
  waiting for transfers between devices  75.6 us (22%)
  blocking collectives  23.5 us (7%)
  other arithmetic  15.4 us (4%)
  between operations  14.7 us (4%)
  matrix products  12.1 us (3%)
  starting transfers between devices  11 us (3%)
    gather x2, local copies, waits for them, and re-layouts, on_device(): jnp.take(bias_table, index_table, axis=3).transpose(1, 0, 2, 3, 4)  88.9 us
    psum x1, waiting for transfers between devices, on_device(): lax.psum(grad_wqkv.astype(jnp.bfloat16), 'lat').astype(jnp.float32)  44.6 us
    gather x1, local copies, waits for them, and re-layouts, label_places(): return index_table[token_first, token_second]  41.2 us
    psum x1, waiting for transfers between devices, on_device(): lax.psum(grad_wqkv.astype(jnp.bfloat16), 'lon').astype(jnp.float32)  23.9 us
    scatter x2, local copies, waits for them, and re-layouts, table_grad(): jnp.zeros((groups * HEADS, POS), jnp.float32).at[:, places].set(canonical)  14.4 us
    transpose x1, local copies, waits for them, and re-layouts, table_grad(): score_grad.reshape(groups * HEADS, WZ, WH, WW, WZ, WH, WW)  14.1 us
    psum x1, blocking collectives, on_device(): lax.psum(grad_gain.astype(jnp.bfloat16), 'lon').astype(jnp.float32)  13.7 us
    ppermute x8, starting transfers between devices, from_behind(): return lax.ppermute(value, axis, pairs)  10.9 us
  transfers between devices with their start and end apart: 10, of which 6 were waited for; matrix products, arithmetic and copies ran while one was open for 57% of the time, Pallas kernels for 0%

commit v1 on v0

v1 whole, which is shorter than its diff:
```python
import functools

import jax
import jax.numpy as jnp
import numpy as np
from jax import lax
from jax.experimental import pallas as pl
from jax.experimental.pallas import tpu as pltpu
from jax.sharding import PartitionSpec as P

HEADS = 6
WZ = 2
WH = 6
WW = 12
BLOCK = WZ * WH
WIN = BLOCK * WW
SPANS = 2 * WW - 1
SPREAD = 384
LANES = 128
PAD_LON = 16
PAD_QUAD = 80
LARGE = 1e30

epsilon = 1e-05

f32, bf16 = jnp.float32, jnp.bfloat16


def call(body, outs, scratch=(), flops=0, moved=0, **kwargs):
    return pl.pallas_call(
        body,
        out_shape=outs,
        scratch_shapes=list(scratch),
        compiler_params=pltpu.CompilerParams(vmem_limit_bytes=48 * 1024 * 1024),
        cost_estimate=pl.CostEstimate(flops=flops, bytes_accessed=moved, transcendentals=0),
        **kwargs,
    )


def struct(shape, dtype):
    return jax.ShapeDtypeStruct(shape, dtype)


def quadrants(levels, lat_rows, lon_cols):
    lat_cut, lon_cut = WH // 2, WW // 2
    high_lat, low_lat = range(lat_cut, lat_rows), range(lat_cut)
    high_lon, low_lon = range(lon_cut, lon_cols), range(lon_cut)
    return (high_lat, high_lon), (high_lat, low_lon), (low_lat, high_lon), (low_lat, low_lon)


def pack_matrix(levels, lat_rows, lon_cols):
    picks = np.zeros((4 * PAD_QUAD, levels * lat_rows * PAD_LON), np.float32)
    for q, (rows, cols) in enumerate(quadrants(levels, lat_rows, lon_cols)):
        at = q * PAD_QUAD
        for z in range(levels):
            for a in rows:
                for o in cols:
                    picks[at, (z * lat_rows + a) * PAD_LON + o] = 1
                    at += 1
    return jnp.asarray(picks, bf16)


def window_matrix(levels, lat_rows, lon_cols):
    lat_cut, lon_cut, level_cut = WH // 2, WW // 2, WZ // 2
    picks = np.zeros((levels // WZ * WIN, 4 * PAD_QUAD), np.float32)
    for q, (rows, cols) in enumerate(quadrants(levels, lat_rows, lon_cols)):
        at = q * PAD_QUAD
        for z in range(levels):
            for a in rows:
                for o in cols:
                    level = (z - level_cut) % levels
                    lat = (a - lat_cut) % lat_rows
                    lon = (o - lon_cut) % lon_cols
                    token = lon * BLOCK + level % WZ * WH + lat
                    picks[level // WZ * WIN + token, at] = 1
                    at += 1
    return jnp.asarray(picks, bf16)


def spread_matrices():
    last, first = np.zeros((2, WIN, SPREAD), np.float32)
    for span in range(SPANS):
        for cell in range(BLOCK):
            if span < WW - 1:
                last[cell * WW + span, span * BLOCK + cell] = 1
            else:
                first[cell * WW + span - (WW - 1), span * BLOCK + cell] = 1
    return jnp.asarray(last, bf16), jnp.asarray(first, bf16)


def apart():
    cell = np.arange(16)[:, None] % BLOCK
    other = np.arange(SPREAD)[None, :] % BLOCK
    level = (cell // WH >= WZ // 2) != (other // WH >= WZ // 2)
    row = (cell % WH >= WH // 2) != (other % WH >= WH // 2)
    return jnp.asarray(level, f32), jnp.asarray(row, f32)


def pack_body(features, cotangent, picks, *outs):
    levels, lat_rows, lon_cols, width = features.shape
    for at, ref in enumerate((features, cotangent)):
        cells = ref[...].astype(f32)
        fill = jnp.zeros((levels, lat_rows, PAD_LON - lon_cols, width), f32)
        cells = jnp.concatenate((cells, fill), 2).reshape(levels * lat_rows * PAD_LON, width)
        packed = jnp.dot(picks[...], cells.astype(bf16), preferred_element_type=f32).astype(bf16)
        for q, out in enumerate(outs):
            out[:, at * width : (at + 1) * width] = packed[q * PAD_QUAD : (q + 1) * PAD_QUAD]


def unpack_body(here, from_lon, from_lat, from_both, picks, outputs, grad_features):
    levels, lat_rows, lon_cols, width = outputs.shape
    for at, ref in enumerate((outputs, grad_features)):
        part = slice(at * width, (at + 1) * width)
        quads = jnp.concatenate([q[:, part] for q in (here, from_lon, from_lat, from_both)], 0)
        cells = lax.dot_general(
            picks[...], quads, (((0,), (0,)), ((), ())), preferred_element_type=f32
        )
        ref[...] = cells.reshape(levels, lat_rows, PAD_LON, width)[:, :, :lon_cols].astype(bf16)


def spread_index(index_table, last, first):
    parts = []
    rows = [
        jnp.concatenate([index_table[c * WW + a : c * WW + a + 1, :] for c in range(BLOCK)], 0)
        for a in (WW - 1, 0)
    ]
    fill = jnp.zeros((16 - BLOCK, WIN), f32)
    for cut in (lambda v: v // LANES, lambda v: v % LANES):
        total = jnp.zeros((16, SPREAD), f32)
        for labels, picks in zip(rows, (last, first)):
            value = jnp.concatenate((cut(labels).astype(f32), fill), 0).astype(bf16)
            total += jnp.dot(value, picks[...], preferred_element_type=f32)
        parts.append(total.astype(jnp.int32))
    return parts


def bias_body(bias_table, index_table, last, first, level_apart, row_apart, out, chunk_out, lane_out, table):
    level_win, _, heads, labels = bias_table.shape
    chunk, lane = spread_index(index_table, last, first)
    chunk_out[...] = chunk
    lane_out[...] = lane
    chunks = -(-labels // LANES)
    for t in range(level_win):
        table[8 * t : 8 * t + heads, :labels] = bias_table[t, 0]
    top = lax.axis_index("lat") == lax.axis_size("lat") - 1
    barred_rows = jnp.logical_and(row_apart[...] > 0, top)
    for t in range(level_win):
        barred = barred_rows
        if t == level_win - 1:
            barred = jnp.logical_or(barred, level_apart[...] > 0)
        for h in range(heads):
            row = 8 * t + h
            tiles = []
            for tile in range(SPREAD // LANES):
                at = slice(tile * LANES, (tile + 1) * LANES)
                found = jnp.zeros((16, LANES), f32)
                for c in range(chunks):
                    source = jnp.broadcast_to(
                        table[row : row + 1, c * LANES : (c + 1) * LANES], (16, LANES)
                    )
                    taken = jnp.take_along_axis(source, lane[:, at], axis=1, mode="promise_in_bounds")
                    found = jnp.where(chunk[:, at] == c, taken, found)
                tiles.append(found)
            value = jnp.where(barred, -LARGE, jnp.concatenate(tiles, 1))
            for a in range(WW):
                shift = (WW - 1 - a) * BLOCK
                out[t * heads + h, a * BLOCK : (a + 1) * BLOCK, :] = value[
                    :BLOCK, shift : shift + WIN
                ]


def inverse_body(chunk, lane, chunk_out, lane_out):
    pieces = SPREAD // LANES
    labels = chunk_out.shape[0]
    valid = SPANS * BLOCK
    total = jnp.zeros((2 * labels, LANES), f32)
    wide = lax.broadcasted_iota(jnp.int32, (labels, SPREAD), 1)
    tall = lax.broadcasted_iota(jnp.int32, (labels, SPREAD), 0)
    lanes = lax.broadcasted_iota(jnp.int32, (LANES, SPREAD), 0)
    for cell in range(BLOCK):
        own = jnp.logical_and(chunk[cell : cell + 1, :] == tall, wide < valid)
        piece = jnp.where(own, (cell * pieces + wide // LANES).astype(f32), 0.0)
        spot = jnp.where(own, (wide % LANES).astype(f32), 0.0)
        both = jnp.concatenate((piece, spot), 0).astype(bf16)
        hit = jnp.where(lane[cell : cell + 1, :] == lanes, 1.0, 0.0).astype(bf16)
        total += lax.dot_general(both, hit, (((1,), (1,)), ((), ())), preferred_element_type=f32)
    chunk_out[...] = total[:labels].astype(jnp.int32)
    lane_out[...] = total[labels:].astype(jnp.int32)


def place_body(blocks, piece, spot, out):
    count, rows, _ = blocks.shape
    per = rows // BLOCK
    pieces = SPREAD // LANES
    chunks = piece.shape[0]
    at_piece = [jnp.broadcast_to(piece[c : c + 1, :], (8, LANES)) for c in range(out.shape[1] // LANES)]
    at_spot = [jnp.broadcast_to(spot[c : c + 1, :], (8, LANES)) for c in range(out.shape[1] // LANES)]
    found = [jnp.zeros((8, LANES), f32) for _ in at_piece]
    values = [blocks[b].astype(f32) for b in range(count)]
    for cell in range(BLOCK):
        for tile in range(pieces):
            source = jnp.concatenate(
                [
                    values[h // per * pieces + tile][h % per * BLOCK + cell : h % per * BLOCK + cell + 1]
                    for h in range(HEADS)
                ]
                + [jnp.zeros((8 - HEADS, LANES), f32)],
                0,
            )
            for c in range(len(found)):
                taken = jnp.take_along_axis(source, at_spot[c], axis=1, mode="promise_in_bounds")
                found[c] = jnp.where(at_piece[c] == cell * pieces + tile, taken, found[c])
    for c in range(len(found)):
        out[:, c * LANES : (c + 1) * LANES] = found[c].astype(bf16)


def window_body(
    here, from_lon, from_lat, from_both, picks, norm_gain, norm_shift, w_qkv, w_out, bias,
    out_here, out_lon, out_lat, out_both, keep, send, gathered, proj_grad, sums, tables,
):
    width = w_out.shape[0]
    level_win = bias.shape[0] // HEADS
    head_size = width // HEADS
    scaling = head_size ** (-0.5)
    quads = jnp.concatenate([q[...] for q in (here, from_lon, from_lat, from_both)], 0)
    features = jnp.dot(picks[...], quads[:, :width], preferred_element_type=f32)
    cotangent = jnp.dot(picks[...], quads[:, width:], preferred_element_type=f32)
    grad_shifted = cotangent.astype(bf16)
    gain = norm_gain[...]
    center = features - jnp.mean(features, -1, keepdims=True)
    inv_std = lax.rsqrt(jnp.mean(center * center, -1, keepdims=True) + epsilon)
    x_hat = center * inv_std
    normed = (x_hat * gain + norm_shift[...]).astype(bf16)
    query, key, value = (
        jnp.dot(normed, w_qkv[:, k * width : (k + 1) * width], preferred_element_type=f32).astype(bf16)
        for k in range(3)
    )
    grad_heads = lax.dot_general(
        grad_shifted, w_out[...], (((1,), (1,)), ((), ())), preferred_element_type=f32
    ).astype(bf16)
    head_of = lax.broadcasted_iota(jnp.int32, (1, width), 1) // head_size
    mixed_parts = []
    for t in range(level_win):
        rows = slice(t * WIN, (t + 1) * WIN)
        q, k, v, g = query[rows], key[rows], value[rows], grad_heads[rows]
        q_heads = [jnp.where(head_of == h, q, jnp.zeros_like(q)) for h in range(HEADS)]
        g_heads = [jnp.where(head_of == h, g, jnp.zeros_like(g)) for h in range(HEADS)]
        mixed = jnp.zeros((WIN, width), f32)
        grad_query = jnp.zeros((WIN, width), f32)
        grad_key = jnp.zeros((WIN, width), f32)
        grad_value = jnp.zeros((WIN, width), f32)
        for h in range(HEADS):
            logits = lax.dot_general(
                q_heads[h], k, (((1,), (1,)), ((), ())), preferred_element_type=f32
            )
            logits = logits * scaling + bias[t * HEADS + h]
            raised = jnp.exp(logits - jnp.max(logits, -1, keepdims=True))
            weights = raised * (1.0 / jnp.sum(raised, -1, keepdims=True))
            weights_bf = weights.astype(bf16)
            mixed = jnp.where(
                head_of == h, jnp.dot(weights_bf, v, preferred_element_type=f32), mixed
            )
            grad_weights = lax.dot_general(
                g_heads[h], v, (((1,), (1,)), ((), ())), preferred_element_type=f32
            )
            grad_value += lax.dot_general(
                weights_bf, g_heads[h], (((0,), (0,)), ((), ())), preferred_element_type=f32
            )
            grad_logits = weights * (
                grad_weights - jnp.sum(weights * grad_weights, -1, keepdims=True)
            )
            logit_bf = grad_logits.astype(bf16)
            grad_query = jnp.where(
                head_of == h, jnp.dot(logit_bf, k, preferred_element_type=f32), grad_query
            )
            grad_key += lax.dot_general(
                logit_bf, q_heads[h], (((0,), (0,)), ((), ())), preferred_element_type=f32
            )
            total = jnp.zeros((BLOCK, SPREAD), f32)
            for a in range(WW):
                shift = (WW - 1 - a) * BLOCK
                piece = grad_logits[a * BLOCK : (a + 1) * BLOCK]
                piece = jnp.concatenate((piece, jnp.zeros((BLOCK, SPREAD - WIN), f32)), 1)
                total += pltpu.roll(piece, shift, 1) if shift else piece
            for tile in range(SPREAD // LANES):
                tables[t, h, tile] = total[:, tile * LANES : (tile + 1) * LANES]
        mixed_parts.append(mixed.astype(bf16))
        proj_grad[rows, :width] = (grad_query * scaling).astype(bf16)
        proj_grad[rows, width : 2 * width] = (grad_key * scaling).astype(bf16)
        proj_grad[rows, 2 * width :] = grad_value.astype(bf16)
    mixed = jnp.concatenate(mixed_parts, 0)
    attn = jnp.dot(mixed, w_out[...], preferred_element_type=f32).astype(bf16)
    outputs = (features + attn.astype(f32)).astype(bf16)
    grad_proj = proj_grad[...]
    grad_input = lax.dot_general(
        grad_proj, w_qkv[...], (((1,), (1,)), ((), ())), preferred_element_type=f32
    )
    upstream = grad_input.astype(bf16).astype(f32)
    gain_part = jnp.sum(upstream * x_hat, 0, keepdims=True)
    shift_part = jnp.sum(upstream, 0, keepdims=True)
    g_hat = upstream * gain
    centred = (
        g_hat
        - jnp.mean(g_hat, -1, keepdims=True)
        - x_hat * jnp.mean(g_hat * x_hat, -1, keepdims=True)
    )
    grad_features = (cotangent + inv_std * centred).astype(bf16)
    for at, result in enumerate((outputs, grad_features)):
        back = lax.dot_general(
            picks[...], result, (((0,), (0,)), ((), ())), preferred_element_type=f32
        ).astype(bf16)
        for q, out in enumerate((out_here, out_lon, out_lat, out_both)):
            out[:, at * width : (at + 1) * width] = back[q * PAD_QUAD : (q + 1) * PAD_QUAD]
    sums[:, : 3 * width] = lax.dot_general(
        normed, grad_proj, (((0,), (0,)), ((), ())), preferred_element_type=f32
    )
    sums[:, 3 * width :] = lax.dot_general(
        mixed, grad_shifted, (((0,), (0,)), ((), ())), preferred_element_type=f32
    )
    chunks, blocks, size, _ = gathered.shape
    lat_count = chunks // 2
    edge = jnp.zeros((size - 4, LANES), f32)
    fill = jnp.zeros((1, 2 * LANES - width), f32)
    ends = [gain_part[:, :LANES], jnp.concatenate((gain_part[:, LANES:], fill), 1)]
    ends += [shift_part[:, :LANES], jnp.concatenate((shift_part[:, LANES:], fill), 1)]
    ends = jnp.concatenate(ends + [edge], 0).astype(bf16)
    for j in range(chunks):
        for b in range(blocks - 1):
            gathered[j, b] = sums[
                j * size : (j + 1) * size, b * LANES : (b + 1) * LANES
            ].astype(bf16)
        gathered[j, blocks - 1] = ends
    core = lax.axis_index("lon") % 2
    lat = lax.axis_index("lat")
    per = size // BLOCK
    for half, out in enumerate((keep, send)):
        side = core ^ half
        for at in range(lat_count):
            out[at * blocks : (at + 1) * blocks] = gathered[side * lat_count + (lat ^ at)]
        for h in range(0, HEADS, per):
            for tile in range(SPREAD // LANES):
                block = jnp.concatenate([tables[side, h + i, tile] for i in range(per)], 0)
                out[lat_count * blocks + h // per * (SPREAD // LANES) + tile] = block.astype(bf16)


def tree(values):
    while len(values) > 1:
        values = [a + b for a, b in zip(values[::2], values[1::2])]
    return values[0]


def halves_body(keep, came, *outs):
    at = 0
    for out in outs:
        count = out.shape[0]
        part = slice(at, at + count)
        out[...] = (keep[part].astype(f32) + came[part].astype(f32)).astype(bf16)
        at += count


def lats_body(*refs):
    *pieces, tail, out = refs
    blocks = pieces[0].shape[0]
    out[:blocks] = tree([p[...].astype(f32) for p in pieces]).astype(bf16)
    out[blocks:] = tail[...]


def lons_body(count, *refs):
    pieces, (weights, tail) = refs[:count], refs[count:]
    blocks = weights.shape[0]
    total = tree([p[...].astype(f32) for p in pieces]).astype(bf16)
    weights[...] = total[:blocks]
    tail[...] = total[blocks:]


def finish_body(lat_count, factor, *refs):
    near, far = refs[:lat_count], refs[lat_count : 2 * lat_count]
    table_near, table_far, grad_gain, grad_shift, grad_wqkv, grad_wout, grad_table, chunks, halves = refs[
        2 * lat_count :
    ]
    core = lax.axis_index("lon") % 2
    lat = lax.axis_index("lat")
    _, blocks, size, _ = chunks.shape
    for half, group in enumerate((near, far)):
        for at, ref in enumerate(group):
            chunks[(core ^ half) * lat_count + (lat ^ at)] = ref[...].astype(f32) * factor
    halves[core] = table_near[...].astype(f32) * factor
    halves[core ^ 1] = table_far[...].astype(f32) * factor
    width = grad_wout.shape[0]
    for j in range(chunks.shape[0]):
        rows = slice(j * size, (j + 1) * size)
        whole = jnp.concatenate([chunks[j, b] for b in range(blocks - 1)], 1)
        grad_wqkv[rows, :] = whole[:, : 3 * width]
        grad_wout[rows, :] = whole[:, 3 * width :]
    rest = width - LANES
    for at, out in enumerate((grad_gain, grad_shift)):
        out[:, :LANES] = chunks[0, blocks - 1, 2 * at : 2 * at + 1]
        out[:, LANES:] = chunks[0, blocks - 1, 2 * at + 1 : 2 * at + 2, :rest]
    for t in range(grad_table.shape[0]):
        grad_table[t, 0] = halves[t, : grad_table.shape[2], : grad_table.shape[3]]


def swap(value, axis, distance):
    count = lax.axis_size(axis)
    return lax.ppermute(value, axis, [(source, source ^ distance) for source in range(count)])


def send_back(value, lat_step, lon_step):
    lat_count, lon_count = lax.axis_size("lat"), lax.axis_size("lon")
    pairs = [
        (r * lon_count + c, (r + lat_step) % lat_count * lon_count + (c + lon_step) % lon_count)
        for r in range(lat_count)
        for c in range(lon_count)
    ]
    return lax.ppermute(value, ("lat", "lon"), pairs)


def on_device(features, norm_gain, norm_shift, w_qkv, w_out, bias_table, index_table, cotangent):
    levels, lat_rows, lon_cols, width = features.shape
    level_win, _, heads, labels = bias_table.shape
    lat_count, lon_count = lax.axis_size("lat"), lax.axis_size("lon")
    grid = (levels, lat_rows, lon_cols)
    to_quads, to_windows = pack_matrix(*grid), window_matrix(*grid)
    quad = struct((PAD_QUAD, 2 * width), bf16)
    steps = ((0, 1), (1, 0), (1, 1))

    here, *edges = call(pack_body, (quad,) * 4)(features, cotangent, to_quads)
    came = [send_back(e, -lat, -lon) for e, (lat, lon) in zip(edges, steps)]

    spread = struct((16, SPREAD), jnp.int32)
    bias, chunk, lane = call(
        bias_body,
        (struct((level_win * heads, WIN, WIN), f32), spread, spread),
        [pltpu.VMEM((8 * level_win, -(-labels // LANES) * LANES), f32)],
        moved=4 * 10**6,
    )(bias_table, index_table, *spread_matrices(), *apart())

    size = width // (2 * lat_count)
    blocks = 4 * width // LANES + 1
    table_blocks = HEADS * BLOCK * SPREAD // (size * LANES)
    half = struct((lat_count * blocks + table_blocks, size, LANES), bf16)
    out_here, *backs, keep, send = call(
        window_body,
        (quad,) * 4 + (half, half),
        [
            pltpu.VMEM((2 * lat_count, blocks, size, LANES), bf16),
            pltpu.VMEM((level_win * WIN, 3 * width), bf16),
            pltpu.VMEM((width, 4 * width), f32),
            pltpu.VMEM((level_win, heads, SPREAD // LANES, BLOCK, LANES), f32),
        ],
    )(here, *came, to_windows, norm_gain[None], norm_shift[None], w_qkv, w_out, bias)

    returned = [send_back(b, lat, lon) for b, (lat, lon) in zip(backs, steps)]

    chunk_shape = struct((blocks, size, LANES), bf16)
    tail_shape = struct((table_blocks, size, LANES), bf16)
    *pieces, tail = call(halves_body, (chunk_shape,) * lat_count + (tail_shape,))(
        keep, swap(send, "lon", 1)
    )
    pieces = pieces[:1] + [swap(p, "lat", at + 1) for at, p in enumerate(pieces[1:])]
    part = call(lats_body, struct((blocks + table_blocks, size, LANES), bf16))(*pieces, tail)
    parts = [part] + [swap(part, "lon", 2 * at) for at in range(1, lon_count // 2)]
    weights, tail = call(functools.partial(lons_body, len(parts)), (chunk_shape, tail_shape))(*parts)
    near = [weights] + [swap(weights, "lat", at) for at in range(1, lat_count)]

    places = struct((32, LANES), jnp.int32)
    piece, spot = call(inverse_body, (places, places))(chunk, lane)
    table_near = call(place_body, struct((8, -(-labels // LANES) * LANES), bf16))(tail, piece, spot)
    table_far = swap(table_near, "lon", 1)
    far = [swap(n, "lon", 1) for n in near]

    outputs, grad_features = call(unpack_body, (struct(features.shape, bf16),) * 2)(
        out_here, *returned, to_quads
    )
    factor = (levels * lat_rows * lat_count * lon_cols * lon_count) ** (-0.5)
    row = struct((1, width), f32)
    grad_gain, grad_shift, grad_wqkv, grad_wout, grad_table = call(
        functools.partial(finish_body, lat_count, factor),
        (row, row, struct(w_qkv.shape, f32), struct(w_out.shape, f32), struct(bias_table.shape, f32)),
        [
            pltpu.VMEM((2 * lat_count, blocks, size, LANES), f32),
            pltpu.VMEM((2,) + table_near.shape, f32),
        ],
    )(*near, *far, table_near, table_far)
    return (
        outputs,
        grad_features,
        grad_gain[0],
        grad_shift[0],
        grad_wqkv,
        grad_wout,
        grad_table,
    )


def solution(mesh):
    placed = (
        P(None, "lat", "lon", None),
        P(),
        P(),
        P(),
        P(),
        P(None, "lat", None, None),
        P(),
        P(None, "lat", "lon", None),
    )
    return jax.shard_map(
        on_device,
        mesh=mesh,
        in_specs=placed,
        out_specs=(
            P(None, "lat", "lon", None),
            P(None, "lat", "lon", None),
            P(),
            P(),
            P(),
            P(),
            P(None, "lat", None, None),
        ),
        check_vma=False,
    )
```

time: 350 us -> 57.8 us (0.17)
  local copies, waits for them, and re-layouts: 196 us -> 10.4 us
  waiting for transfers between devices: 75.6 us -> 8.79 us
  blocking collectives: 23.5 us -> 0 us
  Pallas kernels: 0 us -> 16.4 us
  other arithmetic: 15.4 us -> 0 us
  between operations: 14.7 us -> 0.88 us
  matrix products: 12.1 us -> 0 us
  starting transfers between devices: 11 us -> 20.9 us
    gather x3 -> x0, local copies, waits for them, and re-layouts: 130 us -> none  [the longest x2 88.9 us: on_device(): jnp.take(bias_table, index_table, axis=3).transpose(1, 0, 2, 3, 4)]
    psum x2 -> x0, waiting for transfers between devices: 68.6 us -> none  [the longest x1 44.6 us: on_device(): lax.psum(grad_wqkv.astype(jnp.bfloat16), 'lat').astype(jnp.float32)]
    psum x2 -> x0, blocking collectives: 23.5 us -> none  [the longest x1 13.7 us: on_device(): lax.psum(grad_gain.astype(jnp.bfloat16), 'lon').astype(jnp.float32)]
    reshape x10 -> x0, local copies, waits for them, and re-layouts: 23.2 us -> none  [the longest x1 10.1 us: table_grad(): score_grad.reshape(groups * HEADS, WZ, WH, WW, WZ, WH, WW)]
    pallas_call x0 -> x10, Pallas kernels: none -> 16.4 us  [the longest x1 6.87 us: on_device(): call(window_body, (quad,) * 4 + (half, half), [pltpu.VMEM((2 * lat_count,...]
    scatter x2 -> x0, local copies, waits for them, and re-layouts: 14.4 us -> none  [table_grad(): jnp.zeros((groups * HEADS, POS), jnp.float32).at[:, places].set(canonical)]
    transpose x1 -> x0, local copies, waits for them, and re-layouts: 14.1 us -> none  [table_grad(): score_grad.reshape(groups * HEADS, WZ, WH, WW, WZ, WH, WW)]
    dot_general x13 -> x0, matrix products: 12.1 us -> none  [the longest x1 3.28 us: window_pass(): jnp.einsum('bhij,bjhe->bihe', weights_bf, value_part, preferred_element_t...]
  transfers between devices with their start and end apart: 10 -> 21, of which waited for: 6 -> 7; matrix products, arithmetic and copies ran while one was open for 57% -> 4% of each run, Pallas kernels for 0% -> 14%
where the time goes in v1:
time: 57.8 us; the launch traced here: 57.4 us
  starting transfers between devices  20.9 us (36%)
  Pallas kernels  16.4 us (28%)
  local copies, waits for them, and re-layouts  10.4 us (18%)
  waiting for transfers between devices  8.79 us (15%)
  between operations  0.88 us (2%)
    ppermute x15, starting transfers between devices, swap(): lax.ppermute(value, axis, [(source, source ^ distance) for source in rang...  13 us
    unnamed x30, local copies, waits for them, and re-layouts  10.4 us
    ppermute x15, waiting for transfers between devices, swap(): lax.ppermute(value, axis, [(source, source ^ distance) for source in rang...  8.63 us
    ppermute x6, starting transfers between devices, send_back(): return lax.ppermute(value, ('lat', 'lon'), pairs)  7.89 us
    pallas_call x1, Pallas kernels, on_device(): call(window_body, (quad,) * 4 + (half, half), [pltpu.VMEM((2 * lat_count,...  6.87 us
    pallas_call x1, Pallas kernels, on_device(): call(bias_body, (struct((level_win * heads, WIN, WIN), f32), spread, spre...  5.43 us
    pallas_call x1, Pallas kernels, on_device(): call(place_body, struct((8, -(-labels // LANES) * LANES), bf16))  1.48 us
  transfers between devices with their start and end apart: 21, of which 7 were waited for; matrix products, arithmetic and copies ran while one was open for 4% of the time, Pallas kernels for 14%

profile of v1, /device:TPU:0, one launch (start us, length us, event | category | flops | bytes accessed | tf_op | source)
XLA Modules:
  0.0 57.4 jit_solution(9845748907075001189)
XLA Ops:
  0.6 0.0 copy-start.3
  0.7 1.0 %copy.21.features = bf16[4,6,12,192]{3,2,1,0:T(8,128)(2,1)S(1)} copy(bf16[4,6,12,192]{3,0,2,1:T(4,128)(2,1)} %param.14) | data formatting | bytes 221184 | tf_op args[0]
  1.7 0.9 %copy.22.cotangent = bf16[4,6,12,192]{3,2,1,0:T(8,128)(2,1)S(1)} copy(bf16[4,6,12,192]{3,0,2,1:T(4,128)(2,1)} %param.21) | data formatting | bytes 221184 | tf_op args[7]
  2.6 0.0 copy-start
  2.6 0.9 %copy-done = bf16[320,384]{1,0:T(8,128)(2,1)S(1)} copy-done((bf16[320,384]{1,0:T(8,128)(2,1)S(1)}, bf16[320,384]{1,0:T(8,128)(2,1)}, u32[]{:S(2)}) %copy-start) | copy-done | bytes 245784
  3.6 0.4 shard_map.189
  4.0 4.5 %collective-permute-start = (bf16[80,384]{1,0:T(8,128)(2,1)S(1)}, bf16[80,384]{1,0:T(8,128)(2,1)S(1)}, u32[]{:S(2)}, u32[]{:S(2)}) collective-permute-start(bf16[80,384]{1,0:T(8,128)(2,1)S(1)} %get-tuple-element.37), channel_id=1, source_target_pairs={{0,7},{1,0},{2,1},{3,2},{4,3},{5,4},{6,5},{7,6},{8,15},{9,8},{10,9... | collective-permute-start | bytes 184328 | tf_op jit(solution)/shard_map/ppermute | solution.py:415
  8.5 2.4 %collective-permute-start.1 = (bf16[80,384]{1,0:T(8,128)(2,1)S(1)}, bf16[80,384]{1,0:T(8,128)(2,1)S(1)}, u32[]{:S(2)}, u32[]{:S(2)}) collective-permute-start(bf16[80,384]{1,0:T(8,128)(2,1)S(1)} %get-tuple-element.38), channel_id=1, source_target_pairs={{0,24},{1,25},{2,26},{3,27},{4,28},{5,29},{6,30},{7,31},{8,0},{9,1... | collective-permute-start | bytes 184328 | tf_op jit(solution)/shard_map/ppermute | solution.py:415
  11.0 0.4 collective-permute-start.2
  11.3 0.9 %copy.23.bias_table = f32[2,1,6,3312]{3,2,1,0:T(8,128)S(1)} copy(f32[2,1,6,3312]{3,1,2,0:T(1,128)} %param.19) | data formatting | bytes 317952 | tf_op args[5]
  12.3 0.0 copy-start.5
  12.3 0.9 %copy-done.5 = bf16[144,384]{1,0:T(8,128)(2,1)S(1)} copy-done((bf16[144,384]{1,0:T(8,128)(2,1)S(1)}, bf16[144,384]{1,0:T(8,128)(2,1)}, u32[]{:S(2)}) %copy-start.5) | copy-done | bytes 110616
  13.2 0.9 %copy-done.6 = bf16[144,384]{1,0:T(8,128)(2,1)S(1)} copy-done((bf16[144,384]{1,0:T(8,128)(2,1)S(1)}, bf16[144,384]{1,0:T(8,128)(2,1)}, u32[]{:S(2)}) %copy-start.6) | copy-done | bytes 110616
  14.1 0.7 %copy-done.8 = f32[16,384]{1,0:T(8,128)S(1)} copy-done((f32[16,384]{1,0:T(8,128)S(1)}, f32[16,384]{1,0:T(8,128)}, u32[]{:S(2)}) %copy-start.8) | copy-done | bytes 24600
  14.8 0.7 %copy-done.9 = f32[16,384]{1,0:T(8,128)S(1)} copy-done((f32[16,384]{1,0:T(8,128)S(1)}, f32[16,384]{1,0:T(8,128)}, u32[]{:S(2)}) %copy-start.9) | copy-done | bytes 24600
  15.6 5.4 %shard_map.190 = (f32[12,144,144]{2,1,0:T(8,128)S(1)}, s32[16,384]{1,0:T(8,128)S(1)}, s32[16,384]{1,0:T(8,128)S(1)}) custom-call(f32[2,1,6,3312]{3,2,1,0:T(8,128)S(1)} %copy.23.bias_table, s32[144,144]{1,0:T(8,128)S(1)} %copy-done.4, bf16[144,384]{1,0:T(8,128)(2,1)S(1)} %copy-done.6, bf16[144,384]{1,0:T(8,128)(2,1)S(1)} %copy-done.5, ...), custom_call_target="tpu_custom_call" | custom-call | bytes 4000000 | tf_op jit(solution)/shard_map/pallas_call | solution.py:431
  21.0 0.0 collective-permute-done.from_lon
  21.0 0.0 collective-permute-done.1.from_lat
  21.0 0.0 collective-permute-done.2.from_both
  21.1 0.0 copy-start.7
  21.1 0.9 %copy-done.7 = bf16[192,192]{1,0:T(8,128)(2,1)S(1)} copy-done((bf16[192,192]{1,0:T(8,128)(2,1)S(1)}, bf16[192,192]{1,0:T(8,128)(2,1)}, u32[]{:S(2)}) %copy-start.7) | copy-done | bytes 73752
  22.0 6.9 %shard_map.191 = (bf16[80,384]{1,0:T(8,128)(2,1)S(1)}, bf16[80,384]{1,0:T(8,128)(2,1)S(1)}, bf16[80,384]{1,0:T(8,128)(2,1)S(1)}, bf16[80,384]{1,0:T(8,128)(2,1)S...) custom-call(bf16[80,384]{1,0:T(8,128)(2,1)S(1)} %get-tuple-element.36.here, ...), custom_call_target="tpu_custom_call" | custom-call | tf_op jit(solution)/shard_map/pallas_call | solution.py:442
  28.9 0.4 collective-permute-start.6
  29.2 1.2 %collective-permute-done.6.came = bf16[37,24,128]{2,1,0:T(8,128)(2,1)S(1)} collective-permute-done((bf16[37,24,128]{2,1,0:T(8,128)(2,1)S(1)}, bf16[37,24,128]{2,1,0:T(8,128)(2,1)S(1)}, u32[]{:S(2)}, u32[]{:S(2)}) %collective-permute-start.6) | collective-permute-done | bytes 227360 | tf_op jit(solution)/shard_map/ppermute | solution.py:405
  30.4 0.1 shard_map.193
  30.5 1.6 %collective-permute-start.7 = (bf16[7,24,128]{2,1,0:T(8,128)(2,1)S(1)}, bf16[7,24,128]{2,1,0:T(8,128)(2,1)S(1)}, u32[]{:S(2)}, u32[]{:S(2)}) collective-permute-start(bf16[7,24,128]{2,1,0:T(8,128)(2,1)S(1)} %get-tuple-element.50), channel_id=1, source_target_pairs={{0,8},{8,0},{16,24},{24,16},{1,9},{9,1},{17,25},{25,17},{2,10},{10... | collective-permute-start | bytes 129032 | tf_op jit(solution)/shard_map/ppermute | solution.py:405
  32.0 0.5 collective-permute-start.8
  32.5 1.5 %collective-permute-start.9 = (bf16[7,24,128]{2,1,0:T(8,128)(2,1)S(1)}, bf16[7,24,128]{2,1,0:T(8,128)(2,1)S(1)}, u32[]{:S(2)}, u32[]{:S(2)}) collective-permute-start(bf16[7,24,128]{2,1,0:T(8,128)(2,1)S(1)} %get-tuple-element.52), channel_id=1, source_target_pairs={{0,24},{8,16},{16,8},{24,0},{1,25},{9,17},{17,9},{25,1},{2,26},{10... | collective-permute-start | bytes 129032 | tf_op jit(solution)/shard_map/ppermute | solution.py:405
  34.0 0.5 collective-permute-done.7.refs_1_
  34.6 2.0 %collective-permute-done.8.refs_2_ = bf16[7,24,128]{2,1,0:T(8,128)(2,1)S(1)} collective-permute-done((bf16[7,24,128]{2,1,0:T(8,128)(2,1)S(1)}, bf16[7,24,128]{2,1,0:T(8,128)(2,1)S(1)}, u32[]{:S(2)}, u32[]{:S(2)}) %collective-permute-start.8) | collective-permute-done | bytes 43040 | tf_op jit(solution)/shard_map/ppermute | solution.py:405
  36.5 0.9 %collective-permute-done.9.refs_3_ = bf16[7,24,128]{2,1,0:T(8,128)(2,1)S(1)} collective-permute-done((bf16[7,24,128]{2,1,0:T(8,128)(2,1)S(1)}, bf16[7,24,128]{2,1,0:T(8,128)(2,1)S(1)}, u32[]{:S(2)}, u32[]{:S(2)}) %collective-permute-start.9) | collective-permute-done | bytes 43040 | tf_op jit(solution)/shard_map/ppermute | solution.py:405
  37.5 0.6 %collective-permute-start.12 = (bf16[16,24,128]{2,1,0:T(8,128)(2,1)S(1)}, bf16[16,24,128]{2,1,0:T(8,128)(2,1)S(1)}, u32[]{:S(2)}, u32[]{:S(2)}) collective-permute-start(bf16[16,24,128]{2,1,0:T(8,128)(2,1)S(1)} %shard_map.194.refs_0_), channel_id=1, source_target_pairs={{0,6},{1,7},{2,4},{3,5},{4,2},{5,3},{6,0},{7,1},{8,14},{9,15},{10,... | collective-permute-start | bytes 294920 | tf_op jit(solution)/shard_map/ppermute | solution.py:405
  38.1 0.0 collective-permute-start.11
  38.1 3.8 %collective-permute-start.10 = (bf16[16,24,128]{2,1,0:T(8,128)(2,1)S(1)}, bf16[16,24,128]{2,1,0:T(8,128)(2,1)S(1)}, u32[]{:S(2)}, u32[]{:S(2)}) collective-permute-start(bf16[16,24,128]{2,1,0:T(8,128)(2,1)S(1)} %shard_map.194.refs_0_), channel_id=1, source_target_pairs={{0,2},{1,3},{2,0},{3,1},{4,6},{5,7},{6,4},{7,5},{8,10},{9,11},{10,... | collective-permute-start | bytes 294920 | tf_op jit(solution)/shard_map/ppermute | solution.py:405
  41.9 0.0 collective-permute-start.3
  41.9 0.5 collective-permute-start.4
  42.5 2.5 %collective-permute-done.12.refs_3_ = bf16[16,24,128]{2,1,0:T(8,128)(2,1)S(1)} collective-permute-done((bf16[16,24,128]{2,1,0:T(8,128)(2,1)S(1)}, bf16[16,24,128]{2,1,0:T(8,128)(2,1)S(1)}, u32[]{:S(2)}, u32[]{:S(2)}) %collective-permute-start.12) | collective-permute-done | bytes 98336 | tf_op jit(solution)/shard_map/ppermute | solution.py:405
  45.0 0.0 collective-permute-start.5
  45.0 1.5 %collective-permute-done.11.refs_2_ = bf16[16,24,128]{2,1,0:T(8,128)(2,1)S(1)} collective-permute-done((bf16[16,24,128]{2,1,0:T(8,128)(2,1)S(1)}, bf16[16,24,128]{2,1,0:T(8,128)(2,1)S(1)}, u32[]{:S(2)}, u32[]{:S(2)}) %collective-permute-start.11) | collective-permute-done | bytes 98336 | tf_op jit(solution)/shard_map/ppermute | solution.py:405
  46.5 0.0 collective-permute-done.10.refs_1_
  46.5 0.1 shard_map.195
  46.5 1.6 %collective-permute-start.15 = (bf16[7,24,128]{2,1,0:T(8,128)(2,1)S(1)}, bf16[7,24,128]{2,1,0:T(8,128)(2,1)S(1)}, u32[]{:S(2)}, u32[]{:S(2)}) collective-permute-start(bf16[7,24,128]{2,1,0:T(8,128)(2,1)S(1)} %get-tuple-element.54.refs_0_), channel_id=1, source_target_pairs={{0,24},{8,16},{16,8},{24,0},{1,25},{9,17},{17,9},{25,1},{2,26},{10... | collective-permute-start | bytes 129032 | tf_op jit(solution)/shard_map/ppermute | solution.py:405
  48.1 0.5 collective-permute-start.14
  48.6 0.0 collective-permute-done.3.from_lon
  48.6 1.5 %collective-permute-start.13 = (bf16[7,24,128]{2,1,0:T(8,128)(2,1)S(1)}, bf16[7,24,128]{2,1,0:T(8,128)(2,1)S(1)}, u32[]{:S(2)}, u32[]{:S(2)}) collective-permute-start(bf16[7,24,128]{2,1,0:T(8,128)(2,1)S(1)} %get-tuple-element.54.refs_0_), channel_id=1, source_target_pairs={{0,8},{8,0},{16,24},{24,16},{1,9},{9,1},{17,25},{25,17},{2,10},{10... | collective-permute-start | bytes 129032 | tf_op jit(solution)/shard_map/ppermute | solution.py:405
  50.1 0.6 %shard_map.196 = (s32[32,128]{1,0:T(8,128)S(1)}, s32[32,128]{1,0:T(8,128)S(1)}) custom-call(s32[16,384]{1,0:T(8,128)S(1)} %get-tuple-element.56.chunk, s32[16,384]{1,0:T(8,128)S(1)} %get-tuple-element.57.lane), custom_call_target="tpu_custom_call" | custom-call | tf_op jit(solution)/shard_map/pallas_call | solution.py:467
  50.7 1.5 %shard_map.197.refs_8_ = bf16[8,3328]{1,0:T(8,128)(2,1)S(1)} custom-call(bf16[9,24,128]{2,1,0:T(8,128)(2,1)S(1)} %get-tuple-element.55.blocks, s32[32,128]{1,0:T(8,128)S(1)} %get-tuple-element.58.piece, s32[32,128]{1,0:T(8,128)S(1)} %get-tuple-element.59.spot), custom_call_target="tpu_custom_call" | custom-call | tf_op jit(solution)/shard_map/pallas_call | solution.py:468
  52.2 0.0 collective-permute-done.4.from_lat
  52.2 0.1 collective-permute-start.20
  52.3 0.1 collective-permute-done.5.from_both
  52.4 0.3 collective-permute-start.16
  52.8 0.2 collective-permute-start.19
  53.0 0.0 collective-permute-done.14.refs_2_
  53.0 0.4 collective-permute-start.18
  53.3 0.2 collective-permute-start.17
  53.5 0.5 shard_map.192
  54.0 0.8 %copy.24 = bf16[4,6,12,192]{3,0,2,1:T(4,128)(2,1)} copy(bf16[4,6,12,192]{3,2,1,0:T(8,128)(2,1)S(1)} %get-tuple-element.65) | data formatting | bytes 221184
  54.7 0.8 %copy.25 = bf16[4,6,12,192]{3,0,2,1:T(4,128)(2,1)} copy(bf16[4,6,12,192]{3,2,1,0:T(8,128)(2,1)S(1)} %get-tuple-element.66) | data formatting | bytes 221184
  55.5 0.0 collective-permute-done.16.refs_4_
  55.5 0.0 collective-permute-done.20.refs_9_
  55.5 0.0 collective-permute-done.19.refs_7_
  55.5 0.0 collective-permute-done.17.refs_5_
  55.6 1.0 %shard_map.198 = (f32[1,192]{1,0:T(1,128)}, f32[1,192]{1,0:T(1,128)}, f32[192,576]{1,0:T(8,128)}, f32[192,192]{1,0:T(8,128)}, f32[2,1,6,3312]{3,2,1,0:T(8,128)S(1)}) custom-call(bf16[7,24,128]{2,1,0:T(8,128)(2,1)S(1)} %get-tuple-element.54.refs_0_, bf16[7,24,128]{2,1,0:T(8,128)(2,1)S(1)} %collective-permute-done.13.refs_1_, ...), custom_call_target="tpu_custom_call" | custom-call | tf_op jit(solution)/shard_map/pallas_call | solution.py:477
  56.5 0.8 %copy.26 = f32[2,1,6,3312]{3,1,2,0:T(1,128)} copy(f32[2,1,6,3312]{3,2,1,0:T(8,128)S(1)} %get-tuple-element.71) | data formatting | bytes 317952
  (18 shorter events, 0.1 us)
Async XLA Ops:
  0.6 20.4 %copy-start.3 = (bf16[288,320]{1,0:T(8,128)(2,1)S(1)}, bf16[288,320]{1,0:T(8,128)(2,1)}, u32[]{:S(2)}) copy-start(bf16[288,320]{1,0:T(8,128)(2,1)} %constant.13.clone.picks) | copy-start | bytes 552964
  0.6 11.6 %copy-start.4 = (s32[144,144]{1,0:T(8,128)S(1)}, s32[144,144]{1,0:T(8,128)}, u32[]{:S(2)}) copy-start(s32[144,144]{1,0:T(8,128)} %index_table.1) | copy-start | bytes 248836
  0.7 20.4 %copy-start.2 = (bf16[192,576]{1,0:T(8,128)(2,1)S(1)}, bf16[192,576]{1,0:T(8,128)(2,1)}, u32[]{:S(2)}) copy-start(bf16[192,576]{1,0:T(8,128)(2,1)} %w_qkv.1) | copy-start | bytes 663556
  0.7 20.4 %copy-start.11 = (f32[192]{0:T(256)S(1)}, f32[192]{0:T(256)}, u32[]{:S(2)}) copy-start(f32[192]{0:T(256)} %param.16) | copy-start | bytes 2308
  0.7 20.4 %copy-start.10 = (f32[192]{0:T(256)S(1)}, f32[192]{0:T(256)}, u32[]{:S(2)}) copy-start(f32[192]{0:T(256)} %param.15) | copy-start | bytes 2308
  2.6 0.9 %copy-start = (bf16[320,384]{1,0:T(8,128)(2,1)S(1)}, bf16[320,384]{1,0:T(8,128)(2,1)}, u32[]{:S(2)}) copy-start(bf16[320,384]{1,0:T(8,128)(2,1)} %constant.12.clone.picks) | copy-start | bytes 737284
  4.0 17.0 %collective-permute-start = (bf16[80,384]{1,0:T(8,128)(2,1)S(1)}, bf16[80,384]{1,0:T(8,128)(2,1)S(1)}, u32[]{:S(2)}, u32[]{:S(2)}) collective-permute-start(bf16[80,384]{1,0:T(8,128)(2,1)S(1)} %get-tuple-element.37), channel_id=1, source_target_pairs={{0,7},{1,0},{2,1},{3,2},{4,3},{5,4},{6,5},{7,6},{8,15},{9,8},{10,9... | collective-permute-start | bytes 184328 | tf_op jit(solution)/shard_map/ppermute | solution.py:415
  8.5 12.5 %collective-permute-start.1 = (bf16[80,384]{1,0:T(8,128)(2,1)S(1)}, bf16[80,384]{1,0:T(8,128)(2,1)S(1)}, u32[]{:S(2)}, u32[]{:S(2)}) collective-permute-start(bf16[80,384]{1,0:T(8,128)(2,1)S(1)} %get-tuple-element.38), channel_id=1, source_target_pairs={{0,24},{1,25},{2,26},{3,27},{4,28},{5,29},{6,30},{7,31},{8,0},{9,1... | collective-permute-start | bytes 184328 | tf_op jit(solution)/shard_map/ppermute | solution.py:415
  11.0 10.1 %collective-permute-start.2 = (bf16[80,384]{1,0:T(8,128)(2,1)S(1)}, bf16[80,384]{1,0:T(8,128)(2,1)S(1)}, u32[]{:S(2)}, u32[]{:S(2)}) collective-permute-start(bf16[80,384]{1,0:T(8,128)(2,1)S(1)} %get-tuple-element.39), channel_id=1, source_target_pairs={{0,31},{1,24},{2,25},{3,26},{4,27},{5,28},{6,29},{7,30},{8,7},{9,0... | collective-permute-start | bytes 184328 | tf_op jit(solution)/shard_map/ppermute | solution.py:415
  12.3 0.9 %copy-start.5 = (bf16[144,384]{1,0:T(8,128)(2,1)S(1)}, bf16[144,384]{1,0:T(8,128)(2,1)}, u32[]{:S(2)}) copy-start(bf16[144,384]{1,0:T(8,128)(2,1)} %constant.15.clone.first) | copy-start | bytes 331780
  13.2 0.9 %copy-start.6 = (bf16[144,384]{1,0:T(8,128)(2,1)S(1)}, bf16[144,384]{1,0:T(8,128)(2,1)}, u32[]{:S(2)}) copy-start(bf16[144,384]{1,0:T(8,128)(2,1)} %constant.14.clone.last) | copy-start | bytes 331780
  14.1 0.7 %copy-start.8 = (f32[16,384]{1,0:T(8,128)S(1)}, f32[16,384]{1,0:T(8,128)}, u32[]{:S(2)}) copy-start(f32[16,384]{1,0:T(8,128)} %constant.17.clone.row_apart) | copy-start | bytes 73732
  14.8 0.7 %copy-start.9 = (f32[16,384]{1,0:T(8,128)S(1)}, f32[16,384]{1,0:T(8,128)}, u32[]{:S(2)}) copy-start(f32[16,384]{1,0:T(8,128)} %constant.16.clone.level_apart) | copy-start | bytes 73732
  21.1 0.9 %copy-start.7 = (bf16[192,192]{1,0:T(8,128)(2,1)S(1)}, bf16[192,192]{1,0:T(8,128)(2,1)}, u32[]{:S(2)}) copy-start(bf16[192,192]{1,0:T(8,128)(2,1)} %w_out.1) | copy-start | bytes 221188
  22.0 31.5 %copy-start.1 = (bf16[320,384]{1,0:T(8,128)(2,1)S(1)}, bf16[320,384]{1,0:T(8,128)(2,1)}, u32[]{:S(2)}) copy-start(bf16[320,384]{1,0:T(8,128)(2,1)} %constant.12.clone.picks) | copy-start | bytes 737284
  28.9 1.6 %collective-permute-start.6 = (bf16[37,24,128]{2,1,0:T(8,128)(2,1)S(1)}, bf16[37,24,128]{2,1,0:T(8,128)(2,1)S(1)}, u32[]{:S(2)}, u32[]{:S(2)}) collective-permute-start(bf16[37,24,128]{2,1,0:T(8,128)(2,1)S(1)} %get-tuple-element.48), channel_id=1, source_target_pairs={{0,1},{1,0},{2,3},{3,2},{4,5},{5,4},{6,7},{7,6},{8,9},{9,8},{10,11... | collective-permute-start | bytes 681992 | tf_op jit(solution)/shard_map/ppermute | solution.py:405
  30.5 4.1 %collective-permute-start.7 = (bf16[7,24,128]{2,1,0:T(8,128)(2,1)S(1)}, bf16[7,24,128]{2,1,0:T(8,128)(2,1)S(1)}, u32[]{:S(2)}, u32[]{:S(2)}) collective-permute-start(bf16[7,24,128]{2,1,0:T(8,128)(2,1)S(1)} %get-tuple-element.50), channel_id=1, source_target_pairs={{0,8},{8,0},{16,24},{24,16},{1,9},{9,1},{17,25},{25,17},{2,10},{10... | collective-permute-start | bytes 129032 | tf_op jit(solution)/shard_map/ppermute | solution.py:405
  32.0 4.5 %collective-permute-start.8 = (bf16[7,24,128]{2,1,0:T(8,128)(2,1)S(1)}, bf16[7,24,128]{2,1,0:T(8,128)(2,1)S(1)}, u32[]{:S(2)}, u32[]{:S(2)}) collective-permute-start(bf16[7,24,128]{2,1,0:T(8,128)(2,1)S(1)} %get-tuple-element.51), channel_id=1, source_target_pairs={{0,16},{8,24},{16,0},{24,8},{1,17},{9,25},{17,1},{25,9},{2,18},{10... | collective-permute-start | bytes 129032 | tf_op jit(solution)/shard_map/ppermute | solution.py:405
  32.5 4.9 %collective-permute-start.9 = (bf16[7,24,128]{2,1,0:T(8,128)(2,1)S(1)}, bf16[7,24,128]{2,1,0:T(8,128)(2,1)S(1)}, u32[]{:S(2)}, u32[]{:S(2)}) collective-permute-start(bf16[7,24,128]{2,1,0:T(8,128)(2,1)S(1)} %get-tuple-element.52), channel_id=1, source_target_pairs={{0,24},{8,16},{16,8},{24,0},{1,25},{9,17},{17,9},{25,1},{2,26},{10... | collective-permute-start | bytes 129032 | tf_op jit(solution)/shard_map/ppermute | solution.py:405
  37.5 7.5 %collective-permute-start.12 = (bf16[16,24,128]{2,1,0:T(8,128)(2,1)S(1)}, bf16[16,24,128]{2,1,0:T(8,128)(2,1)S(1)}, u32[]{:S(2)}, u32[]{:S(2)}) collective-permute-start(bf16[16,24,128]{2,1,0:T(8,128)(2,1)S(1)} %shard_map.194.refs_0_), channel_id=1, source_target_pairs={{0,6},{1,7},{2,4},{3,5},{4,2},{5,3},{6,0},{7,1},{8,14},{9,15},{10,... | collective-permute-start | bytes 294920 | tf_op jit(solution)/shard_map/ppermute | solution.py:405
  38.1 8.3 %collective-permute-start.11 = (bf16[16,24,128]{2,1,0:T(8,128)(2,1)S(1)}, bf16[16,24,128]{2,1,0:T(8,128)(2,1)S(1)}, u32[]{:S(2)}, u32[]{:S(2)}) collective-permute-start(bf16[16,24,128]{2,1,0:T(8,128)(2,1)S(1)} %shard_map.194.refs_0_), channel_id=1, source_target_pairs={{0,4},{1,5},{2,6},{3,7},{4,0},{5,1},{6,2},{7,3},{8,12},{9,13},{10,... | collective-permute-start | bytes 294920 | tf_op jit(solution)/shard_map/ppermute | solution.py:405
  38.1 8.3 %collective-permute-start.10 = (bf16[16,24,128]{2,1,0:T(8,128)(2,1)S(1)}, bf16[16,24,128]{2,1,0:T(8,128)(2,1)S(1)}, u32[]{:S(2)}, u32[]{:S(2)}) collective-permute-start(bf16[16,24,128]{2,1,0:T(8,128)(2,1)S(1)} %shard_map.194.refs_0_), channel_id=1, source_target_pairs={{0,2},{1,3},{2,0},{3,1},{4,6},{5,7},{6,4},{7,5},{8,10},{9,11},{10,... | collective-permute-start | bytes 294920 | tf_op jit(solution)/shard_map/ppermute | solution.py:405
  41.9 6.6 %collective-permute-start.3 = (bf16[80,384]{1,0:T(8,128)(2,1)S(1)}, bf16[80,384]{1,0:T(8,128)(2,1)S(1)}, u32[]{:S(2)}, u32[]{:S(2)}) collective-permute-start(bf16[80,384]{1,0:T(8,128)(2,1)S(1)} %get-tuple-element.42), channel_id=1, source_target_pairs={{0,1},{1,2},{2,3},{3,4},{4,5},{5,6},{6,7},{7,0},{8,9},{9,10},{10,1... | collective-permute-start | bytes 184328 | tf_op jit(solution)/shard_map/ppermute | solution.py:415
  41.9 10.3 %collective-permute-start.4 = (bf16[80,384]{1,0:T(8,128)(2,1)S(1)}, bf16[80,384]{1,0:T(8,128)(2,1)S(1)}, u32[]{:S(2)}, u32[]{:S(2)}) collective-permute-start(bf16[80,384]{1,0:T(8,128)(2,1)S(1)} %get-tuple-element.43), channel_id=1, source_target_pairs={{0,8},{1,9},{2,10},{3,11},{4,12},{5,13},{6,14},{7,15},{8,16},{9,17... | collective-permute-start | bytes 184328 | tf_op jit(solution)/shard_map/ppermute | solution.py:415
  45.0 7.4 %collective-permute-start.5 = (bf16[80,384]{1,0:T(8,128)(2,1)S(1)}, bf16[80,384]{1,0:T(8,128)(2,1)S(1)}, u32[]{:S(2)}, u32[]{:S(2)}) collective-permute-start(bf16[80,384]{1,0:T(8,128)(2,1)S(1)} %get-tuple-element.44), channel_id=1, source_target_pairs={{0,9},{1,10},{2,11},{3,12},{4,13},{5,14},{6,15},{7,8},{8,17},{9,18... | collective-permute-start | bytes 184328 | tf_op jit(solution)/shard_map/ppermute | solution.py:415
  46.5 6.3 %collective-permute-start.15 = (bf16[7,24,128]{2,1,0:T(8,128)(2,1)S(1)}, bf16[7,24,128]{2,1,0:T(8,128)(2,1)S(1)}, u32[]{:S(2)}, u32[]{:S(2)}) collective-permute-start(bf16[7,24,128]{2,1,0:T(8,128)(2,1)S(1)} %get-tuple-element.54.refs_0_), channel_id=1, source_target_pairs={{0,24},{8,16},{16,8},{24,0},{1,25},{9,17},{17,9},{25,1},{2,26},{10... | collective-permute-start | bytes 129032 | tf_op jit(solution)/shard_map/ppermute | solution.py:405
  48.1 4.9 %collective-permute-start.14 = (bf16[7,24,128]{2,1,0:T(8,128)(2,1)S(1)}, bf16[7,24,128]{2,1,0:T(8,128)(2,1)S(1)}, u32[]{:S(2)}, u32[]{:S(2)}) collective-permute-start(bf16[7,24,128]{2,1,0:T(8,128)(2,1)S(1)} %get-tuple-element.54.refs_0_), channel_id=1, source_target_pairs={{0,16},{8,24},{16,0},{24,8},{1,17},{9,25},{17,1},{25,9},{2,18},{10... | collective-permute-start | bytes 129032 | tf_op jit(solution)/shard_map/ppermute | solution.py:405
  48.6 4.7 %collective-permute-start.13 = (bf16[7,24,128]{2,1,0:T(8,128)(2,1)S(1)}, bf16[7,24,128]{2,1,0:T(8,128)(2,1)S(1)}, u32[]{:S(2)}, u32[]{:S(2)}) collective-permute-start(bf16[7,24,128]{2,1,0:T(8,128)(2,1)S(1)} %get-tuple-element.54.refs_0_), channel_id=1, source_target_pairs={{0,8},{8,0},{16,24},{24,16},{1,9},{9,1},{17,25},{25,17},{2,10},{10... | collective-permute-start | bytes 129032 | tf_op jit(solution)/shard_map/ppermute | solution.py:405
  52.2 3.3 %collective-permute-start.20 = (bf16[8,3328]{1,0:T(8,128)(2,1)S(1)}, bf16[8,3328]{1,0:T(8,128)(2,1)S(1)}, u32[]{:S(2)}, u32[]{:S(2)}) collective-permute-start(bf16[8,3328]{1,0:T(8,128)(2,1)S(1)} %shard_map.197.refs_8_), channel_id=1, source_target_pairs={{0,1},{1,0},{2,3},{3,2},{4,5},{5,4},{6,7},{7,6},{8,9},{9,8},{10,11... | collective-permute-start | bytes 159752 | tf_op jit(solution)/shard_map/ppermute | solution.py:405
  52.4 3.1 %collective-permute-start.16 = (bf16[7,24,128]{2,1,0:T(8,128)(2,1)S(1)}, bf16[7,24,128]{2,1,0:T(8,128)(2,1)S(1)}, u32[]{:S(2)}, u32[]{:S(2)}) collective-permute-start(bf16[7,24,128]{2,1,0:T(8,128)(2,1)S(1)} %get-tuple-element.54.refs_0_), channel_id=1, source_target_pairs={{0,1},{1,0},{2,3},{3,2},{4,5},{5,4},{6,7},{7,6},{8,9},{9,8},{10,11... | collective-permute-start | bytes 129032 | tf_op jit(solution)/shard_map/ppermute | solution.py:405
  52.8 2.7 %collective-permute-start.19 = (bf16[7,24,128]{2,1,0:T(8,128)(2,1)S(1)}, bf16[7,24,128]{2,1,0:T(8,128)(2,1)S(1)}, u32[]{:S(2)}, u32[]{:S(2)}) collective-permute-start(bf16[7,24,128]{2,1,0:T(8,128)(2,1)S(1)} %collective-permute-done.15.refs_3_), channel_id=1, source_target_pairs={{0,1},{1,0},{2,3},{3,2},{4,5},{5,4},{6,7},{7,6},{8,9},{9,8},{10,11... | collective-permute-start | bytes 129032 | tf_op jit(solution)/shard_map/ppermute | solution.py:405
  53.0 2.6 %collective-permute-start.18 = (bf16[7,24,128]{2,1,0:T(8,128)(2,1)S(1)}, bf16[7,24,128]{2,1,0:T(8,128)(2,1)S(1)}, u32[]{:S(2)}, u32[]{:S(2)}) collective-permute-start(bf16[7,24,128]{2,1,0:T(8,128)(2,1)S(1)} %collective-permute-done.14.refs_2_), channel_id=1, source_target_pairs={{0,1},{1,0},{2,3},{3,2},{4,5},{5,4},{6,7},{7,6},{8,9},{9,8},{10,11... | collective-permute-start | bytes 129032 | tf_op jit(solution)/shard_map/ppermute | solution.py:405
  53.3 2.2 %collective-permute-start.17 = (bf16[7,24,128]{2,1,0:T(8,128)(2,1)S(1)}, bf16[7,24,128]{2,1,0:T(8,128)(2,1)S(1)}, u32[]{:S(2)}, u32[]{:S(2)}) collective-permute-start(bf16[7,24,128]{2,1,0:T(8,128)(2,1)S(1)} %collective-permute-done.13.refs_1_), channel_id=1, source_target_pairs={{0,1},{1,0},{2,3},{3,2},{4,5},{5,4},{6,7},{7,6},{8,9},{9,8},{10,11... | collective-permute-start | bytes 129032 | tf_op jit(solution)/shard_map/ppermute | solution.py:405

commit v2 on v1

--- a/solution.py
+++ b/solution.py
@@ -2,7 +2,6 @@
 
 import jax
 import jax.numpy as jnp
-import numpy as np
 from jax import lax
 from jax.experimental import pallas as pl
 from jax.experimental.pallas import tpu as pltpu
@@ -17,8 +16,7 @@
 SPANS = 2 * WW - 1
 SPREAD = 384
 LANES = 128
-PAD_LON = 16
-PAD_QUAD = 80
+PAD_LEVEL = 8
 LARGE = 1e30
 
 epsilon = 1e-05
@@ -41,115 +39,131 @@
     return jax.ShapeDtypeStruct(shape, dtype)
 
 
-def quadrants(levels, lat_rows, lon_cols):
+def quotient(value, divisor):
+    return (value * (65536 // divisor + 1)) >> 16
+
+
+def columns(shape, dim):
+    return lax.broadcasted_iota(jnp.int32, shape, dim)
+
+
+def hot(condition):
+    return jnp.where(condition, 1.0, 0.0).astype(bf16)
+
+
+def quadrants(lat_rows, lon_cols):
     lat_cut, lon_cut = WH // 2, WW // 2
-    high_lat, low_lat = range(lat_cut, lat_rows), range(lat_cut)
-    high_lon, low_lon = range(lon_cut, lon_cols), range(lon_cut)
+    high_lat, low_lat = slice(lat_cut, lat_rows), slice(lat_cut)
+    high_lon, low_lon = slice(lon_cut, lon_cols), slice(lon_cut)
     return (high_lat, high_lon), (high_lat, low_lon), (low_lat, high_lon), (low_lat, low_lon)
 
 
-def pack_matrix(levels, lat_rows, lon_cols):
-    picks = np.zeros((4 * PAD_QUAD, levels * lat_rows * PAD_LON), np.float32)
-    for q, (rows, cols) in enumerate(quadrants(levels, lat_rows, lon_cols)):
-        at = q * PAD_QUAD
-        for z in range(levels):
-            for a in rows:
-                for o in cols:
-                    picks[at, (z * lat_rows + a) * PAD_LON + o] = 1
-                    at += 1
-    return jnp.asarray(picks, bf16)
-
-
-def window_matrix(levels, lat_rows, lon_cols):
+def window_matrix(levels, room):
     lat_cut, lon_cut, level_cut = WH // 2, WW // 2, WZ // 2
-    picks = np.zeros((levels // WZ * WIN, 4 * PAD_QUAD), np.float32)
-    for q, (rows, cols) in enumerate(quadrants(levels, lat_rows, lon_cols)):
-        at = q * PAD_QUAD
-        for z in range(levels):
-            for a in rows:
-                for o in cols:
-                    level = (z - level_cut) % levels
-                    lat = (a - lat_cut) % lat_rows
-                    lon = (o - lon_cut) % lon_cols
-                    token = lon * BLOCK + level % WZ * WH + lat
-                    picks[level // WZ * WIN + token, at] = 1
-                    at += 1
-    return jnp.asarray(picks, bf16)
-
-
-def spread_matrices():
-    last, first = np.zeros((2, WIN, SPREAD), np.float32)
-    for span in range(SPANS):
-        for cell in range(BLOCK):
-            if span < WW - 1:
-                last[cell * WW + span, span * BLOCK + cell] = 1
-            else:
-                first[cell * WW + span - (WW - 1), span * BLOCK + cell] = 1
-    return jnp.asarray(last, bf16), jnp.asarray(first, bf16)
-
-
-def apart():
-    cell = np.arange(16)[:, None] % BLOCK
-    other = np.arange(SPREAD)[None, :] % BLOCK
-    level = (cell // WH >= WZ // 2) != (other // WH >= WZ // 2)
-    row = (cell % WH >= WH // 2) != (other % WH >= WH // 2)
-    return jnp.asarray(level, f32), jnp.asarray(row, f32)
-
-
-def pack_body(features, cotangent, picks, *outs):
-    levels, lat_rows, lon_cols, width = features.shape
-    for at, ref in enumerate((features, cotangent)):
-        cells = ref[...].astype(f32)
-        fill = jnp.zeros((levels, lat_rows, PAD_LON - lon_cols, width), f32)
-        cells = jnp.concatenate((cells, fill), 2).reshape(levels * lat_rows * PAD_LON, width)
-        packed = jnp.dot(picks[...], cells.astype(bf16), preferred_element_type=f32).astype(bf16)
-        for q, out in enumerate(outs):
-            out[:, at * width : (at + 1) * width] = packed[q * PAD_QUAD : (q + 1) * PAD_QUAD]
-
-
-def unpack_body(here, from_lon, from_lat, from_both, picks, outputs, grad_features):
-    levels, lat_rows, lon_cols, width = outputs.shape
-    for at, ref in enumerate((outputs, grad_features)):
-        part = slice(at * width, (at + 1) * width)
-        quads = jnp.concatenate([q[:, part] for q in (here, from_lon, from_lat, from_both)], 0)
-        cells = lax.dot_general(
-            picks[...], quads, (((0,), (0,)), ((), ())), preferred_element_type=f32
+    count = levels // WZ * WIN
+    token = columns((count, 1), 0)
+    window = quotient(token, WIN)
+    inside = token - window * WIN
+    lon = quotient(inside, BLOCK)
+    cell = inside - lon * BLOCK
+    depth = quotient(cell, WH)
+    lat = cell - depth * WH
+    level = window * WZ + depth + level_cut
+    level = jnp.where(level >= levels, level - levels, level)
+    late_lon, late_lat = lon >= lon_cut, lat >= lat_cut
+    quad = jnp.where(late_lat, 2, 0) + jnp.where(late_lon, 1, 0)
+    row = jnp.where(late_lat, lat - lat_cut, lat)
+    col = jnp.where(late_lon, lon - lon_cut, lon)
+    source = ((quad * lat_cut + row) * lon_cut + col) * room + level
+    return hot(columns((count, WIN // WZ * room), 1) == source)
+
+
+def pack_body(count, *refs):
+    features, cotangent, *plain = refs[: count + 2]
+    *outs, sems = refs[count + 2 :]
+    lat_rows, lon_cols, _, _ = features.shape
+    pairs = []
+    for (rows, cols), out in zip(quadrants(lat_rows, lon_cols), outs):
+        pairs += [(features.at[rows, cols], out.at[0]), (cotangent.at[rows, cols], out.at[1])]
+    pairs += zip(plain, outs[4:])
+    copies = [pltpu.make_async_copy(*pair, sems.at[at]) for at, pair in enumerate(pairs)]
+    for copy in copies:
+        copy.start()
+    for copy in copies:
+        copy.wait()
+
+
+def unpack_body(here, lat_piece, lon_pair, outputs, grad_features):
+    lat_rows, lon_cols, levels, width = outputs.shape
+    blocks = here.shape[0]
+    start = lat_piece.shape[0] - 2 * blocks
+    quads = (
+        here[...],
+        lon_pair[:blocks],
+        lat_piece[start : start + blocks],
+        lon_pair[blocks:],
+    )
+    for (rows, cols), quad in zip(quadrants(lat_rows, lon_cols), quads):
+        tiles = quad.astype(f32).reshape(3, -1, LANES)
+        rest = width - LANES
+        pair = (
+            jnp.concatenate((tiles[0], tiles[2][:, :rest]), 1),
+            jnp.concatenate((tiles[1], tiles[2][:, rest:]), 1),
         )
-        ref[...] = cells.reshape(levels, lat_rows, PAD_LON, width)[:, :, :lon_cols].astype(bf16)
-
-
-def spread_index(index_table, last, first):
+        for value, out in zip(pair, (outputs, grad_features)):
+            value = value.reshape(WH // 2, WW // 2, levels, width)
+            out[rows, cols] = value.astype(bf16)
+
+
+def spread_index(index_table):
     parts = []
     rows = [
         jnp.concatenate([index_table[c * WW + a : c * WW + a + 1, :] for c in range(BLOCK)], 0)
         for a in (WW - 1, 0)
     ]
     fill = jnp.zeros((16 - BLOCK, WIN), f32)
-    for cut in (lambda v: v // LANES, lambda v: v % LANES):
+    token = columns((WIN, 1), 0)
+    cell = quotient(token, WW)
+    entry = (token - cell * WW) * BLOCK + cell
+    wide = columns((WIN, SPREAD), 1)
+    cut_at = (WW - 1) * BLOCK
+    picks = (
+        hot(jnp.logical_and(entry == wide, wide < cut_at)),
+        hot(entry + cut_at == wide),
+    )
+    for cut in (lambda v: v >> 7, lambda v: v & (LANES - 1)):
         total = jnp.zeros((16, SPREAD), f32)
-        for labels, picks in zip(rows, (last, first)):
+        for labels, pick in zip(rows, picks):
             value = jnp.concatenate((cut(labels).astype(f32), fill), 0).astype(bf16)
-            total += jnp.dot(value, picks[...], preferred_element_type=f32)
+            total += jnp.dot(value, pick, preferred_element_type=f32)
         parts.append(total.astype(jnp.int32))
     return parts
 
 
-def bias_body(bias_table, index_table, last, first, level_apart, row_apart, out, chunk_out, lane_out, table):
-    level_win, _, heads, labels = bias_table.shape
-    chunk, lane = spread_index(index_table, last, first)
+def bias_body(bias_table, index_table, out, chunk_out, lane_out, table):
+    level_win, heads, _, labels = bias_table.shape
+    chunk, lane = spread_index(index_table)
     chunk_out[...] = chunk
     lane_out[...] = lane
     chunks = -(-labels // LANES)
     for t in range(level_win):
-        table[8 * t : 8 * t + heads, :labels] = bias_table[t, 0]
+        for h in range(heads):
+            table[t * heads + h : t * heads + h + 1, :labels] = bias_table[t, h]
+    cell = columns((16, 1), 0)
+    other = columns((1, SPREAD), 1)
+    other = other - quotient(other, BLOCK) * BLOCK
+    level_apart = (cell >= WH) != (other >= WH)
+    cell = jnp.where(cell >= WH, cell - WH, cell)
+    other = jnp.where(other >= WH, other - WH, other)
+    row_apart = (cell >= WH // 2) != (other >= WH // 2)
     top = lax.axis_index("lat") == lax.axis_size("lat") - 1
-    barred_rows = jnp.logical_and(row_apart[...] > 0, top)
+    barred_rows = jnp.logical_and(row_apart, top)
     for t in range(level_win):
         barred = barred_rows
         if t == level_win - 1:
-            barred = jnp.logical_or(barred, level_apart[...] > 0)
+            barred = jnp.logical_or(barred, level_apart)
         for h in range(heads):
-            row = 8 * t + h
+            row = t * heads + h
             tiles = []
             for tile in range(SPREAD // LANES):
                 at = slice(tile * LANES, (tile + 1) * LANES)
@@ -164,9 +178,7 @@
             value = jnp.where(barred, -LARGE, jnp.concatenate(tiles, 1))
             for a in range(WW):
                 shift = (WW - 1 - a) * BLOCK
-                out[t * heads + h, a * BLOCK : (a + 1) * BLOCK, :] = value[
-                    :BLOCK, shift : shift + WIN
-                ]
+                out[row, a * BLOCK : (a + 1) * BLOCK, :] = value[:BLOCK, shift : shift + WIN]
 
 
 def inverse_body(chunk, lane, chunk_out, lane_out):
@@ -215,16 +227,31 @@
 
 
 def window_body(
-    here, from_lon, from_lat, from_both, picks, norm_gain, norm_shift, w_qkv, w_out, bias,
-    out_here, out_lon, out_lat, out_both, keep, send, gathered, proj_grad, sums, tables,
+    here, from_lon, from_lat, from_both, norm_gain, norm_shift, w_qkv, w_out, bias,
+    out_here, out_lon, out_lat, keep, send, gathered, proj_grad, sums, tables,
 ):
     width = w_out.shape[0]
     level_win = bias.shape[0] // HEADS
     head_size = width // HEADS
     scaling = head_size ** (-0.5)
-    quads = jnp.concatenate([q[...] for q in (here, from_lon, from_lat, from_both)], 0)
-    features = jnp.dot(picks[...], quads[:, :width], preferred_element_type=f32)
-    cotangent = jnp.dot(picks[...], quads[:, width:], preferred_element_type=f32)
+    _, lat_half, lon_half, levels, _ = here.shape
+    quad_rows = lat_half * lon_half * PAD_LEVEL
+    fill = jnp.zeros((lat_half, lon_half, PAD_LEVEL - levels, width), f32)
+    picks = window_matrix(levels, PAD_LEVEL)
+    features, cotangent = (
+        jnp.dot(
+            picks,
+            jnp.concatenate(
+                [
+                    jnp.concatenate((quad[at].astype(f32), fill), 2).reshape(quad_rows, width)
+                    for quad in (here, from_lon, from_lat, from_both)
+                ],
+                0,
+            ).astype(bf16),
+            preferred_element_type=f32,
+        )
+        for at in range(2)
+    )
     grad_shifted = cotangent.astype(bf16)
     gain = norm_gain[...]
     center = features - jnp.mean(features, -1, keepdims=True)
@@ -305,19 +332,30 @@
         - x_hat * jnp.mean(g_hat * x_hat, -1, keepdims=True)
     )
     grad_features = (cotangent + inv_std * centred).astype(bf16)
-    for at, result in enumerate((outputs, grad_features)):
-        back = lax.dot_general(
-            picks[...], result, (((0,), (0,)), ((), ())), preferred_element_type=f32
-        ).astype(bf16)
-        for q, out in enumerate((out_here, out_lon, out_lat, out_both)):
-            out[:, at * width : (at + 1) * width] = back[q * PAD_QUAD : (q + 1) * PAD_QUAD]
+    picks = window_matrix(levels, levels)
+    back = [
+        lax.dot_general(picks, result, (((0,), (0,)), ((), ())), preferred_element_type=f32)
+        for result in (outputs, grad_features)
+    ]
+    rest = width - LANES
+    tiles = [b[:, :LANES] for b in back]
+    tiles.append(jnp.concatenate([b[:, LANES:] for b in back], 1))
+    size = gathered.shape[2]
+    groups = lat_half * lon_half * levels // size
+    for at, tile in enumerate(tiles):
+        for q, (out, first) in enumerate(
+            ((out_here, 0), (out_lon, 0), (out_lat, 0), (out_lat, 3 * groups))
+        ):
+            for i in range(groups):
+                row = (q * groups + i) * size
+                out[first + at * groups + i] = tile[row : row + size].astype(bf16)
     sums[:, : 3 * width] = lax.dot_general(
         normed, grad_proj, (((0,), (0,)), ((), ())), preferred_element_type=f32
     )
     sums[:, 3 * width :] = lax.dot_general(
         mixed, grad_shifted, (((0,), (0,)), ((), ())), preferred_element_type=f32
     )
-    chunks, blocks, size, _ = gathered.shape
+    chunks, blocks, _, _ = gathered.shape
     lat_count = chunks // 2
     edge = jnp.zeros((size - 4, LANES), f32)
     fill = jnp.zeros((1, 2 * LANES - width), f32)
@@ -336,7 +374,9 @@
     for half, out in enumerate((keep, send)):
         side = core ^ half
         for at in range(lat_count):
-            out[at * blocks : (at + 1) * blocks] = gathered[side * lat_count + (lat ^ at)]
+            out[at * blocks : (at + 1) * blocks] = gathered[
+                side * lat_count + lax.rem(lat + at, lat_count)
+            ]
         for h in range(0, HEADS, per):
             for tile in range(SPREAD // LANES):
                 block = jnp.concatenate([tables[side, h + i, tile] for i in range(per)], 0)
@@ -349,20 +389,26 @@
     return values[0]
 
 
-def halves_body(keep, came, *outs):
+def halves_body(keep, came, quads, *outs):
+    *pieces, tail = outs
+    blocks = pieces[0].shape[0]
     at = 0
     for out in outs:
-        count = out.shape[0]
+        count = tail.shape[0] if out is tail else blocks
         part = slice(at, at + count)
-        out[...] = (keep[part].astype(f32) + came[part].astype(f32)).astype(bf16)
+        out[:count] = (keep[part].astype(f32) + came[part].astype(f32)).astype(bf16)
         at += count
+    pieces[1][blocks:] = quads[...]
 
 
 def lats_body(*refs):
-    *pieces, tail, out = refs
+    *pieces, tail, quad, out, onward = refs
     blocks = pieces[0].shape[0]
-    out[:blocks] = tree([p[...].astype(f32) for p in pieces]).astype(bf16)
+    out[:blocks] = tree([p[:blocks].astype(f32) for p in pieces]).astype(bf16)
     out[blocks:] = tail[...]
+    count = quad.shape[0]
+    onward[:count] = quad[...]
+    onward[count:] = pieces[1][blocks + count :]
 
 
 def lons_body(count, *refs):
@@ -383,7 +429,7 @@
     _, blocks, size, _ = chunks.shape
     for half, group in enumerate((near, far)):
         for at, ref in enumerate(group):
-            chunks[(core ^ half) * lat_count + (lat ^ at)] = ref[...].astype(f32) * factor
+            chunks[(core ^ half) * lat_count + lax.rem(lat + lat_count - at, lat_count)] = ref[...].astype(f32) * factor
     halves[core] = table_near[...].astype(f32) * factor
     halves[core ^ 1] = table_far[...].astype(f32) * factor
     width = grad_wout.shape[0]
@@ -396,8 +442,10 @@
     for at, out in enumerate((grad_gain, grad_shift)):
         out[:, :LANES] = chunks[0, blocks - 1, 2 * at : 2 * at + 1]
         out[:, LANES:] = chunks[0, blocks - 1, 2 * at + 1 : 2 * at + 2, :rest]
-    for t in range(grad_table.shape[0]):
-        grad_table[t, 0] = halves[t, : grad_table.shape[2], : grad_table.shape[3]]
+    level_win, heads, _, labels = grad_table.shape
+    for t in range(level_win):
+        for h in range(heads):
+            grad_table[t, h] = halves[t, h : h + 1, :labels]
 
 
 def swap(value, axis, distance):
@@ -405,7 +453,7 @@
     return lax.ppermute(value, axis, [(source, source ^ distance) for source in range(count)])
 
 
-def send_back(value, lat_step, lon_step):
+def shifted(value, lat_step, lon_step):
     lat_count, lon_count = lax.axis_size("lat"), lax.axis_size("lon")
     pairs = [
         (r * lon_count + c, (r + lat_step) % lat_count * lon_count + (c + lon_step) % lon_count)
@@ -419,77 +467,105 @@
     levels, lat_rows, lon_cols, width = features.shape
     level_win, _, heads, labels = bias_table.shape
     lat_count, lon_count = lax.axis_size("lat"), lax.axis_size("lon")
-    grid = (levels, lat_rows, lon_cols)
-    to_quads, to_windows = pack_matrix(*grid), window_matrix(*grid)
-    quad = struct((PAD_QUAD, 2 * width), bf16)
+    quad = struct((2, WH // 2, WW // 2, levels, width), bf16)
     steps = ((0, 1), (1, 0), (1, 1))
 
-    here, *edges = call(pack_body, (quad,) * 4)(features, cotangent, to_quads)
-    came = [send_back(e, -lat, -lon) for e, (lat, lon) in zip(edges, steps)]
+    plain = (
+        norm_gain[None], norm_shift[None], w_qkv, w_out, bias_table.transpose(0, 2, 1, 3), index_table
+    )
+    far_side = pl.BlockSpec(memory_space=pltpu.HBM)
+    *packed, gain, shift, w_qkv, w_out, table, labels_of = call(
+        functools.partial(pack_body, len(plain)),
+        (quad,) * 4 + tuple(struct(p.shape, p.dtype) for p in plain),
+        [pltpu.SemaphoreType.DMA((8 + len(plain),))],
+        in_specs=[far_side] * (2 + len(plain)),
+    )(
+        *(
+            pltpu.with_memory_space_constraint(v, pltpu.HBM)
+            for v in (features.transpose(1, 2, 0, 3), cotangent.transpose(1, 2, 0, 3), *plain)
+        )
+    )
+    here, *edges = packed
+    came = [shifted(e, -lat, -lon) for e, (lat, lon) in zip(edges, steps)]
 
     spread = struct((16, SPREAD), jnp.int32)
+    whole_lanes = -(-labels // LANES) * LANES
     bias, chunk, lane = call(
         bias_body,
         (struct((level_win * heads, WIN, WIN), f32), spread, spread),
-        [pltpu.VMEM((8 * level_win, -(-labels // LANES) * LANES), f32)],
-        moved=4 * 10**6,
-    )(bias_table, index_table, *spread_matrices(), *apart())
+        [pltpu.VMEM((level_win * heads, whole_lanes), f32)],
+        moved=16 * 10**6,
+    )(table, labels_of)
 
     size = width // (2 * lat_count)
     blocks = 4 * width // LANES + 1
     table_blocks = HEADS * BLOCK * SPREAD // (size * LANES)
-    half = struct((lat_count * blocks + table_blocks, size, LANES), bf16)
-    out_here, *backs, keep, send = call(
+    quad_blocks = 2 * WH // 2 * WW // 2 * levels * width // (size * LANES)
+
+    def stack(count):
+        return struct((count, size, LANES), bf16)
+
+    half = stack(lat_count * blocks + table_blocks)
+    out_here, out_lon, out_lat, keep, send = call(
         window_body,
-        (quad,) * 4 + (half, half),
+        (stack(quad_blocks), stack(quad_blocks), stack(2 * quad_blocks), half, half),
         [
             pltpu.VMEM((2 * lat_count, blocks, size, LANES), bf16),
             pltpu.VMEM((level_win * WIN, 3 * width), bf16),
             pltpu.VMEM((width, 4 * width), f32),
             pltpu.VMEM((level_win, heads, SPREAD // LANES, BLOCK, LANES), f32),
         ],
-    )(here, *came, to_windows, norm_gain[None], norm_shift[None], w_qkv, w_out, bias)
-
-    returned = [send_back(b, lat, lon) for b, (lat, lon) in zip(backs, steps)]
-
-    chunk_shape = struct((blocks, size, LANES), bf16)
-    tail_shape = struct((table_blocks, size, LANES), bf16)
-    *pieces, tail = call(halves_body, (chunk_shape,) * lat_count + (tail_shape,))(
-        keep, swap(send, "lon", 1)
-    )
-    pieces = pieces[:1] + [swap(p, "lat", at + 1) for at, p in enumerate(pieces[1:])]
-    part = call(lats_body, struct((blocks + table_blocks, size, LANES), bf16))(*pieces, tail)
+        moved=25 * 10**6,
+    )(here, *came, gain, shift, w_qkv, w_out, bias)
+
+    shapes = [stack(blocks)] * lat_count + [stack(table_blocks)]
+    shapes[1] = stack(blocks + 2 * quad_blocks)
+    *pieces, tail = call(halves_body, tuple(shapes))(keep, swap(send, "lon", 1), out_lat)
+    pieces = [shifted(p, at, 0) if at else p for at, p in enumerate(pieces)]
+    part, onward = call(lats_body, (stack(blocks + table_blocks), stack(2 * quad_blocks)))(
+        *pieces, tail, out_lon
+    )
     parts = [part] + [swap(part, "lon", 2 * at) for at in range(1, lon_count // 2)]
-    weights, tail = call(functools.partial(lons_body, len(parts)), (chunk_shape, tail_shape))(*parts)
-    near = [weights] + [swap(weights, "lat", at) for at in range(1, lat_count)]
-
+    lon_pair = shifted(onward, 0, 1)
+    part, chunk, lane = lax.optimization_barrier((part, chunk, lane))
     places = struct((32, LANES), jnp.int32)
-    piece, spot = call(inverse_body, (places, places))(chunk, lane)
-    table_near = call(place_body, struct((8, -(-labels // LANES) * LANES), bf16))(tail, piece, spot)
+    piece, spot = call(inverse_body, (places, places), moved=2 * 10**6)(chunk, lane)
+    weights, tail = call(functools.partial(lons_body, len(parts)), (stack(blocks), stack(table_blocks)))(
+        *parts
+    )
+    near = [weights] + [shifted(weights, at, 0) for at in range(1, lat_count)]
+    table_near = call(place_body, struct((8, whole_lanes), bf16), moved=5 * 10**6)(tail, piece, spot)
     table_far = swap(table_near, "lon", 1)
     far = [swap(n, "lon", 1) for n in near]
 
-    outputs, grad_features = call(unpack_body, (struct(features.shape, bf16),) * 2)(
-        out_here, *returned, to_quads
+    cells = struct((lat_rows, lon_cols, levels, width), bf16)
+    outputs, grad_features = call(unpack_body, (cells, cells), moved=2 * 10**6)(
+        out_here, pieces[1], lon_pair
     )
     factor = (levels * lat_rows * lat_count * lon_cols * lon_count) ** (-0.5)
     row = struct((1, width), f32)
     grad_gain, grad_shift, grad_wqkv, grad_wout, grad_table = call(
         functools.partial(finish_body, lat_count, factor),
-        (row, row, struct(w_qkv.shape, f32), struct(w_out.shape, f32), struct(bias_table.shape, f32)),
+        (
+            row,
+            row,
+            struct(w_qkv.shape, f32),
+            struct(w_out.shape, f32),
+            struct((level_win, heads, 1, labels), f32),
+        ),
         [
             pltpu.VMEM((2 * lat_count, blocks, size, LANES), f32),
             pltpu.VMEM((2,) + table_near.shape, f32),
         ],
     )(*near, *far, table_near, table_far)
     return (
-        outputs,
-        grad_features,
+        outputs.transpose(2, 0, 1, 3),
+        grad_features.transpose(2, 0, 1, 3),
         grad_gain[0],
         grad_shift[0],
         grad_wqkv,
         grad_wout,
-        grad_table,
+        grad_table.transpose(0, 2, 1, 3),
     )
 
 

time: 57.8 us -> 51.6 us (0.89)
  local copies, waits for them, and re-layouts: 10.4 us -> 0 us
  waiting for transfers between devices: 8.79 us -> 12.4 us
  Pallas kernels: 16.4 us -> 17.9 us
    unnamed x30 -> x0, local copies, waits for them, and re-layouts: 10.4 us -> none
    ppermute x15 -> x9, starting transfers between devices: 13 us -> 5.88 us  [swap(): lax.ppermute(value, axis, [(source, source ^ distance) for source in rang...]
    ppermute x6 -> x10, starting transfers between devices: 7.89 us -> 14.6 us  [shifted(): return lax.ppermute(value, ('lat', 'lon'), pairs)]
    ppermute x6 -> x10, waiting for transfers between devices: 0.16 us -> 4.67 us  [shifted(): return lax.ppermute(value, ('lat', 'lon'), pairs)]
    pallas_call x8, Pallas kernels: 10 us -> 11.4 us  [the longest x1 6.94 us: on_device(): call(window_body, (stack(quad_blocks), stack(quad_blocks), stack(2 * quad...]
    ppermute x15 -> x9, waiting for transfers between devices: 8.63 us -> 7.68 us  [swap(): lax.ppermute(value, axis, [(source, source ^ distance) for source in rang...]
  transfers between devices with their start and end apart: 21 -> 19, of which waited for: 7 -> 6; matrix products, arithmetic and copies ran while one was open for 4% -> 0% of each run, Pallas kernels for 14% -> 16%
where the time goes in v2:
time: 51.6 us; the launch traced here: 51.4 us
  starting transfers between devices  20.5 us (40%)
  Pallas kernels  17.9 us (35%)
  waiting for transfers between devices  12.4 us (24%)
  between operations  0.75 us (1%)
    ppermute x10, starting transfers between devices, shifted(): return lax.ppermute(value, ('lat', 'lon'), pairs)  14.6 us
    ppermute x9, waiting for transfers between devices, swap(): lax.ppermute(value, axis, [(source, source ^ distance) for source in rang...  7.68 us
    pallas_call x1, Pallas kernels, on_device(): call(window_body, (stack(quad_blocks), stack(quad_blocks), stack(2 * quad...  6.94 us
    ppermute x9, starting transfers between devices, swap(): lax.ppermute(value, axis, [(source, source ^ distance) for source in rang...  5.88 us
    pallas_call x1, Pallas kernels, on_device(): call(bias_body, (struct((level_win * heads, WIN, WIN), f32), spread, spre...  5.44 us
    ppermute x10, waiting for transfers between devices, shifted(): return lax.ppermute(value, ('lat', 'lon'), pairs)  4.67 us
    pallas_call x1, Pallas kernels, on_device(): call(place_body, struct((8, whole_lanes), bf16), moved=5 * 10 ** 6)  1.47 us
    pallas_call x1, Pallas kernels, on_device(): call(functools.partial(pack_body, len(plain)), (quad,) * 4 + tuple((struc...  1.42 us
  transfers between devices with their start and end apart: 19, of which 6 were waited for; matrix products, arithmetic and copies ran while one was open for 0% of the time, Pallas kernels for 16%

profile of v2, /device:TPU:0, one launch (start us, length us, event | category | flops | bytes accessed | tf_op | source)
XLA Modules:
  0.0 51.4 jit_solution(7050370730045005894)
XLA Ops:
  0.6 1.4 %shard_map.135 = (bf16[2,3,6,4,192]{4,3,2,1,0:T(4,128)(2,1)S(1)}, bf16[2,3,6,4,192]{4,3,2,1,0:T(4,128)(2,1)S(1)}, bf16[2,3,6,4,192]{4,3,2,1,0:T(4,128)(2,1)S(1)}...) custom-call(bf16[6,12,4,192]{3,2,1,0:T(4,128)(2,1)} %bitcast.11, ...), custom_call_target="tpu_custom_call" | custom-call | tf_op jit(solution)/shard_map/pallas_call | solution.py:477
  2.1 4.5 %collective-permute-start = (bf16[2,3,6,4,192]{4,3,2,1,0:T(4,128)(2,1)S(1)}, bf16[2,3,6,4,192]{4,3,2,1,0:T(4,128)(2,1)S(1)}, u32[]{:S(2)}, u32[]{:S(2)}) collective-permute-start(bf16[2,3,6,4,192]{4,3,2,1,0:T(4,128)(2,1)S(1)} %get-tuple-element.46), channel_id=1, source_target_pairs={{0,7},{1,0},{2,1},{3,2},{4,3},{5,4},{6,5},{7,6},{8,15},{9,8},{10,9... | collective-permute-start | bytes 165896 | tf_op jit(solution)/shard_map/ppermute | solution.py:463
  6.6 2.4 %collective-permute-start.1 = (bf16[2,3,6,4,192]{4,3,2,1,0:T(4,128)(2,1)S(1)}, bf16[2,3,6,4,192]{4,3,2,1,0:T(4,128)(2,1)S(1)}, u32[]{:S(2)}, u32[]{:S(2)}) collective-permute-start(bf16[2,3,6,4,192]{4,3,2,1,0:T(4,128)(2,1)S(1)} %get-tuple-element.47), channel_id=1, source_target_pairs={{0,24},{1,25},{2,26},{3,27},{4,28},{5,29},{6,30},{7,31},{8,0},{9,1... | collective-permute-start | bytes 165896 | tf_op jit(solution)/shard_map/ppermute | solution.py:463
  9.0 0.4 collective-permute-start.2
  9.4 5.4 %shard_map.136 = (f32[12,144,144]{2,1,0:T(8,128)S(1)}, s32[16,384]{1,0:T(8,128)S(1)}, s32[16,384]{1,0:T(8,128)S(1)}) custom-call(f32[2,6,1,3312]{3,2,1,0:T(1,128)S(1)} %get-tuple-element.53.bias_table, s32[144,144]{1,0:T(8,128)S(1)} %get-tuple-element.54.index_table), custom_call_target="tpu_custom_call" | custom-call | bytes 16000000 | tf_op jit(solution)/shard_map/pallas_call | solution.py:493
  14.9 0.0 collective-permute-done.from_lon
  14.9 0.0 collective-permute-done.1.from_lat
  14.9 0.0 collective-permute-done.2.from_both
  14.9 6.9 %shard_map.137 = (bf16[9,24,128]{2,1,0:T(8,128)(2,1)S(1)}, bf16[9,24,128]{2,1,0:T(8,128)(2,1)S(1)}, bf16[18,24,128]{2,1,0:T(8,128)(2,1)S(1)}, bf16[37,24,128]{2,1,0:T(8,128)(2,1)S(1)}, bf16[37,24,128]{2,1,0:T(8,128)(2,1)S(1)}) custom-call(bf16[2,3,6,4,192]{4,3,2,1,0:T(4,128)(2,1)S(1)} %get-tuple-element.45.here, ...), custom_call_target="tpu_custom_call" | custom-call | bytes 25000000 | tf_op jit(solution)/shard_map/pallas_call | solution.py:509
  21.8 0.4 collective-permute-start.3
  22.2 1.2 %collective-permute-done.3.came = bf16[37,24,128]{2,1,0:T(8,128)(2,1)S(1)} collective-permute-done((bf16[37,24,128]{2,1,0:T(8,128)(2,1)S(1)}, bf16[37,24,128]{2,1,0:T(8,128)(2,1)S(1)}, u32[]{:S(2)}, u32[]{:S(2)}) %collective-permute-start.3) | collective-permute-done | bytes 227360 | tf_op jit(solution)/shard_map/ppermute | solution.py:453
  23.4 0.1 shard_map.138
  23.5 1.5 %collective-permute-start.4 = (bf16[25,24,128]{2,1,0:T(8,128)(2,1)S(1)}, bf16[25,24,128]{2,1,0:T(8,128)(2,1)S(1)}, u32[]{:S(2)}, u32[]{:S(2)}) collective-permute-start(bf16[25,24,128]{2,1,0:T(8,128)(2,1)S(1)} %get-tuple-element.60), channel_id=1, source_target_pairs={{0,8},{1,9},{2,10},{3,11},{4,12},{5,13},{6,14},{7,15},{8,16},{9,17... | collective-permute-start | bytes 460808 | tf_op jit(solution)/shard_map/ppermute | solution.py:463
  25.0 0.5 collective-permute-start.5
  25.5 1.4 %collective-permute-start.6 = (bf16[7,24,128]{2,1,0:T(8,128)(2,1)S(1)}, bf16[7,24,128]{2,1,0:T(8,128)(2,1)S(1)}, u32[]{:S(2)}, u32[]{:S(2)}) collective-permute-start(bf16[7,24,128]{2,1,0:T(8,128)(2,1)S(1)} %get-tuple-element.63), channel_id=1, source_target_pairs={{0,24},{1,25},{2,26},{3,27},{4,28},{5,29},{6,30},{7,31},{8,0},{9,1... | collective-permute-start | bytes 129032 | tf_op jit(solution)/shard_map/ppermute | solution.py:463
  26.9 4.6 %collective-permute-done.5.refs_2_ = bf16[7,24,128]{2,1,0:T(8,128)(2,1)S(1)} collective-permute-done((bf16[7,24,128]{2,1,0:T(8,128)(2,1)S(1)}, bf16[7,24,128]{2,1,0:T(8,128)(2,1)S(1)}, u32[]{:S(2)}, u32[]{:S(2)}) %collective-permute-start.5) | collective-permute-done | bytes 43040 | tf_op jit(solution)/shard_map/ppermute | solution.py:463
  31.5 0.0 collective-permute-done.6.refs_3_
  31.5 0.0 collective-permute-done.4.refs_1_.lat_piece
  31.5 1.0 %collective-permute-start.10 = (bf16[16,24,128]{2,1,0:T(8,128)(2,1)S(1)}, bf16[16,24,128]{2,1,0:T(8,128)(2,1)S(1)}, u32[]{:S(2)}, u32[]{:S(2)}) collective-permute-start(bf16[16,24,128]{2,1,0:T(8,128)(2,1)S(1)} %get-tuple-element.69.refs_0_), channel_id=1, source_target_pairs={{0,6},{1,7},{2,4},{3,5},{4,2},{5,3},{6,0},{7,1},{8,14},{9,15},{10,... | collective-permute-start | bytes 294920 | tf_op jit(solution)/shard_map/ppermute | solution.py:453
  32.6 0.0 collective-permute-start.9
  32.6 3.4 %collective-permute-start.8 = (bf16[16,24,128]{2,1,0:T(8,128)(2,1)S(1)}, bf16[16,24,128]{2,1,0:T(8,128)(2,1)S(1)}, u32[]{:S(2)}, u32[]{:S(2)}) collective-permute-start(bf16[16,24,128]{2,1,0:T(8,128)(2,1)S(1)} %get-tuple-element.69.refs_0_), channel_id=1, source_target_pairs={{0,2},{1,3},{2,0},{3,1},{4,6},{5,7},{6,4},{7,5},{8,10},{9,11},{10,... | collective-permute-start | bytes 294920 | tf_op jit(solution)/shard_map/ppermute | solution.py:453
  36.0 0.0 collective-permute-start.7
  36.0 3.2 %collective-permute-done.10.refs_3_ = bf16[16,24,128]{2,1,0:T(8,128)(2,1)S(1)} collective-permute-done((bf16[16,24,128]{2,1,0:T(8,128)(2,1)S(1)}, bf16[16,24,128]{2,1,0:T(8,128)(2,1)S(1)}, u32[]{:S(2)}, u32[]{:S(2)}) %collective-permute-start.10) | collective-permute-done | bytes 98336 | tf_op jit(solution)/shard_map/ppermute | solution.py:453
  39.2 2.9 %collective-permute-done.9.refs_2_ = bf16[16,24,128]{2,1,0:T(8,128)(2,1)S(1)} collective-permute-done((bf16[16,24,128]{2,1,0:T(8,128)(2,1)S(1)}, bf16[16,24,128]{2,1,0:T(8,128)(2,1)S(1)}, u32[]{:S(2)}, u32[]{:S(2)}) %collective-permute-start.9) | collective-permute-done | bytes 98336 | tf_op jit(solution)/shard_map/ppermute | solution.py:453
  42.1 0.0 collective-permute-done.8.refs_1_
  42.1 0.1 shard_map.141
  42.1 0.7 %collective-permute-start.13 = (bf16[7,24,128]{2,1,0:T(8,128)(2,1)S(1)}, bf16[7,24,128]{2,1,0:T(8,128)(2,1)S(1)}, u32[]{:S(2)}, u32[]{:S(2)}) collective-permute-start(bf16[7,24,128]{2,1,0:T(8,128)(2,1)S(1)} %get-tuple-element.70.refs_0_), channel_id=1, source_target_pairs={{0,24},{1,25},{2,26},{3,27},{4,28},{5,29},{6,30},{7,31},{8,0},{9,1... | collective-permute-start | bytes 129032 | tf_op jit(solution)/shard_map/ppermute | solution.py:463
  42.8 1.4 %collective-permute-start.12 = (bf16[7,24,128]{2,1,0:T(8,128)(2,1)S(1)}, bf16[7,24,128]{2,1,0:T(8,128)(2,1)S(1)}, u32[]{:S(2)}, u32[]{:S(2)}) collective-permute-start(bf16[7,24,128]{2,1,0:T(8,128)(2,1)S(1)} %get-tuple-element.70.refs_0_), channel_id=1, source_target_pairs={{0,16},{1,17},{2,18},{3,19},{4,20},{5,21},{6,22},{7,23},{8,24},{9,... | collective-permute-start | bytes 129032 | tf_op jit(solution)/shard_map/ppermute | solution.py:463
  44.3 1.6 %collective-permute-start.11 = (bf16[7,24,128]{2,1,0:T(8,128)(2,1)S(1)}, bf16[7,24,128]{2,1,0:T(8,128)(2,1)S(1)}, u32[]{:S(2)}, u32[]{:S(2)}) collective-permute-start(bf16[7,24,128]{2,1,0:T(8,128)(2,1)S(1)} %get-tuple-element.70.refs_0_), channel_id=1, source_target_pairs={{0,8},{1,9},{2,10},{3,11},{4,12},{5,13},{6,14},{7,15},{8,16},{9,17... | collective-permute-start | bytes 129032 | tf_op jit(solution)/shard_map/ppermute | solution.py:463
  45.9 0.6 %shard_map.142 = (s32[32,128]{1,0:T(8,128)S(1)}, s32[32,128]{1,0:T(8,128)S(1)}) custom-call(s32[16,384]{1,0:T(8,128)S(1)} %get-tuple-element.74.chunk, s32[16,384]{1,0:T(8,128)S(1)} %get-tuple-element.75.lane), custom_call_target="tpu_custom_call" | custom-call | bytes 2000000 | tf_op jit(solution)/shard_map/pallas_call | solution.py:532
  46.5 1.5 %shard_map.143.refs_8_ = bf16[8,3328]{1,0:T(8,128)(2,1)S(1)} custom-call(bf16[9,24,128]{2,1,0:T(8,128)(2,1)S(1)} %get-tuple-element.71.blocks, s32[32,128]{1,0:T(8,128)S(1)} %get-tuple-element.76.piece, s32[32,128]{1,0:T(8,128)S(1)} %get-tuple-element.77.spot), custom_call_target="tpu_custom_call" | custom-call | bytes 5000000 | tf_op jit(solution)/shard_map/pallas_call | solution.py:537
  48.0 0.1 collective-permute-start.18
  48.1 0.0 collective-permute-done.7.lon_pair
  48.1 0.5 collective-permute-start.14
  48.6 0.0 collective-permute-done.13.refs_3_
  48.6 0.1 collective-permute-start.17
  48.7 0.0 collective-permute-done.12.refs_2_
  48.7 0.4 collective-permute-start.16
  49.1 0.1 collective-permute-done.11.refs_1_
  49.2 0.0 collective-permute-start.15
  49.2 0.8 %shard_map.140 = (bf16[6,12,4,192]{3,2,1,0:T(4,128)(2,1)}, bf16[6,12,4,192]{3,2,1,0:T(4,128)(2,1)}) custom-call(bf16[9,24,128]{2,1,0:T(8,128)(2,1)S(1)} %get-tuple-element.56.here, bf16[25,24,128]{2,1,0:T(8,128)(2,1)S(1)} %collective-permute-done.4.refs_1_.lat_piece, bf16[18,24,128]{2,1,0:T(8,128)(2,1)S(1)} %collective-permute-done.7.lon_pair), custom_call_target="tpu_custom_call" | custom-call | bytes 2000000 | tf_op jit(solution)/shard_map/pallas_call | solution.py:542
  50.0 0.0 collective-permute-done.14.refs_4_
  50.0 0.0 collective-permute-done.18.refs_9_
  50.0 0.0 collective-permute-done.17.refs_7_
  50.0 0.0 collective-permute-done.16.refs_6_
  50.0 0.4 collective-permute-done.15.refs_5_
  50.4 1.0 %shard_map.144 = (f32[1,192]{1,0:T(1,128)}, f32[1,192]{1,0:T(1,128)}, f32[192,576]{1,0:T(8,128)}, f32[192,192]{1,0:T(8,128)}, f32[2,6,1,3312]{3,2,1,0:T(1,128)}) custom-call(bf16[7,24,128]{2,1,0:T(8,128)(2,1)S(1)} %get-tuple-element.70.refs_0_, bf16[7,24,128]{2,1,0:T(8,128)(2,1)S(1)} %collective-permute-done.11.refs_1_, ...), custom_call_target="tpu_custom_call" | custom-call | tf_op jit(solution)/shard_map/pallas_call | solution.py:547
  (1 shorter events, 0.0 us)
Async XLA Ops:
  2.1 12.8 %collective-permute-start = (bf16[2,3,6,4,192]{4,3,2,1,0:T(4,128)(2,1)S(1)}, bf16[2,3,6,4,192]{4,3,2,1,0:T(4,128)(2,1)S(1)}, u32[]{:S(2)}, u32[]{:S(2)}) collective-permute-start(bf16[2,3,6,4,192]{4,3,2,1,0:T(4,128)(2,1)S(1)} %get-tuple-element.46), channel_id=1, source_target_pairs={{0,7},{1,0},{2,1},{3,2},{4,3},{5,4},{6,5},{7,6},{8,15},{9,8},{10,9... | collective-permute-start | bytes 165896 | tf_op jit(solution)/shard_map/ppermute | solution.py:463
  6.6 8.3 %collective-permute-start.1 = (bf16[2,3,6,4,192]{4,3,2,1,0:T(4,128)(2,1)S(1)}, bf16[2,3,6,4,192]{4,3,2,1,0:T(4,128)(2,1)S(1)}, u32[]{:S(2)}, u32[]{:S(2)}) collective-permute-start(bf16[2,3,6,4,192]{4,3,2,1,0:T(4,128)(2,1)S(1)} %get-tuple-element.47), channel_id=1, source_target_pairs={{0,24},{1,25},{2,26},{3,27},{4,28},{5,29},{6,30},{7,31},{8,0},{9,1... | collective-permute-start | bytes 165896 | tf_op jit(solution)/shard_map/ppermute | solution.py:463
  9.0 5.8 %collective-permute-start.2 = (bf16[2,3,6,4,192]{4,3,2,1,0:T(4,128)(2,1)S(1)}, bf16[2,3,6,4,192]{4,3,2,1,0:T(4,128)(2,1)S(1)}, u32[]{:S(2)}, u32[]{:S(2)}) collective-permute-start(bf16[2,3,6,4,192]{4,3,2,1,0:T(4,128)(2,1)S(1)} %get-tuple-element.48), channel_id=1, source_target_pairs={{0,31},{1,24},{2,25},{3,26},{4,27},{5,28},{6,29},{7,30},{8,7},{9,0... | collective-permute-start | bytes 165896 | tf_op jit(solution)/shard_map/ppermute | solution.py:463
  21.8 1.6 %collective-permute-start.3 = (bf16[37,24,128]{2,1,0:T(8,128)(2,1)S(1)}, bf16[37,24,128]{2,1,0:T(8,128)(2,1)S(1)}, u32[]{:S(2)}, u32[]{:S(2)}) collective-permute-start(bf16[37,24,128]{2,1,0:T(8,128)(2,1)S(1)} %get-tuple-element.58), channel_id=1, source_target_pairs={{0,1},{1,0},{2,3},{3,2},{4,5},{5,4},{6,7},{7,6},{8,9},{9,8},{10,11... | collective-permute-start | bytes 681992 | tf_op jit(solution)/shard_map/ppermute | solution.py:453
  23.5 8.0 %collective-permute-start.4 = (bf16[25,24,128]{2,1,0:T(8,128)(2,1)S(1)}, bf16[25,24,128]{2,1,0:T(8,128)(2,1)S(1)}, u32[]{:S(2)}, u32[]{:S(2)}) collective-permute-start(bf16[25,24,128]{2,1,0:T(8,128)(2,1)S(1)} %get-tuple-element.60), channel_id=1, source_target_pairs={{0,8},{1,9},{2,10},{3,11},{4,12},{5,13},{6,14},{7,15},{8,16},{9,17... | collective-permute-start | bytes 460808 | tf_op jit(solution)/shard_map/ppermute | solution.py:463
  25.0 6.5 %collective-permute-start.5 = (bf16[7,24,128]{2,1,0:T(8,128)(2,1)S(1)}, bf16[7,24,128]{2,1,0:T(8,128)(2,1)S(1)}, u32[]{:S(2)}, u32[]{:S(2)}) collective-permute-start(bf16[7,24,128]{2,1,0:T(8,128)(2,1)S(1)} %get-tuple-element.62), channel_id=1, source_target_pairs={{0,16},{1,17},{2,18},{3,19},{4,20},{5,21},{6,22},{7,23},{8,24},{9,... | collective-permute-start | bytes 129032 | tf_op jit(solution)/shard_map/ppermute | solution.py:463
  25.5 6.0 %collective-permute-start.6 = (bf16[7,24,128]{2,1,0:T(8,128)(2,1)S(1)}, bf16[7,24,128]{2,1,0:T(8,128)(2,1)S(1)}, u32[]{:S(2)}, u32[]{:S(2)}) collective-permute-start(bf16[7,24,128]{2,1,0:T(8,128)(2,1)S(1)} %get-tuple-element.63), channel_id=1, source_target_pairs={{0,24},{1,25},{2,26},{3,27},{4,28},{5,29},{6,30},{7,31},{8,0},{9,1... | collective-permute-start | bytes 129032 | tf_op jit(solution)/shard_map/ppermute | solution.py:463
  31.5 7.6 %collective-permute-start.10 = (bf16[16,24,128]{2,1,0:T(8,128)(2,1)S(1)}, bf16[16,24,128]{2,1,0:T(8,128)(2,1)S(1)}, u32[]{:S(2)}, u32[]{:S(2)}) collective-permute-start(bf16[16,24,128]{2,1,0:T(8,128)(2,1)S(1)} %get-tuple-element.69.refs_0_), channel_id=1, source_target_pairs={{0,6},{1,7},{2,4},{3,5},{4,2},{5,3},{6,0},{7,1},{8,14},{9,15},{10,... | collective-permute-start | bytes 294920 | tf_op jit(solution)/shard_map/ppermute | solution.py:453
  32.6 9.5 %collective-permute-start.9 = (bf16[16,24,128]{2,1,0:T(8,128)(2,1)S(1)}, bf16[16,24,128]{2,1,0:T(8,128)(2,1)S(1)}, u32[]{:S(2)}, u32[]{:S(2)}) collective-permute-start(bf16[16,24,128]{2,1,0:T(8,128)(2,1)S(1)} %get-tuple-element.69.refs_0_), channel_id=1, source_target_pairs={{0,4},{1,5},{2,6},{3,7},{4,0},{5,1},{6,2},{7,3},{8,12},{9,13},{10,... | collective-permute-start | bytes 294920 | tf_op jit(solution)/shard_map/ppermute | solution.py:453
  32.6 9.5 %collective-permute-start.8 = (bf16[16,24,128]{2,1,0:T(8,128)(2,1)S(1)}, bf16[16,24,128]{2,1,0:T(8,128)(2,1)S(1)}, u32[]{:S(2)}, u32[]{:S(2)}) collective-permute-start(bf16[16,24,128]{2,1,0:T(8,128)(2,1)S(1)} %get-tuple-element.69.refs_0_), channel_id=1, source_target_pairs={{0,2},{1,3},{2,0},{3,1},{4,6},{5,7},{6,4},{7,5},{8,10},{9,11},{10,... | collective-permute-start | bytes 294920 | tf_op jit(solution)/shard_map/ppermute | solution.py:453
  36.0 12.1 %collective-permute-start.7 = (bf16[18,24,128]{2,1,0:T(8,128)(2,1)S(1)}, bf16[18,24,128]{2,1,0:T(8,128)(2,1)S(1)}, u32[]{:S(2)}, u32[]{:S(2)}) collective-permute-start(bf16[18,24,128]{2,1,0:T(8,128)(2,1)S(1)} %get-tuple-element.66), channel_id=1, source_target_pairs={{0,1},{1,2},{2,3},{3,4},{4,5},{5,6},{6,7},{7,0},{8,9},{9,10},{10,1... | collective-permute-start | bytes 331784 | tf_op jit(solution)/shard_map/ppermute | solution.py:463
  42.1 6.5 %collective-permute-start.13 = (bf16[7,24,128]{2,1,0:T(8,128)(2,1)S(1)}, bf16[7,24,128]{2,1,0:T(8,128)(2,1)S(1)}, u32[]{:S(2)}, u32[]{:S(2)}) collective-permute-start(bf16[7,24,128]{2,1,0:T(8,128)(2,1)S(1)} %get-tuple-element.70.refs_0_), channel_id=1, source_target_pairs={{0,24},{1,25},{2,26},{3,27},{4,28},{5,29},{6,30},{7,31},{8,0},{9,1... | collective-permute-start | bytes 129032 | tf_op jit(solution)/shard_map/ppermute | solution.py:463
  42.8 5.9 %collective-permute-start.12 = (bf16[7,24,128]{2,1,0:T(8,128)(2,1)S(1)}, bf16[7,24,128]{2,1,0:T(8,128)(2,1)S(1)}, u32[]{:S(2)}, u32[]{:S(2)}) collective-permute-start(bf16[7,24,128]{2,1,0:T(8,128)(2,1)S(1)} %get-tuple-element.70.refs_0_), channel_id=1, source_target_pairs={{0,16},{1,17},{2,18},{3,19},{4,20},{5,21},{6,22},{7,23},{8,24},{9,... | collective-permute-start | bytes 129032 | tf_op jit(solution)/shard_map/ppermute | solution.py:463
  44.3 4.9 %collective-permute-start.11 = (bf16[7,24,128]{2,1,0:T(8,128)(2,1)S(1)}, bf16[7,24,128]{2,1,0:T(8,128)(2,1)S(1)}, u32[]{:S(2)}, u32[]{:S(2)}) collective-permute-start(bf16[7,24,128]{2,1,0:T(8,128)(2,1)S(1)} %get-tuple-element.70.refs_0_), channel_id=1, source_target_pairs={{0,8},{1,9},{2,10},{3,11},{4,12},{5,13},{6,14},{7,15},{8,16},{9,17... | collective-permute-start | bytes 129032 | tf_op jit(solution)/shard_map/ppermute | solution.py:463
  48.0 2.0 %collective-permute-start.18 = (bf16[8,3328]{1,0:T(8,128)(2,1)S(1)}, bf16[8,3328]{1,0:T(8,128)(2,1)S(1)}, u32[]{:S(2)}, u32[]{:S(2)}) collective-permute-start(bf16[8,3328]{1,0:T(8,128)(2,1)S(1)} %shard_map.143.refs_8_), channel_id=1, source_target_pairs={{0,1},{1,0},{2,3},{3,2},{4,5},{5,4},{6,7},{7,6},{8,9},{9,8},{10,11... | collective-permute-start | bytes 159752 | tf_op jit(solution)/shard_map/ppermute | solution.py:453
  48.1 1.9 %collective-permute-start.14 = (bf16[7,24,128]{2,1,0:T(8,128)(2,1)S(1)}, bf16[7,24,128]{2,1,0:T(8,128)(2,1)S(1)}, u32[]{:S(2)}, u32[]{:S(2)}) collective-permute-start(bf16[7,24,128]{2,1,0:T(8,128)(2,1)S(1)} %get-tuple-element.70.refs_0_), channel_id=1, source_target_pairs={{0,1},{1,0},{2,3},{3,2},{4,5},{5,4},{6,7},{7,6},{8,9},{9,8},{10,11... | collective-permute-start | bytes 129032 | tf_op jit(solution)/shard_map/ppermute | solution.py:453
  48.6 1.4 %collective-permute-start.17 = (bf16[7,24,128]{2,1,0:T(8,128)(2,1)S(1)}, bf16[7,24,128]{2,1,0:T(8,128)(2,1)S(1)}, u32[]{:S(2)}, u32[]{:S(2)}) collective-permute-start(bf16[7,24,128]{2,1,0:T(8,128)(2,1)S(1)} %collective-permute-done.13.refs_3_), channel_id=1, source_target_pairs={{0,1},{1,0},{2,3},{3,2},{4,5},{5,4},{6,7},{7,6},{8,9},{9,8},{10,11... | collective-permute-start | bytes 129032 | tf_op jit(solution)/shard_map/ppermute | solution.py:453
  48.7 1.3 %collective-permute-start.16 = (bf16[7,24,128]{2,1,0:T(8,128)(2,1)S(1)}, bf16[7,24,128]{2,1,0:T(8,128)(2,1)S(1)}, u32[]{:S(2)}, u32[]{:S(2)}) collective-permute-start(bf16[7,24,128]{2,1,0:T(8,128)(2,1)S(1)} %collective-permute-done.12.refs_2_), channel_id=1, source_target_pairs={{0,1},{1,0},{2,3},{3,2},{4,5},{5,4},{6,7},{7,6},{8,9},{9,8},{10,11... | collective-permute-start | bytes 129032 | tf_op jit(solution)/shard_map/ppermute | solution.py:453
  49.2 1.2 %collective-permute-start.15 = (bf16[7,24,128]{2,1,0:T(8,128)(2,1)S(1)}, bf16[7,24,128]{2,1,0:T(8,128)(2,1)S(1)}, u32[]{:S(2)}, u32[]{:S(2)}) collective-permute-start(bf16[7,24,128]{2,1,0:T(8,128)(2,1)S(1)} %collective-permute-done.11.refs_1_), channel_id=1, source_target_pairs={{0,1},{1,0},{2,3},{3,2},{4,5},{5,4},{6,7},{7,6},{8,9},{9,8},{10,11... | collective-permute-start | bytes 129032 | tf_op jit(solution)/shard_map/ppermute | solution.py:453

commit v3 on v2

--- a/solution.py
+++ b/solution.py
@@ -17,6 +17,9 @@
 SPREAD = 384
 LANES = 128
 PAD_LEVEL = 8
+SUBLANES = 8
+TAIL = SPANS * BLOCK - 2 * LANES
+TABLE_ROWS = 2 * HEADS * BLOCK + 16
 LARGE = 1e30
 
 epsilon = 1e-05
@@ -93,18 +96,12 @@
         copy.wait()
 
 
-def unpack_body(here, lat_piece, lon_pair, outputs, grad_features):
+def unpack_body(here, from_lon, from_lat, from_both, outputs, grad_features):
     lat_rows, lon_cols, levels, width = outputs.shape
-    blocks = here.shape[0]
-    start = lat_piece.shape[0] - 2 * blocks
-    quads = (
-        here[...],
-        lon_pair[:blocks],
-        lat_piece[start : start + blocks],
-        lon_pair[blocks:],
-    )
-    for (rows, cols), quad in zip(quadrants(lat_rows, lon_cols), quads):
-        tiles = quad.astype(f32).reshape(3, -1, LANES)
+    for (rows, cols), quad in zip(
+        quadrants(lat_rows, lon_cols), (here, from_lon, from_lat, from_both)
+    ):
+        tiles = quad[...].astype(f32).reshape(3, -1, LANES)
         rest = width - LANES
         pair = (
             jnp.concatenate((tiles[0], tiles[2][:, :rest]), 1),
@@ -201,26 +198,28 @@
 
 
 def place_body(blocks, piece, spot, out):
-    count, rows, _ = blocks.shape
-    per = rows // BLOCK
     pieces = SPREAD // LANES
-    chunks = piece.shape[0]
-    at_piece = [jnp.broadcast_to(piece[c : c + 1, :], (8, LANES)) for c in range(out.shape[1] // LANES)]
-    at_spot = [jnp.broadcast_to(spot[c : c + 1, :], (8, LANES)) for c in range(out.shape[1] // LANES)]
-    found = [jnp.zeros((8, LANES), f32) for _ in at_piece]
-    values = [blocks[b].astype(f32) for b in range(count)]
+    head = columns((SUBLANES, 1), 0)
+    at_piece, at_spot, at_tail = [], [], []
+    for c in range(out.shape[1] // LANES):
+        at_piece.append(jnp.broadcast_to(piece[c : c + 1, :], (SUBLANES, LANES)))
+        at_spot.append(jnp.broadcast_to(spot[c : c + 1, :], (SUBLANES, LANES)))
+        at_tail.append((at_spot[c] + TAIL * head) & (LANES - 1))
+    found = [jnp.zeros((SUBLANES, LANES), f32) for _ in at_piece]
+    values = blocks[...].astype(f32).reshape(TABLE_ROWS, LANES)
+    fill = jnp.zeros((SUBLANES - HEADS, LANES), f32)
     for cell in range(BLOCK):
         for tile in range(pieces):
-            source = jnp.concatenate(
-                [
-                    values[h // per * pieces + tile][h % per * BLOCK + cell : h % per * BLOCK + cell + 1]
-                    for h in range(HEADS)
-                ]
-                + [jnp.zeros((8 - HEADS, LANES), f32)],
-                0,
-            )
+            if tile < pieces - 1:
+                starts = [(tile * HEADS + h) * BLOCK + cell for h in range(HEADS)]
+                source = jnp.concatenate([values[r : r + 1] for r in starts] + [fill], 0)
+                spots = at_spot
+            else:
+                row = tile * HEADS * BLOCK + cell
+                source = jnp.broadcast_to(values[row : row + 1], (SUBLANES, LANES))
+                spots = at_tail
             for c in range(len(found)):
-                taken = jnp.take_along_axis(source, at_spot[c], axis=1, mode="promise_in_bounds")
+                taken = jnp.take_along_axis(source, spots[c], axis=1, mode="promise_in_bounds")
                 found[c] = jnp.where(at_piece[c] == cell * pieces + tile, taken, found[c])
     for c in range(len(found)):
         out[:, c * LANES : (c + 1) * LANES] = found[c].astype(bf16)
@@ -228,7 +227,7 @@
 
 def window_body(
     here, from_lon, from_lat, from_both, norm_gain, norm_shift, w_qkv, w_out, bias,
-    out_here, out_lon, out_lat, keep, send, gathered, proj_grad, sums, tables,
+    out_here, out_lon, out_lat, out_both, keep, send, gathered, proj_grad, sums, tables,
 ):
     width = w_out.shape[0]
     level_win = bias.shape[0] // HEADS
@@ -309,8 +308,14 @@
                 piece = grad_logits[a * BLOCK : (a + 1) * BLOCK]
                 piece = jnp.concatenate((piece, jnp.zeros((BLOCK, SPREAD - WIN), f32)), 1)
                 total += pltpu.roll(piece, shift, 1) if shift else piece
-            for tile in range(SPREAD // LANES):
-                tables[t, h, tile] = total[:, tile * LANES : (tile + 1) * LANES]
+            for tile in range(2):
+                row = (tile * HEADS + h) * BLOCK
+                tables[t, row : row + BLOCK, :] = total[:, tile * LANES : (tile + 1) * LANES]
+            last = total[:, 2 * LANES :]
+            tails = tails + pltpu.roll(last, h * TAIL, 1) if h else last
+        row = 2 * HEADS * BLOCK
+        tables[t, row : row + BLOCK, :] = tails
+        tables[t, row + BLOCK :, :] = jnp.zeros((TABLE_ROWS - row - BLOCK, LANES), f32)
         mixed_parts.append(mixed.astype(bf16))
         proj_grad[rows, :width] = (grad_query * scaling).astype(bf16)
         proj_grad[rows, width : 2 * width] = (grad_key * scaling).astype(bf16)
@@ -340,15 +345,11 @@
     rest = width - LANES
     tiles = [b[:, :LANES] for b in back]
     tiles.append(jnp.concatenate([b[:, LANES:] for b in back], 1))
-    size = gathered.shape[2]
-    groups = lat_half * lon_half * levels // size
+    groups = lat_half * lon_half * levels // SUBLANES
     for at, tile in enumerate(tiles):
-        for q, (out, first) in enumerate(
-            ((out_here, 0), (out_lon, 0), (out_lat, 0), (out_lat, 3 * groups))
-        ):
-            for i in range(groups):
-                row = (q * groups + i) * size
-                out[first + at * groups + i] = tile[row : row + size].astype(bf16)
+        tile = tile.astype(bf16).reshape(4, groups, SUBLANES, LANES)
+        for q, out in enumerate((out_here, out_lon, out_lat, out_both)):
+            out[at * groups : (at + 1) * groups] = tile[q]
     sums[:, : 3 * width] = lax.dot_general(
         normed, grad_proj, (((0,), (0,)), ((), ())), preferred_element_type=f32
     )
@@ -357,30 +358,31 @@
     )
     chunks, blocks, _, _ = gathered.shape
     lat_count = chunks // 2
-    edge = jnp.zeros((size - 4, LANES), f32)
+    size = width // chunks
     fill = jnp.zeros((1, 2 * LANES - width), f32)
     ends = [gain_part[:, :LANES], jnp.concatenate((gain_part[:, LANES:], fill), 1)]
     ends += [shift_part[:, :LANES], jnp.concatenate((shift_part[:, LANES:], fill), 1)]
-    ends = jnp.concatenate(ends + [edge], 0).astype(bf16)
+    ends = jnp.concatenate(ends + [jnp.zeros((SUBLANES - 4, LANES), f32)], 0).astype(bf16)
     for j in range(chunks):
-        for b in range(blocks - 1):
-            gathered[j, b] = sums[
-                j * size : (j + 1) * size, b * LANES : (b + 1) * LANES
-            ].astype(bf16)
+        piece = jnp.concatenate(
+            [
+                sums[j * size : (j + 1) * size, b * LANES : (b + 1) * LANES]
+                for b in range(4 * width // LANES)
+            ],
+            0,
+        )
+        gathered[j, : blocks - 1] = piece.reshape(blocks - 1, SUBLANES, LANES).astype(bf16)
         gathered[j, blocks - 1] = ends
     core = lax.axis_index("lon") % 2
     lat = lax.axis_index("lat")
-    per = size // BLOCK
     for half, out in enumerate((keep, send)):
         side = core ^ half
         for at in range(lat_count):
             out[at * blocks : (at + 1) * blocks] = gathered[
-                side * lat_count + lax.rem(lat + at, lat_count)
+                side * lat_count + (lat ^ at)
             ]
-        for h in range(0, HEADS, per):
-            for tile in range(SPREAD // LANES):
-                block = jnp.concatenate([tables[side, h + i, tile] for i in range(per)], 0)
-                out[lat_count * blocks + h // per * (SPREAD // LANES) + tile] = block.astype(bf16)
+        table = tables[side].reshape(TABLE_ROWS // SUBLANES, SUBLANES, LANES)
+        out[lat_count * blocks :] = table.astype(bf16)
 
 
 def tree(values):
@@ -389,26 +391,19 @@
     return values[0]
 
 
-def halves_body(keep, came, quads, *outs):
-    *pieces, tail = outs
-    blocks = pieces[0].shape[0]
+def halves_body(keep, came, *outs):
     at = 0
     for out in outs:
-        count = tail.shape[0] if out is tail else blocks
-        part = slice(at, at + count)
-        out[:count] = (keep[part].astype(f32) + came[part].astype(f32)).astype(bf16)
-        at += count
-    pieces[1][blocks:] = quads[...]
+        part = slice(at, at + out.shape[0])
+        out[...] = (keep[part].astype(f32) + came[part].astype(f32)).astype(bf16)
+        at += out.shape[0]
 
 
 def lats_body(*refs):
-    *pieces, tail, quad, out, onward = refs
+    *pieces, tail, out = refs
     blocks = pieces[0].shape[0]
-    out[:blocks] = tree([p[:blocks].astype(f32) for p in pieces]).astype(bf16)
+    out[:blocks] = tree([p[...].astype(f32) for p in pieces]).astype(bf16)
     out[blocks:] = tail[...]
-    count = quad.shape[0]
-    onward[:count] = quad[...]
-    onward[count:] = pieces[1][blocks + count :]
 
 
 def lons_body(count, *refs):
@@ -426,16 +421,20 @@
     ]
     core = lax.axis_index("lon") % 2
     lat = lax.axis_index("lat")
-    _, blocks, size, _ = chunks.shape
+    count, blocks, _, _ = chunks.shape
     for half, group in enumerate((near, far)):
         for at, ref in enumerate(group):
-            chunks[(core ^ half) * lat_count + lax.rem(lat + lat_count - at, lat_count)] = ref[...].astype(f32) * factor
+            chunks[(core ^ half) * lat_count + (lat ^ at)] = ref[...].astype(f32) * factor
     halves[core] = table_near[...].astype(f32) * factor
     halves[core ^ 1] = table_far[...].astype(f32) * factor
     width = grad_wout.shape[0]
-    for j in range(chunks.shape[0]):
+    size = width // count
+    for j in range(count):
         rows = slice(j * size, (j + 1) * size)
-        whole = jnp.concatenate([chunks[j, b] for b in range(blocks - 1)], 1)
+        tall = chunks[j, : blocks - 1].reshape((blocks - 1) * SUBLANES, LANES)
+        whole = jnp.concatenate(
+            [tall[b * size : (b + 1) * size] for b in range(tall.shape[0] // size)], 1
+        )
         grad_wqkv[rows, :] = whole[:, : 3 * width]
         grad_wout[rows, :] = whole[:, 3 * width :]
     rest = width - LANES
@@ -497,50 +496,49 @@
         moved=16 * 10**6,
     )(table, labels_of)
 
-    size = width // (2 * lat_count)
-    blocks = 4 * width // LANES + 1
-    table_blocks = HEADS * BLOCK * SPREAD // (size * LANES)
-    quad_blocks = 2 * WH // 2 * WW // 2 * levels * width // (size * LANES)
+    blocks = 4 * width * width // (2 * lat_count) // (SUBLANES * LANES) + 1
+    table_blocks = TABLE_ROWS // SUBLANES
+    quad_blocks = 2 * WH // 2 * WW // 2 * levels * width // (SUBLANES * LANES)
 
     def stack(count):
-        return struct((count, size, LANES), bf16)
+        return struct((count, SUBLANES, LANES), bf16)
 
     half = stack(lat_count * blocks + table_blocks)
-    out_here, out_lon, out_lat, keep, send = call(
+    out_here, *backs, keep, send = call(
         window_body,
-        (stack(quad_blocks), stack(quad_blocks), stack(2 * quad_blocks), half, half),
+        (stack(quad_blocks),) * 4 + (half, half),
         [
-            pltpu.VMEM((2 * lat_count, blocks, size, LANES), bf16),
+            pltpu.VMEM((2 * lat_count, blocks, SUBLANES, LANES), bf16),
             pltpu.VMEM((level_win * WIN, 3 * width), bf16),
             pltpu.VMEM((width, 4 * width), f32),
-            pltpu.VMEM((level_win, heads, SPREAD // LANES, BLOCK, LANES), f32),
+            pltpu.VMEM((level_win, TABLE_ROWS, LANES), f32),
         ],
         moved=25 * 10**6,
     )(here, *came, gain, shift, w_qkv, w_out, bias)
 
-    shapes = [stack(blocks)] * lat_count + [stack(table_blocks)]
-    shapes[1] = stack(blocks + 2 * quad_blocks)
-    *pieces, tail = call(halves_body, tuple(shapes))(keep, swap(send, "lon", 1), out_lat)
-    pieces = [shifted(p, at, 0) if at else p for at, p in enumerate(pieces)]
-    part, onward = call(lats_body, (stack(blocks + table_blocks), stack(2 * quad_blocks)))(
-        *pieces, tail, out_lon
-    )
-    parts = [part] + [swap(part, "lon", 2 * at) for at in range(1, lon_count // 2)]
-    lon_pair = shifted(onward, 0, 1)
-    part, chunk, lane = lax.optimization_barrier((part, chunk, lane))
+    send, chunk, lane = lax.optimization_barrier((send, chunk, lane))
+    came = swap(send, "lon", 1)
     places = struct((32, LANES), jnp.int32)
     piece, spot = call(inverse_body, (places, places), moved=2 * 10**6)(chunk, lane)
+    came, piece, spot = lax.optimization_barrier((came, piece, spot))
+    *pieces, tail = call(halves_body, (stack(blocks),) * lat_count + (stack(table_blocks),))(keep, came)
+    pieces = [swap(p, "lat", at) if at else p for at, p in enumerate(pieces)]
+    part = call(lats_body, stack(blocks + table_blocks))(*pieces, tail)
+    parts = [part] + [swap(part, "lon", 2 * at) for at in range(1, lon_count // 2)]
+    returned = [shifted(b, lat, lon) for b, (lat, lon) in zip(backs, steps)]
     weights, tail = call(functools.partial(lons_body, len(parts)), (stack(blocks), stack(table_blocks)))(
         *parts
     )
-    near = [weights] + [shifted(weights, at, 0) for at in range(1, lat_count)]
-    table_near = call(place_body, struct((8, whole_lanes), bf16), moved=5 * 10**6)(tail, piece, spot)
+    near = [weights] + [swap(weights, "lat", at) for at in range(1, lat_count)]
+    table_near = call(place_body, struct((SUBLANES, whole_lanes), bf16), moved=5 * 10**6)(
+        tail, piece, spot
+    )
     table_far = swap(table_near, "lon", 1)
     far = [swap(n, "lon", 1) for n in near]
 
     cells = struct((lat_rows, lon_cols, levels, width), bf16)
     outputs, grad_features = call(unpack_body, (cells, cells), moved=2 * 10**6)(
-        out_here, pieces[1], lon_pair
+        out_here, *returned
     )
     factor = (levels * lat_rows * lat_count * lon_cols * lon_count) ** (-0.5)
     row = struct((1, width), f32)
@@ -554,7 +552,7 @@
             struct((level_win, heads, 1, labels), f32),
         ),
         [
-            pltpu.VMEM((2 * lat_count, blocks, size, LANES), f32),
+            pltpu.VMEM((2 * lat_count, blocks, SUBLANES, LANES), f32),
             pltpu.VMEM((2,) + table_near.shape, f32),
         ],
     )(*near, *far, table_near, table_far)

time: 51.6 us -> 47.8 us (0.926)
  waiting for transfers between devices: 12.4 us -> 7.75 us
    ppermute x9 -> x15, starting transfers between devices: 5.88 us -> 13 us  [swap(): lax.ppermute(value, axis, [(source, source ^ distance) for source in rang...]
    ppermute x10 -> x6, starting transfers between devices: 14.6 us -> 8.04 us  [shifted(): return lax.ppermute(value, ('lat', 'lon'), pairs)]
    ppermute x10 -> x6, waiting for transfers between devices: 4.67 us -> 0.79 us  [shifted(): return lax.ppermute(value, ('lat', 'lon'), pairs)]
    ppermute x9 -> x15, waiting for transfers between devices: 7.68 us -> 6.96 us  [swap(): lax.ppermute(value, axis, [(source, source ^ distance) for source in rang...]
  transfers between devices with their start and end apart: 19 -> 21, of which waited for: 6 -> 8; matrix products, arithmetic and copies ran while one was open for 0% -> 0% of each run, Pallas kernels for 16% -> 18%
where the time goes in v3:
time: 47.8 us; the launch traced here: 47.7 us
  starting transfers between devices  21 us (44%)
  Pallas kernels  18.1 us (38%)
  waiting for transfers between devices  7.75 us (16%)
  between operations  0.75 us (2%)
    ppermute x15, starting transfers between devices, swap(): lax.ppermute(value, axis, [(source, source ^ distance) for source in rang...  13 us
    ppermute x6, starting transfers between devices, shifted(): return lax.ppermute(value, ('lat', 'lon'), pairs)  8.04 us
    pallas_call x1, Pallas kernels, on_device(): call(window_body, (stack(quad_blocks),) * 4 + (half, half), [pltpu.VMEM((...  7.26 us
    ppermute x15, waiting for transfers between devices, swap(): lax.ppermute(value, axis, [(source, source ^ distance) for source in rang...  6.96 us
    pallas_call x1, Pallas kernels, on_device(): call(bias_body, (struct((level_win * heads, WIN, WIN), f32), spread, spre...  5.44 us
    pallas_call x1, Pallas kernels, on_device(): call(place_body, struct((SUBLANES, whole_lanes), bf16), moved=5 * 10 ** 6)  1.46 us
    pallas_call x1, Pallas kernels, on_device(): call(functools.partial(pack_body, len(plain)), (quad,) * 4 + tuple((struc...  1.42 us
    pallas_call x1, Pallas kernels, on_device(): call(functools.partial(finish_body, lat_count, factor), (row, row, struct...  1.02 us
  transfers between devices with their start and end apart: 21, of which 8 were waited for; matrix products, arithmetic and copies ran while one was open for 0% of the time, Pallas kernels for 18%

profile of v3, /device:TPU:0, one launch (start us, length us, event | category | flops | bytes accessed | tf_op | source)
XLA Modules:
  0.0 47.7 jit_solution(16187598279069516467)
XLA Ops:
  0.6 1.4 %shard_map.135 = (bf16[2,3,6,4,192]{4,3,2,1,0:T(4,128)(2,1)S(1)}, bf16[2,3,6,4,192]{4,3,2,1,0:T(4,128)(2,1)S(1)}, bf16[2,3,6,4,192]{4,3,2,1,0:T(4,128)(2,1)S(1)}...) custom-call(bf16[6,12,4,192]{3,2,1,0:T(4,128)(2,1)} %bitcast.11, ...), custom_call_target="tpu_custom_call" | custom-call | tf_op jit(solution)/shard_map/pallas_call | solution.py:476
  2.1 4.5 %collective-permute-start = (bf16[2,3,6,4,192]{4,3,2,1,0:T(4,128)(2,1)S(1)}, bf16[2,3,6,4,192]{4,3,2,1,0:T(4,128)(2,1)S(1)}, u32[]{:S(2)}, u32[]{:S(2)}) collective-permute-start(bf16[2,3,6,4,192]{4,3,2,1,0:T(4,128)(2,1)S(1)} %get-tuple-element.49), channel_id=1, source_target_pairs={{0,7},{1,0},{2,1},{3,2},{4,3},{5,4},{6,5},{7,6},{8,15},{9,8},{10,9... | collective-permute-start | bytes 165896 | tf_op jit(solution)/shard_map/ppermute | solution.py:462
  6.6 2.4 %collective-permute-start.1 = (bf16[2,3,6,4,192]{4,3,2,1,0:T(4,128)(2,1)S(1)}, bf16[2,3,6,4,192]{4,3,2,1,0:T(4,128)(2,1)S(1)}, u32[]{:S(2)}, u32[]{:S(2)}) collective-permute-start(bf16[2,3,6,4,192]{4,3,2,1,0:T(4,128)(2,1)S(1)} %get-tuple-element.50), channel_id=1, source_target_pairs={{0,24},{1,25},{2,26},{3,27},{4,28},{5,29},{6,30},{7,31},{8,0},{9,1... | collective-permute-start | bytes 165896 | tf_op jit(solution)/shard_map/ppermute | solution.py:462
  9.0 0.4 collective-permute-start.2
  9.4 5.4 %shard_map.136 = (f32[12,144,144]{2,1,0:T(8,128)S(1)}, s32[16,384]{1,0:T(8,128)S(1)}, s32[16,384]{1,0:T(8,128)S(1)}) custom-call(f32[2,6,1,3312]{3,2,1,0:T(1,128)S(1)} %get-tuple-element.56.bias_table, s32[144,144]{1,0:T(8,128)S(1)} %get-tuple-element.57.index_table), custom_call_target="tpu_custom_call" | custom-call | bytes 16000000 | tf_op jit(solution)/shard_map/pallas_call | solution.py:492
  14.9 0.0 collective-permute-done.from_lon
  14.9 0.0 collective-permute-done.1.from_lat
  14.9 0.0 collective-permute-done.2.from_both
  14.9 7.3 %shard_map.137 = (bf16[27,8,128]{2,1,0:T(8,128)(2,1)S(1)}, bf16[27,8,128]{2,1,0:T(8,128)(2,1)S(1)}, bf16[27,8,128]{2,1,0:T(8,128)(2,1)S(1)}, bf16[27,8,128]{2,1,...) custom-call(bf16[2,3,6,4,192]{4,3,2,1,0:T(4,128)(2,1)S(1)} %get-tuple-element.48.here, ...), custom_call_target="tpu_custom_call" | custom-call | bytes 25000000 | tf_op jit(solution)/shard_map/pallas_call | solution.py:507
  22.2 0.3 collective-permute-start.6
  22.5 0.6 %shard_map.139 = (s32[32,128]{1,0:T(8,128)S(1)}, s32[32,128]{1,0:T(8,128)S(1)}) custom-call(s32[16,384]{1,0:T(8,128)S(1)} %get-tuple-element.70.chunk, s32[16,384]{1,0:T(8,128)S(1)} %get-tuple-element.71.lane), custom_call_target="tpu_custom_call" | custom-call | bytes 2000000 | tf_op jit(solution)/shard_map/pallas_call | solution.py:522
  23.2 0.5 %collective-permute-done.6.came = bf16[96,8,128]{2,1,0:T(8,128)(2,1)S(1)} collective-permute-done((bf16[96,8,128]{2,1,0:T(8,128)(2,1)S(1)}, bf16[96,8,128]{2,1,0:T(8,128)(2,1)S(1)}, u32[]{:S(2)}, u32[]{:S(2)}) %collective-permute-start.6) | collective-permute-done | bytes 196640 | tf_op jit(solution)/shard_map/ppermute | solution.py:452
  23.7 1.6 %collective-permute-start.7 = (bf16[19,8,128]{2,1,0:T(8,128)(2,1)S(1)}, bf16[19,8,128]{2,1,0:T(8,128)(2,1)S(1)}, u32[]{:S(2)}, u32[]{:S(2)}) collective-permute-start(bf16[19,8,128]{2,1,0:T(8,128)(2,1)S(1)} %get-tuple-element.76), channel_id=1, source_target_pairs={{0,8},{8,0},{16,24},{24,16},{1,9},{9,1},{17,25},{25,17},{2,10},{10... | collective-permute-start | bytes 116744 | tf_op jit(solution)/shard_map/ppermute | solution.py:452
  25.3 0.5 %collective-permute-start.8 = (bf16[19,8,128]{2,1,0:T(8,128)(2,1)S(1)}, bf16[19,8,128]{2,1,0:T(8,128)(2,1)S(1)}, u32[]{:S(2)}, u32[]{:S(2)}) collective-permute-start(bf16[19,8,128]{2,1,0:T(8,128)(2,1)S(1)} %get-tuple-element.77), channel_id=1, source_target_pairs={{0,16},{8,24},{16,0},{24,8},{1,17},{9,25},{17,1},{25,9},{2,18},{10... | collective-permute-start | bytes 116744 | tf_op jit(solution)/shard_map/ppermute | solution.py:452
  25.8 1.5 %collective-permute-start.9 = (bf16[19,8,128]{2,1,0:T(8,128)(2,1)S(1)}, bf16[19,8,128]{2,1,0:T(8,128)(2,1)S(1)}, u32[]{:S(2)}, u32[]{:S(2)}) collective-permute-start(bf16[19,8,128]{2,1,0:T(8,128)(2,1)S(1)} %get-tuple-element.78), channel_id=1, source_target_pairs={{0,24},{8,16},{16,8},{24,0},{1,25},{9,17},{17,9},{25,1},{2,26},{10... | collective-permute-start | bytes 116744 | tf_op jit(solution)/shard_map/ppermute | solution.py:452
  27.3 0.5 %collective-permute-done.7.refs_1_ = bf16[19,8,128]{2,1,0:T(8,128)(2,1)S(1)} collective-permute-done((bf16[19,8,128]{2,1,0:T(8,128)(2,1)S(1)}, bf16[19,8,128]{2,1,0:T(8,128)(2,1)S(1)}, u32[]{:S(2)}, u32[]{:S(2)}) %collective-permute-start.7) | collective-permute-done | bytes 38944 | tf_op jit(solution)/shard_map/ppermute | solution.py:452
  27.8 1.9 %collective-permute-done.8.refs_2_ = bf16[19,8,128]{2,1,0:T(8,128)(2,1)S(1)} collective-permute-done((bf16[19,8,128]{2,1,0:T(8,128)(2,1)S(1)}, bf16[19,8,128]{2,1,0:T(8,128)(2,1)S(1)}, u32[]{:S(2)}, u32[]{:S(2)}) %collective-permute-start.8) | collective-permute-done | bytes 38944 | tf_op jit(solution)/shard_map/ppermute | solution.py:452
  29.7 1.0 %collective-permute-done.9.refs_3_ = bf16[19,8,128]{2,1,0:T(8,128)(2,1)S(1)} collective-permute-done((bf16[19,8,128]{2,1,0:T(8,128)(2,1)S(1)}, bf16[19,8,128]{2,1,0:T(8,128)(2,1)S(1)}, u32[]{:S(2)}, u32[]{:S(2)}) %collective-permute-start.9) | collective-permute-done | bytes 38944 | tf_op jit(solution)/shard_map/ppermute | solution.py:452
  30.7 1.1 %collective-permute-start.12 = (bf16[39,8,128]{2,1,0:T(8,128)(2,1)S(1)}, bf16[39,8,128]{2,1,0:T(8,128)(2,1)S(1)}, u32[]{:S(2)}, u32[]{:S(2)}) collective-permute-start(bf16[39,8,128]{2,1,0:T(8,128)(2,1)S(1)} %shard_map.141.refs_0_), channel_id=1, source_target_pairs={{0,6},{1,7},{2,4},{3,5},{4,2},{5,3},{6,0},{7,1},{8,14},{9,15},{10,... | collective-permute-start | bytes 239624 | tf_op jit(solution)/shard_map/ppermute | solution.py:452
  31.8 0.0 collective-permute-start.11
  31.8 3.3 %collective-permute-start.10 = (bf16[39,8,128]{2,1,0:T(8,128)(2,1)S(1)}, bf16[39,8,128]{2,1,0:T(8,128)(2,1)S(1)}, u32[]{:S(2)}, u32[]{:S(2)}) collective-permute-start(bf16[39,8,128]{2,1,0:T(8,128)(2,1)S(1)} %shard_map.141.refs_0_), channel_id=1, source_target_pairs={{0,2},{1,3},{2,0},{3,1},{4,6},{5,7},{6,4},{7,5},{8,10},{9,11},{10,... | collective-permute-start | bytes 239624 | tf_op jit(solution)/shard_map/ppermute | solution.py:452
  35.1 0.0 collective-permute-start.3
  35.1 0.5 %collective-permute-start.4 = (bf16[27,8,128]{2,1,0:T(8,128)(2,1)S(1)}, bf16[27,8,128]{2,1,0:T(8,128)(2,1)S(1)}, u32[]{:S(2)}, u32[]{:S(2)}) collective-permute-start(bf16[27,8,128]{2,1,0:T(8,128)(2,1)S(1)} %get-tuple-element.61), channel_id=1, source_target_pairs={{0,8},{1,9},{2,10},{3,11},{4,12},{5,13},{6,14},{7,15},{8,16},{9,17... | collective-permute-start | bytes 165896 | tf_op jit(solution)/shard_map/ppermute | solution.py:462
  35.7 1.8 %collective-permute-done.12.refs_3_ = bf16[39,8,128]{2,1,0:T(8,128)(2,1)S(1)} collective-permute-done((bf16[39,8,128]{2,1,0:T(8,128)(2,1)S(1)}, bf16[39,8,128]{2,1,0:T(8,128)(2,1)S(1)}, u32[]{:S(2)}, u32[]{:S(2)}) %collective-permute-start.12) | collective-permute-done | bytes 79904 | tf_op jit(solution)/shard_map/ppermute | solution.py:452
  37.5 0.1 collective-permute-start.5
  37.6 1.2 %collective-permute-done.11.refs_2_ = bf16[39,8,128]{2,1,0:T(8,128)(2,1)S(1)} collective-permute-done((bf16[39,8,128]{2,1,0:T(8,128)(2,1)S(1)}, bf16[39,8,128]{2,1,0:T(8,128)(2,1)S(1)}, u32[]{:S(2)}, u32[]{:S(2)}) %collective-permute-start.11) | collective-permute-done | bytes 79904 | tf_op jit(solution)/shard_map/ppermute | solution.py:452
  38.8 0.0 collective-permute-done.10.refs_1_
  38.9 1.6 %collective-permute-start.15 = (bf16[19,8,128]{2,1,0:T(8,128)(2,1)S(1)}, bf16[19,8,128]{2,1,0:T(8,128)(2,1)S(1)}, u32[]{:S(2)}, u32[]{:S(2)}) collective-permute-start(bf16[19,8,128]{2,1,0:T(8,128)(2,1)S(1)} %get-tuple-element.80.refs_0_), channel_id=1, source_target_pairs={{0,24},{8,16},{16,8},{24,0},{1,25},{9,17},{17,9},{25,1},{2,26},{10... | collective-permute-start | bytes 116744 | tf_op jit(solution)/shard_map/ppermute | solution.py:452
  40.4 0.6 %collective-permute-start.14 = (bf16[19,8,128]{2,1,0:T(8,128)(2,1)S(1)}, bf16[19,8,128]{2,1,0:T(8,128)(2,1)S(1)}, u32[]{:S(2)}, u32[]{:S(2)}) collective-permute-start(bf16[19,8,128]{2,1,0:T(8,128)(2,1)S(1)} %get-tuple-element.80.refs_0_), channel_id=1, source_target_pairs={{0,16},{8,24},{16,0},{24,8},{1,17},{9,25},{17,1},{25,9},{2,18},{10... | collective-permute-start | bytes 116744 | tf_op jit(solution)/shard_map/ppermute | solution.py:452
  41.0 0.0 collective-permute-done.3.from_lon
  41.0 1.4 %collective-permute-start.13 = (bf16[19,8,128]{2,1,0:T(8,128)(2,1)S(1)}, bf16[19,8,128]{2,1,0:T(8,128)(2,1)S(1)}, u32[]{:S(2)}, u32[]{:S(2)}) collective-permute-start(bf16[19,8,128]{2,1,0:T(8,128)(2,1)S(1)} %get-tuple-element.80.refs_0_), channel_id=1, source_target_pairs={{0,8},{8,0},{16,24},{24,16},{1,9},{9,1},{17,25},{25,17},{2,10},{10... | collective-permute-start | bytes 116744 | tf_op jit(solution)/shard_map/ppermute | solution.py:452
  42.4 1.5 %shard_map.143.refs_8_ = bf16[8,3328]{1,0:T(8,128)(2,1)S(1)} custom-call(bf16[20,8,128]{2,1,0:T(8,128)(2,1)S(1)} %get-tuple-element.81.blocks, s32[32,128]{1,0:T(8,128)S(1)} %get-tuple-element.82.piece, s32[32,128]{1,0:T(8,128)S(1)} %get-tuple-element.83.spot), custom_call_target="tpu_custom_call" | custom-call | bytes 5000000 | tf_op jit(solution)/shard_map/pallas_call | solution.py:533
  43.9 0.0 collective-permute-done.4.from_lat
  43.9 0.1 collective-permute-start.20
  44.0 0.8 %collective-permute-done.5.from_both = bf16[27,8,128]{2,1,0:T(8,128)(2,1)S(1)} collective-permute-done((bf16[27,8,128]{2,1,0:T(8,128)(2,1)S(1)}, bf16[27,8,128]{2,1,0:T(8,128)(2,1)S(1)}, u32[]{:S(2)}, u32[]{:S(2)}) %collective-permute-start.5) | collective-permute-done | bytes 55328 | tf_op jit(solution)/shard_map/ppermute | solution.py:462
  44.8 0.0 collective-permute-start.16
  44.8 0.0 collective-permute-done.15.refs_3_
  44.8 0.5 %collective-permute-start.19 = (bf16[19,8,128]{2,1,0:T(8,128)(2,1)S(1)}, bf16[19,8,128]{2,1,0:T(8,128)(2,1)S(1)}, u32[]{:S(2)}, u32[]{:S(2)}) collective-permute-start(bf16[19,8,128]{2,1,0:T(8,128)(2,1)S(1)} %collective-permute-done.15.refs_3_), channel_id=1, source_target_pairs={{0,1},{1,0},{2,3},{3,2},{4,5},{5,4},{6,7},{7,6},{8,9},{9,8},{10,11... | collective-permute-start | bytes 116744 | tf_op jit(solution)/shard_map/ppermute | solution.py:452
  45.3 0.0 collective-permute-done.14.refs_2_
  45.3 0.1 collective-permute-start.18
  45.3 0.0 collective-permute-done.13.refs_1_
  45.3 0.4 collective-permute-start.17
  45.8 0.8 %shard_map.138 = (bf16[6,12,4,192]{3,2,1,0:T(4,128)(2,1)}, bf16[6,12,4,192]{3,2,1,0:T(4,128)(2,1)}) custom-call(bf16[27,8,128]{2,1,0:T(8,128)(2,1)S(1)} %get-tuple-element.59.here, bf16[27,8,128]{2,1,0:T(8,128)(2,1)S(1)} %collective-permute-done.3.from_lon, bf16[27,8,128]{2,1,0:T(8,128)(2,1)S(1)} %collective-permute-done.4.from_lat, ...), custom_call_target="tpu_custom_call" | custom-call | bytes 2000000 | tf_op jit(solution)/shard_map/pallas_call | solution.py:540
  46.6 0.0 collective-permute-done.16.refs_4_
  46.6 0.0 collective-permute-done.20.refs_9_
  46.6 0.0 collective-permute-done.19.refs_7_
  46.6 0.0 collective-permute-done.18.refs_6_
  46.6 0.1 collective-permute-done.17.refs_5_
  46.7 1.0 %shard_map.144 = (f32[1,192]{1,0:T(1,128)}, f32[1,192]{1,0:T(1,128)}, f32[192,576]{1,0:T(8,128)}, f32[192,192]{1,0:T(8,128)}, f32[2,6,1,3312]{3,2,1,0:T(1,128)}) custom-call(bf16[19,8,128]{2,1,0:T(8,128)(2,1)S(1)} %get-tuple-element.80.refs_0_, bf16[19,8,128]{2,1,0:T(8,128)(2,1)S(1)} %collective-permute-done.13.refs_1_, ...), custom_call_target="tpu_custom_call" | custom-call | tf_op jit(solution)/shard_map/pallas_call | solution.py:545
  (3 shorter events, 0.1 us)
Async XLA Ops:
  2.1 12.8 %collective-permute-start = (bf16[2,3,6,4,192]{4,3,2,1,0:T(4,128)(2,1)S(1)}, bf16[2,3,6,4,192]{4,3,2,1,0:T(4,128)(2,1)S(1)}, u32[]{:S(2)}, u32[]{:S(2)}) collective-permute-start(bf16[2,3,6,4,192]{4,3,2,1,0:T(4,128)(2,1)S(1)} %get-tuple-element.49), channel_id=1, source_target_pairs={{0,7},{1,0},{2,1},{3,2},{4,3},{5,4},{6,5},{7,6},{8,15},{9,8},{10,9... | collective-permute-start | bytes 165896 | tf_op jit(solution)/shard_map/ppermute | solution.py:462
  6.6 8.3 %collective-permute-start.1 = (bf16[2,3,6,4,192]{4,3,2,1,0:T(4,128)(2,1)S(1)}, bf16[2,3,6,4,192]{4,3,2,1,0:T(4,128)(2,1)S(1)}, u32[]{:S(2)}, u32[]{:S(2)}) collective-permute-start(bf16[2,3,6,4,192]{4,3,2,1,0:T(4,128)(2,1)S(1)} %get-tuple-element.50), channel_id=1, source_target_pairs={{0,24},{1,25},{2,26},{3,27},{4,28},{5,29},{6,30},{7,31},{8,0},{9,1... | collective-permute-start | bytes 165896 | tf_op jit(solution)/shard_map/ppermute | solution.py:462
  9.0 5.8 %collective-permute-start.2 = (bf16[2,3,6,4,192]{4,3,2,1,0:T(4,128)(2,1)S(1)}, bf16[2,3,6,4,192]{4,3,2,1,0:T(4,128)(2,1)S(1)}, u32[]{:S(2)}, u32[]{:S(2)}) collective-permute-start(bf16[2,3,6,4,192]{4,3,2,1,0:T(4,128)(2,1)S(1)} %get-tuple-element.51), channel_id=1, source_target_pairs={{0,31},{1,24},{2,25},{3,26},{4,27},{5,28},{6,29},{7,30},{8,7},{9,0... | collective-permute-start | bytes 165896 | tf_op jit(solution)/shard_map/ppermute | solution.py:462
  22.2 1.5 %collective-permute-start.6 = (bf16[96,8,128]{2,1,0:T(8,128)(2,1)S(1)}, bf16[96,8,128]{2,1,0:T(8,128)(2,1)S(1)}, u32[]{:S(2)}, u32[]{:S(2)}) collective-permute-start(bf16[96,8,128]{2,1,0:T(8,128)(2,1)S(1)} %get-tuple-element.69), channel_id=1, source_target_pairs={{0,1},{1,0},{2,3},{3,2},{4,5},{5,4},{6,7},{7,6},{8,9},{9,8},{10,11... | collective-permute-start | bytes 589832 | tf_op jit(solution)/shard_map/ppermute | solution.py:452
  23.7 4.0 %collective-permute-start.7 = (bf16[19,8,128]{2,1,0:T(8,128)(2,1)S(1)}, bf16[19,8,128]{2,1,0:T(8,128)(2,1)S(1)}, u32[]{:S(2)}, u32[]{:S(2)}) collective-permute-start(bf16[19,8,128]{2,1,0:T(8,128)(2,1)S(1)} %get-tuple-element.76), channel_id=1, source_target_pairs={{0,8},{8,0},{16,24},{24,16},{1,9},{9,1},{17,25},{25,17},{2,10},{10... | collective-permute-start | bytes 116744 | tf_op jit(solution)/shard_map/ppermute | solution.py:452
  25.3 4.4 %collective-permute-start.8 = (bf16[19,8,128]{2,1,0:T(8,128)(2,1)S(1)}, bf16[19,8,128]{2,1,0:T(8,128)(2,1)S(1)}, u32[]{:S(2)}, u32[]{:S(2)}) collective-permute-start(bf16[19,8,128]{2,1,0:T(8,128)(2,1)S(1)} %get-tuple-element.77), channel_id=1, source_target_pairs={{0,16},{8,24},{16,0},{24,8},{1,17},{9,25},{17,1},{25,9},{2,18},{10... | collective-permute-start | bytes 116744 | tf_op jit(solution)/shard_map/ppermute | solution.py:452
  25.8 4.9 %collective-permute-start.9 = (bf16[19,8,128]{2,1,0:T(8,128)(2,1)S(1)}, bf16[19,8,128]{2,1,0:T(8,128)(2,1)S(1)}, u32[]{:S(2)}, u32[]{:S(2)}) collective-permute-start(bf16[19,8,128]{2,1,0:T(8,128)(2,1)S(1)} %get-tuple-element.78), channel_id=1, source_target_pairs={{0,24},{8,16},{16,8},{24,0},{1,25},{9,17},{17,9},{25,1},{2,26},{10... | collective-permute-start | bytes 116744 | tf_op jit(solution)/shard_map/ppermute | solution.py:452
  30.7 6.8 %collective-permute-start.12 = (bf16[39,8,128]{2,1,0:T(8,128)(2,1)S(1)}, bf16[39,8,128]{2,1,0:T(8,128)(2,1)S(1)}, u32[]{:S(2)}, u32[]{:S(2)}) collective-permute-start(bf16[39,8,128]{2,1,0:T(8,128)(2,1)S(1)} %shard_map.141.refs_0_), channel_id=1, source_target_pairs={{0,6},{1,7},{2,4},{3,5},{4,2},{5,3},{6,0},{7,1},{8,14},{9,15},{10,... | collective-permute-start | bytes 239624 | tf_op jit(solution)/shard_map/ppermute | solution.py:452
  31.8 7.0 %collective-permute-start.11 = (bf16[39,8,128]{2,1,0:T(8,128)(2,1)S(1)}, bf16[39,8,128]{2,1,0:T(8,128)(2,1)S(1)}, u32[]{:S(2)}, u32[]{:S(2)}) collective-permute-start(bf16[39,8,128]{2,1,0:T(8,128)(2,1)S(1)} %shard_map.141.refs_0_), channel_id=1, source_target_pairs={{0,4},{1,5},{2,6},{3,7},{4,0},{5,1},{6,2},{7,3},{8,12},{9,13},{10,... | collective-permute-start | bytes 239624 | tf_op jit(solution)/shard_map/ppermute | solution.py:452
  31.8 7.0 %collective-permute-start.10 = (bf16[39,8,128]{2,1,0:T(8,128)(2,1)S(1)}, bf16[39,8,128]{2,1,0:T(8,128)(2,1)S(1)}, u32[]{:S(2)}, u32[]{:S(2)}) collective-permute-start(bf16[39,8,128]{2,1,0:T(8,128)(2,1)S(1)} %shard_map.141.refs_0_), channel_id=1, source_target_pairs={{0,2},{1,3},{2,0},{3,1},{4,6},{5,7},{6,4},{7,5},{8,10},{9,11},{10,... | collective-permute-start | bytes 239624 | tf_op jit(solution)/shard_map/ppermute | solution.py:452
  35.1 5.9 %collective-permute-start.3 = (bf16[27,8,128]{2,1,0:T(8,128)(2,1)S(1)}, bf16[27,8,128]{2,1,0:T(8,128)(2,1)S(1)}, u32[]{:S(2)}, u32[]{:S(2)}) collective-permute-start(bf16[27,8,128]{2,1,0:T(8,128)(2,1)S(1)} %get-tuple-element.60), channel_id=1, source_target_pairs={{0,1},{1,2},{2,3},{3,4},{4,5},{5,6},{6,7},{7,0},{8,9},{9,10},{10,1... | collective-permute-start | bytes 165896 | tf_op jit(solution)/shard_map/ppermute | solution.py:462
  35.1 8.7 %collective-permute-start.4 = (bf16[27,8,128]{2,1,0:T(8,128)(2,1)S(1)}, bf16[27,8,128]{2,1,0:T(8,128)(2,1)S(1)}, u32[]{:S(2)}, u32[]{:S(2)}) collective-permute-start(bf16[27,8,128]{2,1,0:T(8,128)(2,1)S(1)} %get-tuple-element.61), channel_id=1, source_target_pairs={{0,8},{1,9},{2,10},{3,11},{4,12},{5,13},{6,14},{7,15},{8,16},{9,17... | collective-permute-start | bytes 165896 | tf_op jit(solution)/shard_map/ppermute | solution.py:462
  37.5 7.3 %collective-permute-start.5 = (bf16[27,8,128]{2,1,0:T(8,128)(2,1)S(1)}, bf16[27,8,128]{2,1,0:T(8,128)(2,1)S(1)}, u32[]{:S(2)}, u32[]{:S(2)}) collective-permute-start(bf16[27,8,128]{2,1,0:T(8,128)(2,1)S(1)} %get-tuple-element.62), channel_id=1, source_target_pairs={{0,9},{1,10},{2,11},{3,12},{4,13},{5,14},{6,15},{7,8},{8,17},{9,18... | collective-permute-start | bytes 165896 | tf_op jit(solution)/shard_map/ppermute | solution.py:462
  38.9 5.9 %collective-permute-start.15 = (bf16[19,8,128]{2,1,0:T(8,128)(2,1)S(1)}, bf16[19,8,128]{2,1,0:T(8,128)(2,1)S(1)}, u32[]{:S(2)}, u32[]{:S(2)}) collective-permute-start(bf16[19,8,128]{2,1,0:T(8,128)(2,1)S(1)} %get-tuple-element.80.refs_0_), channel_id=1, source_target_pairs={{0,24},{8,16},{16,8},{24,0},{1,25},{9,17},{17,9},{25,1},{2,26},{10... | collective-permute-start | bytes 116744 | tf_op jit(solution)/shard_map/ppermute | solution.py:452
  40.4 4.9 %collective-permute-start.14 = (bf16[19,8,128]{2,1,0:T(8,128)(2,1)S(1)}, bf16[19,8,128]{2,1,0:T(8,128)(2,1)S(1)}, u32[]{:S(2)}, u32[]{:S(2)}) collective-permute-start(bf16[19,8,128]{2,1,0:T(8,128)(2,1)S(1)} %get-tuple-element.80.refs_0_), channel_id=1, source_target_pairs={{0,16},{8,24},{16,0},{24,8},{1,17},{9,25},{17,1},{25,9},{2,18},{10... | collective-permute-start | bytes 116744 | tf_op jit(solution)/shard_map/ppermute | solution.py:452
  41.0 4.3 %collective-permute-start.13 = (bf16[19,8,128]{2,1,0:T(8,128)(2,1)S(1)}, bf16[19,8,128]{2,1,0:T(8,128)(2,1)S(1)}, u32[]{:S(2)}, u32[]{:S(2)}) collective-permute-start(bf16[19,8,128]{2,1,0:T(8,128)(2,1)S(1)} %get-tuple-element.80.refs_0_), channel_id=1, source_target_pairs={{0,8},{8,0},{16,24},{24,16},{1,9},{9,1},{17,25},{25,17},{2,10},{10... | collective-permute-start | bytes 116744 | tf_op jit(solution)/shard_map/ppermute | solution.py:452
  43.9 2.7 %collective-permute-start.20 = (bf16[8,3328]{1,0:T(8,128)(2,1)S(1)}, bf16[8,3328]{1,0:T(8,128)(2,1)S(1)}, u32[]{:S(2)}, u32[]{:S(2)}) collective-permute-start(bf16[8,3328]{1,0:T(8,128)(2,1)S(1)} %shard_map.143.refs_8_), channel_id=1, source_target_pairs={{0,1},{1,0},{2,3},{3,2},{4,5},{5,4},{6,7},{7,6},{8,9},{9,8},{10,11... | collective-permute-start | bytes 159752 | tf_op jit(solution)/shard_map/ppermute | solution.py:452
  44.8 1.8 %collective-permute-start.16 = (bf16[19,8,128]{2,1,0:T(8,128)(2,1)S(1)}, bf16[19,8,128]{2,1,0:T(8,128)(2,1)S(1)}, u32[]{:S(2)}, u32[]{:S(2)}) collective-permute-start(bf16[19,8,128]{2,1,0:T(8,128)(2,1)S(1)} %get-tuple-element.80.refs_0_), channel_id=1, source_target_pairs={{0,1},{1,0},{2,3},{3,2},{4,5},{5,4},{6,7},{7,6},{8,9},{9,8},{10,11... | collective-permute-start | bytes 116744 | tf_op jit(solution)/shard_map/ppermute | solution.py:452
  44.8 1.8 %collective-permute-start.19 = (bf16[19,8,128]{2,1,0:T(8,128)(2,1)S(1)}, bf16[19,8,128]{2,1,0:T(8,128)(2,1)S(1)}, u32[]{:S(2)}, u32[]{:S(2)}) collective-permute-start(bf16[19,8,128]{2,1,0:T(8,128)(2,1)S(1)} %collective-permute-done.15.refs_3_), channel_id=1, source_target_pairs={{0,1},{1,0},{2,3},{3,2},{4,5},{5,4},{6,7},{7,6},{8,9},{9,8},{10,11... | collective-permute-start | bytes 116744 | tf_op jit(solution)/shard_map/ppermute | solution.py:452
  45.3 1.3 %collective-permute-start.18 = (bf16[19,8,128]{2,1,0:T(8,128)(2,1)S(1)}, bf16[19,8,128]{2,1,0:T(8,128)(2,1)S(1)}, u32[]{:S(2)}, u32[]{:S(2)}) collective-permute-start(bf16[19,8,128]{2,1,0:T(8,128)(2,1)S(1)} %collective-permute-done.14.refs_2_), channel_id=1, source_target_pairs={{0,1},{1,0},{2,3},{3,2},{4,5},{5,4},{6,7},{7,6},{8,9},{9,8},{10,11... | collective-permute-start | bytes 116744 | tf_op jit(solution)/shard_map/ppermute | solution.py:452
  45.3 1.3 %collective-permute-start.17 = (bf16[19,8,128]{2,1,0:T(8,128)(2,1)S(1)}, bf16[19,8,128]{2,1,0:T(8,128)(2,1)S(1)}, u32[]{:S(2)}, u32[]{:S(2)}) collective-permute-start(bf16[19,8,128]{2,1,0:T(8,128)(2,1)S(1)} %collective-permute-done.13.refs_1_), channel_id=1, source_target_pairs={{0,1},{1,0},{2,3},{3,2},{4,5},{5,4},{6,7},{7,6},{8,9},{9,8},{10,11... | collective-permute-start | bytes 116744 | tf_op jit(solution)/shard_map/ppermute | solution.py:452

commit v4 on v3

--- a/solution.py
+++ b/solution.py
@@ -155,27 +155,87 @@
     row_apart = (cell >= WH // 2) != (other >= WH // 2)
     top = lax.axis_index("lat") == lax.axis_size("lat") - 1
     barred_rows = jnp.logical_and(row_apart, top)
-    for t in range(level_win):
-        barred = barred_rows
-        if t == level_win - 1:
-            barred = jnp.logical_or(barred, level_apart)
-        for h in range(heads):
-            row = t * heads + h
-            tiles = []
-            for tile in range(SPREAD // LANES):
-                at = slice(tile * LANES, (tile + 1) * LANES)
-                found = jnp.zeros((16, LANES), f32)
-                for c in range(chunks):
-                    source = jnp.broadcast_to(
-                        table[row : row + 1, c * LANES : (c + 1) * LANES], (16, LANES)
-                    )
-                    taken = jnp.take_along_axis(source, lane[:, at], axis=1, mode="promise_in_bounds")
-                    found = jnp.where(chunk[:, at] == c, taken, found)
-                tiles.append(found)
-            value = jnp.where(barred, -LARGE, jnp.concatenate(tiles, 1))
+    rest = BLOCK - SUBLANES
+    sub = columns((SUBLANES, LANES), 0)
+    early = sub < rest
+
+    def spread_row(row):
+        return jnp.broadcast_to(row, (SUBLANES, LANES))
+
+    def take(source, index):
+        return jnp.take_along_axis(source, index, axis=1, mode="promise_in_bounds")
+
+    tiles = SPREAD // LANES - 1
+    upper, lower = [], []
+    for tile in range(tiles):
+        at = slice(tile * LANES, (tile + 1) * LANES)
+        upper.append((chunk[:SUBLANES, at], lane[:SUBLANES, at]))
+        lower.append(
+            tuple(
+                jnp.concatenate((v[SUBLANES:BLOCK, at], v[SUBLANES:BLOCK, at]), 0)
+                for v in (chunk, lane)
+            )
+        )
+    per = BLOCK // 2
+    tails = []
+    for first in (0, per):
+        packed = []
+        for v in (chunk, lane):
+            total = v[first : first + 1, tiles * LANES :]
+            for i in range(1, per):
+                row = v[first + i : first + i + 1, tiles * LANES :]
+                total = total + pltpu.roll(row, i * TAIL, 1)
+            packed.append(spread_row(total))
+        tails.append(packed)
+    mixed_tail = [jnp.where(early, x, y) for x, y in zip(*tails)]
+    rows = level_win * heads
+    tail_found = [jnp.zeros((SUBLANES, LANES), f32) for _ in range(3)]
+    for c in range(chunks):
+        at = slice(c * LANES, (c + 1) * LANES)
+        first = table[:SUBLANES, at]
+        second = jnp.concatenate((table[SUBLANES:rows, at], table[SUBLANES:rows, at]), 0)
+        for k, (source, (which, spot)) in enumerate(
+            ((first, tails[0]), (first, tails[1]), (second, mixed_tail))
+        ):
+            tail_found[k] = jnp.where(which == c, take(source, spot), tail_found[k])
+    cell = columns((SUBLANES, LANES), 0)
+    entry = columns((SUBLANES, LANES), 1)
+    upper_spot = (jnp.where(cell >= per, cell - per, cell) * TAIL + entry) & (LANES - 1)
+    lower_cell = jnp.where(early, cell, cell - rest) + SUBLANES - per
+    lower_spot = (lower_cell * TAIL + entry) & (LANES - 1)
+
+    for row in range(0, rows, 2):
+        pair = (row, row + 1)
+        found = [[jnp.zeros((SUBLANES, LANES), f32) for _ in range(3)] for _ in range(tiles)]
+        for c in range(chunks):
+            sources = [
+                spread_row(table[r : r + 1, c * LANES : (c + 1) * LANES]) for r in pair
+            ]
+            sources.append(jnp.where(early, *sources))
+            for tile in range(tiles):
+                for k, (which, spot) in enumerate((upper[tile], upper[tile], lower[tile])):
+                    found[tile][k] = jnp.where(which == c, take(sources[k], spot), found[tile][k])
+        ends = []
+        for r in pair:
+            if r < SUBLANES:
+                ends.append([spread_row(tail_found[k][r : r + 1]) for k in range(2)])
+            else:
+                at = r - SUBLANES
+                ends.append([spread_row(tail_found[2][i : i + 1]) for i in (at, rest + at)])
+        last = [take(jnp.where(sub < per, *end), upper_spot) for end in ends]
+        last.append(take(jnp.where(early, ends[0][1], ends[1][1]), lower_spot))
+        found.append(last)
+        for k, r in enumerate(pair):
+            value = jnp.concatenate(
+                [jnp.concatenate((f[k], f[2][k * rest : (k + 1) * rest]), 0) for f in found], 1
+            )
+            barred = barred_rows
+            if r // heads == level_win - 1:
+                barred = jnp.logical_or(barred, level_apart)
+            value = jnp.where(barred[:BLOCK], -LARGE, value)
             for a in range(WW):
                 shift = (WW - 1 - a) * BLOCK
-                out[row, a * BLOCK : (a + 1) * BLOCK, :] = value[:BLOCK, shift : shift + WIN]
+                out[r, a * BLOCK : (a + 1) * BLOCK, :] = value[:, shift : shift + WIN]
 
 
 def inverse_body(chunk, lane, chunk_out, lane_out):
@@ -271,27 +331,27 @@
         q, k, v, g = query[rows], key[rows], value[rows], grad_heads[rows]
         q_heads = [jnp.where(head_of == h, q, jnp.zeros_like(q)) for h in range(HEADS)]
         g_heads = [jnp.where(head_of == h, g, jnp.zeros_like(g)) for h in range(HEADS)]
+        q_heads = jnp.concatenate(q_heads, 0)
+        g_heads = jnp.concatenate(g_heads, 0)
+        all_logits = lax.dot_general(
+            q_heads, k, (((1,), (1,)), ((), ())), preferred_element_type=f32
+        )
+        all_grads = lax.dot_general(
+            g_heads, v, (((1,), (1,)), ((), ())), preferred_element_type=f32
+        )
         mixed = jnp.zeros((WIN, width), f32)
         grad_query = jnp.zeros((WIN, width), f32)
-        grad_key = jnp.zeros((WIN, width), f32)
-        grad_value = jnp.zeros((WIN, width), f32)
+        all_weights, all_logit_grads = [], []
         for h in range(HEADS):
-            logits = lax.dot_general(
-                q_heads[h], k, (((1,), (1,)), ((), ())), preferred_element_type=f32
-            )
-            logits = logits * scaling + bias[t * HEADS + h]
+            span = slice(h * WIN, (h + 1) * WIN)
+            logits = all_logits[span] * scaling + bias[t * HEADS + h]
             raised = jnp.exp(logits - jnp.max(logits, -1, keepdims=True))
             weights = raised * (1.0 / jnp.sum(raised, -1, keepdims=True))
             weights_bf = weights.astype(bf16)
             mixed = jnp.where(
                 head_of == h, jnp.dot(weights_bf, v, preferred_element_type=f32), mixed
             )
-            grad_weights = lax.dot_general(
-                g_heads[h], v, (((1,), (1,)), ((), ())), preferred_element_type=f32
-            )
-            grad_value += lax.dot_general(
-                weights_bf, g_heads[h], (((0,), (0,)), ((), ())), preferred_element_type=f32
-            )
+            grad_weights = all_grads[span]
             grad_logits = weights * (
                 grad_weights - jnp.sum(weights * grad_weights, -1, keepdims=True)
             )
@@ -299,9 +359,8 @@
             grad_query = jnp.where(
                 head_of == h, jnp.dot(logit_bf, k, preferred_element_type=f32), grad_query
             )
-            grad_key += lax.dot_general(
-                logit_bf, q_heads[h], (((0,), (0,)), ((), ())), preferred_element_type=f32
-            )
+            all_weights.append(weights_bf)
+            all_logit_grads.append(logit_bf)
             total = jnp.zeros((BLOCK, SPREAD), f32)
             for a in range(WW):
                 shift = (WW - 1 - a) * BLOCK
@@ -316,6 +375,12 @@
         row = 2 * HEADS * BLOCK
         tables[t, row : row + BLOCK, :] = tails
         tables[t, row + BLOCK :, :] = jnp.zeros((TABLE_ROWS - row - BLOCK, LANES), f32)
+        grad_value, grad_key = (
+            lax.dot_general(
+                jnp.concatenate(left, 0), right, (((0,), (0,)), ((), ())), preferred_element_type=f32
+            )
+            for left, right in ((all_weights, g_heads), (all_logit_grads, q_heads))
+        )
         mixed_parts.append(mixed.astype(bf16))
         proj_grad[rows, :width] = (grad_query * scaling).astype(bf16)
         proj_grad[rows, width : 2 * width] = (grad_key * scaling).astype(bf16)

time: 47.8 us -> 44.6 us (0.933)
  Pallas kernels: 18.1 us -> 14.3 us
  waiting for transfers between devices: 7.75 us -> 8.75 us
    pallas_call x1, Pallas kernels: 7.26 us -> 4.99 us  [on_device(): call(window_body, (stack(quad_blocks),) * 4 + (half, half), [pltpu.VMEM((...]
    pallas_call x1, Pallas kernels: 5.44 us -> 3.91 us  [on_device(): call(bias_body, (struct((level_win * heads, WIN, WIN), f32), spread, spre...]
    ppermute x15, waiting for transfers between devices: 6.96 us -> 8.22 us  [swap(): lax.ppermute(value, axis, [(source, source ^ distance) for source in rang...]
  transfers between devices with their start and end apart: 21 -> 21, of which waited for: 8 -> 8; matrix products, arithmetic and copies ran while one was open for 0% -> 0% of each run, Pallas kernels for 18% -> 15%
where the time goes in v4:
time: 44.6 us; the launch traced here: 44.5 us
  starting transfers between devices  20.6 us (46%)
  Pallas kernels  14.3 us (32%)
  waiting for transfers between devices  8.75 us (20%)
  between operations  0.75 us (2%)
    ppermute x15, starting transfers between devices, swap(): lax.ppermute(value, axis, [(source, source ^ distance) for source in rang...  13 us
    ppermute x15, waiting for transfers between devices, swap(): lax.ppermute(value, axis, [(source, source ^ distance) for source in rang...  8.22 us
    ppermute x6, starting transfers between devices, shifted(): return lax.ppermute(value, ('lat', 'lon'), pairs)  7.65 us
    pallas_call x1, Pallas kernels, on_device(): call(window_body, (stack(quad_blocks),) * 4 + (half, half), [pltpu.VMEM((...  4.99 us
    pallas_call x1, Pallas kernels, on_device(): call(bias_body, (struct((level_win * heads, WIN, WIN), f32), spread, spre...  3.91 us
    pallas_call x1, Pallas kernels, on_device(): call(place_body, struct((SUBLANES, whole_lanes), bf16), moved=5 * 10 ** 6)  1.46 us
    pallas_call x1, Pallas kernels, on_device(): call(functools.partial(pack_body, len(plain)), (quad,) * 4 + tuple((struc...  1.42 us
    pallas_call x1, Pallas kernels, on_device(): call(functools.partial(finish_body, lat_count, factor), (row, row, struct...  1.02 us
  transfers between devices with their start and end apart: 21, of which 8 were waited for; matrix products, arithmetic and copies ran while one was open for 0% of the time, Pallas kernels for 15%

profile of v4, /device:TPU:0, one launch (start us, length us, event | category | flops | bytes accessed | tf_op | source)
XLA Modules:
  0.0 44.5 jit_solution(18264516691106601542)
XLA Ops:
  0.6 1.4 %shard_map.135 = (bf16[2,3,6,4,192]{4,3,2,1,0:T(4,128)(2,1)S(1)}, bf16[2,3,6,4,192]{4,3,2,1,0:T(4,128)(2,1)S(1)}, bf16[2,3,6,4,192]{4,3,2,1,0:T(4,128)(2,1)S(1)}...) custom-call(bf16[6,12,4,192]{3,2,1,0:T(4,128)(2,1)} %bitcast.11, ...), custom_call_target="tpu_custom_call" | custom-call | tf_op jit(solution)/shard_map/pallas_call | solution.py:541
  2.1 4.5 %collective-permute-start = (bf16[2,3,6,4,192]{4,3,2,1,0:T(4,128)(2,1)S(1)}, bf16[2,3,6,4,192]{4,3,2,1,0:T(4,128)(2,1)S(1)}, u32[]{:S(2)}, u32[]{:S(2)}) collective-permute-start(bf16[2,3,6,4,192]{4,3,2,1,0:T(4,128)(2,1)S(1)} %get-tuple-element.49), channel_id=1, source_target_pairs={{0,7},{1,0},{2,1},{3,2},{4,3},{5,4},{6,5},{7,6},{8,15},{9,8},{10,9... | collective-permute-start | bytes 165896 | tf_op jit(solution)/shard_map/ppermute | solution.py:527
  6.6 2.4 %collective-permute-start.1 = (bf16[2,3,6,4,192]{4,3,2,1,0:T(4,128)(2,1)S(1)}, bf16[2,3,6,4,192]{4,3,2,1,0:T(4,128)(2,1)S(1)}, u32[]{:S(2)}, u32[]{:S(2)}) collective-permute-start(bf16[2,3,6,4,192]{4,3,2,1,0:T(4,128)(2,1)S(1)} %get-tuple-element.50), channel_id=1, source_target_pairs={{0,24},{1,25},{2,26},{3,27},{4,28},{5,29},{6,30},{7,31},{8,0},{9,1... | collective-permute-start | bytes 165896 | tf_op jit(solution)/shard_map/ppermute | solution.py:527
  9.0 0.4 collective-permute-start.2
  9.4 3.9 %shard_map.136 = (f32[12,144,144]{2,1,0:T(8,128)S(1)}, s32[16,384]{1,0:T(8,128)S(1)}, s32[16,384]{1,0:T(8,128)S(1)}) custom-call(f32[2,6,1,3312]{3,2,1,0:T(1,128)S(1)} %get-tuple-element.56.bias_table, s32[144,144]{1,0:T(8,128)S(1)} %get-tuple-element.57.index_table), custom_call_target="tpu_custom_call" | custom-call | bytes 16000000 | tf_op jit(solution)/shard_map/pallas_call | solution.py:557
  13.3 0.0 collective-permute-done.from_lon
  13.3 0.0 collective-permute-done.1.from_lat
  13.3 0.0 collective-permute-done.2.from_both
  13.4 5.0 %shard_map.137 = (bf16[27,8,128]{2,1,0:T(8,128)(2,1)S(1)}, bf16[27,8,128]{2,1,0:T(8,128)(2,1)S(1)}, bf16[27,8,128]{2,1,0:T(8,128)(2,1)S(1)}, bf16[27,8,128]{2,1,...) custom-call(bf16[2,3,6,4,192]{4,3,2,1,0:T(4,128)(2,1)S(1)} %get-tuple-element.48.here, ...), custom_call_target="tpu_custom_call" | custom-call | bytes 25000000 | tf_op jit(solution)/shard_map/pallas_call | solution.py:572
  18.4 0.3 collective-permute-start.6
  18.7 0.6 %shard_map.139 = (s32[32,128]{1,0:T(8,128)S(1)}, s32[32,128]{1,0:T(8,128)S(1)}) custom-call(s32[16,384]{1,0:T(8,128)S(1)} %get-tuple-element.70.chunk, s32[16,384]{1,0:T(8,128)S(1)} %get-tuple-element.71.lane), custom_call_target="tpu_custom_call" | custom-call | bytes 2000000 | tf_op jit(solution)/shard_map/pallas_call | solution.py:587
  19.3 0.5 %collective-permute-done.6.came = bf16[96,8,128]{2,1,0:T(8,128)(2,1)S(1)} collective-permute-done((bf16[96,8,128]{2,1,0:T(8,128)(2,1)S(1)}, bf16[96,8,128]{2,1,0:T(8,128)(2,1)S(1)}, u32[]{:S(2)}, u32[]{:S(2)}) %collective-permute-start.6) | collective-permute-done | bytes 196640 | tf_op jit(solution)/shard_map/ppermute | solution.py:517
  19.9 1.5 %collective-permute-start.7 = (bf16[19,8,128]{2,1,0:T(8,128)(2,1)S(1)}, bf16[19,8,128]{2,1,0:T(8,128)(2,1)S(1)}, u32[]{:S(2)}, u32[]{:S(2)}) collective-permute-start(bf16[19,8,128]{2,1,0:T(8,128)(2,1)S(1)} %get-tuple-element.76), channel_id=1, source_target_pairs={{0,8},{8,0},{16,24},{24,16},{1,9},{9,1},{17,25},{25,17},{2,10},{10... | collective-permute-start | bytes 116744 | tf_op jit(solution)/shard_map/ppermute | solution.py:517
  21.5 0.8 %collective-permute-start.8 = (bf16[19,8,128]{2,1,0:T(8,128)(2,1)S(1)}, bf16[19,8,128]{2,1,0:T(8,128)(2,1)S(1)}, u32[]{:S(2)}, u32[]{:S(2)}) collective-permute-start(bf16[19,8,128]{2,1,0:T(8,128)(2,1)S(1)} %get-tuple-element.77), channel_id=1, source_target_pairs={{0,16},{8,24},{16,0},{24,8},{1,17},{9,25},{17,1},{25,9},{2,18},{10... | collective-permute-start | bytes 116744 | tf_op jit(solution)/shard_map/ppermute | solution.py:517
  22.2 1.2 %collective-permute-start.9 = (bf16[19,8,128]{2,1,0:T(8,128)(2,1)S(1)}, bf16[19,8,128]{2,1,0:T(8,128)(2,1)S(1)}, u32[]{:S(2)}, u32[]{:S(2)}) collective-permute-start(bf16[19,8,128]{2,1,0:T(8,128)(2,1)S(1)} %get-tuple-element.78), channel_id=1, source_target_pairs={{0,24},{8,16},{16,8},{24,0},{1,25},{9,17},{17,9},{25,1},{2,26},{10... | collective-permute-start | bytes 116744 | tf_op jit(solution)/shard_map/ppermute | solution.py:517
  23.5 0.5 %collective-permute-done.7.refs_1_ = bf16[19,8,128]{2,1,0:T(8,128)(2,1)S(1)} collective-permute-done((bf16[19,8,128]{2,1,0:T(8,128)(2,1)S(1)}, bf16[19,8,128]{2,1,0:T(8,128)(2,1)S(1)}, u32[]{:S(2)}, u32[]{:S(2)}) %collective-permute-start.7) | collective-permute-done | bytes 38944 | tf_op jit(solution)/shard_map/ppermute | solution.py:517
  24.0 1.9 %collective-permute-done.8.refs_2_ = bf16[19,8,128]{2,1,0:T(8,128)(2,1)S(1)} collective-permute-done((bf16[19,8,128]{2,1,0:T(8,128)(2,1)S(1)}, bf16[19,8,128]{2,1,0:T(8,128)(2,1)S(1)}, u32[]{:S(2)}, u32[]{:S(2)}) %collective-permute-start.8) | collective-permute-done | bytes 38944 | tf_op jit(solution)/shard_map/ppermute | solution.py:517
  25.9 1.2 %collective-permute-done.9.refs_3_ = bf16[19,8,128]{2,1,0:T(8,128)(2,1)S(1)} collective-permute-done((bf16[19,8,128]{2,1,0:T(8,128)(2,1)S(1)}, bf16[19,8,128]{2,1,0:T(8,128)(2,1)S(1)}, u32[]{:S(2)}, u32[]{:S(2)}) %collective-permute-start.9) | collective-permute-done | bytes 38944 | tf_op jit(solution)/shard_map/ppermute | solution.py:517
  27.1 2.4 %collective-permute-start.12 = (bf16[39,8,128]{2,1,0:T(8,128)(2,1)S(1)}, bf16[39,8,128]{2,1,0:T(8,128)(2,1)S(1)}, u32[]{:S(2)}, u32[]{:S(2)}) collective-permute-start(bf16[39,8,128]{2,1,0:T(8,128)(2,1)S(1)} %shard_map.141.refs_0_), channel_id=1, source_target_pairs={{0,6},{1,7},{2,4},{3,5},{4,2},{5,3},{6,0},{7,1},{8,14},{9,15},{10,... | collective-permute-start | bytes 239624 | tf_op jit(solution)/shard_map/ppermute | solution.py:517
  29.5 0.0 collective-permute-start.11
  29.5 2.0 %collective-permute-start.10 = (bf16[39,8,128]{2,1,0:T(8,128)(2,1)S(1)}, bf16[39,8,128]{2,1,0:T(8,128)(2,1)S(1)}, u32[]{:S(2)}, u32[]{:S(2)}) collective-permute-start(bf16[39,8,128]{2,1,0:T(8,128)(2,1)S(1)} %shard_map.141.refs_0_), channel_id=1, source_target_pairs={{0,2},{1,3},{2,0},{3,1},{4,6},{5,7},{6,4},{7,5},{8,10},{9,11},{10,... | collective-permute-start | bytes 239624 | tf_op jit(solution)/shard_map/ppermute | solution.py:517
  31.6 0.0 collective-permute-start.3
  31.6 0.3 collective-permute-start.4
  31.9 2.4 %collective-permute-done.12.refs_3_ = bf16[39,8,128]{2,1,0:T(8,128)(2,1)S(1)} collective-permute-done((bf16[39,8,128]{2,1,0:T(8,128)(2,1)S(1)}, bf16[39,8,128]{2,1,0:T(8,128)(2,1)S(1)}, u32[]{:S(2)}, u32[]{:S(2)}) %collective-permute-start.12) | collective-permute-done | bytes 79904 | tf_op jit(solution)/shard_map/ppermute | solution.py:517
  34.3 0.0 collective-permute-start.5
  34.3 1.6 %collective-permute-done.11.refs_2_ = bf16[39,8,128]{2,1,0:T(8,128)(2,1)S(1)} collective-permute-done((bf16[39,8,128]{2,1,0:T(8,128)(2,1)S(1)}, bf16[39,8,128]{2,1,0:T(8,128)(2,1)S(1)}, u32[]{:S(2)}, u32[]{:S(2)}) %collective-permute-start.11) | collective-permute-done | bytes 79904 | tf_op jit(solution)/shard_map/ppermute | solution.py:517
  35.9 0.0 collective-permute-done.10.refs_1_
  35.9 1.3 %collective-permute-start.15 = (bf16[19,8,128]{2,1,0:T(8,128)(2,1)S(1)}, bf16[19,8,128]{2,1,0:T(8,128)(2,1)S(1)}, u32[]{:S(2)}, u32[]{:S(2)}) collective-permute-start(bf16[19,8,128]{2,1,0:T(8,128)(2,1)S(1)} %get-tuple-element.80.refs_0_), channel_id=1, source_target_pairs={{0,24},{8,16},{16,8},{24,0},{1,25},{9,17},{17,9},{25,1},{2,26},{10... | collective-permute-start | bytes 116744 | tf_op jit(solution)/shard_map/ppermute | solution.py:517
  37.2 0.5 %collective-permute-start.14 = (bf16[19,8,128]{2,1,0:T(8,128)(2,1)S(1)}, bf16[19,8,128]{2,1,0:T(8,128)(2,1)S(1)}, u32[]{:S(2)}, u32[]{:S(2)}) collective-permute-start(bf16[19,8,128]{2,1,0:T(8,128)(2,1)S(1)} %get-tuple-element.80.refs_0_), channel_id=1, source_target_pairs={{0,16},{8,24},{16,0},{24,8},{1,17},{9,25},{17,1},{25,9},{2,18},{10... | collective-permute-start | bytes 116744 | tf_op jit(solution)/shard_map/ppermute | solution.py:517
  37.7 0.0 collective-permute-done.3.from_lon
  37.7 1.8 %collective-permute-start.13 = (bf16[19,8,128]{2,1,0:T(8,128)(2,1)S(1)}, bf16[19,8,128]{2,1,0:T(8,128)(2,1)S(1)}, u32[]{:S(2)}, u32[]{:S(2)}) collective-permute-start(bf16[19,8,128]{2,1,0:T(8,128)(2,1)S(1)} %get-tuple-element.80.refs_0_), channel_id=1, source_target_pairs={{0,8},{8,0},{16,24},{24,16},{1,9},{9,1},{17,25},{25,17},{2,10},{10... | collective-permute-start | bytes 116744 | tf_op jit(solution)/shard_map/ppermute | solution.py:517
  39.5 1.5 %shard_map.143.refs_8_ = bf16[8,3328]{1,0:T(8,128)(2,1)S(1)} custom-call(bf16[20,8,128]{2,1,0:T(8,128)(2,1)S(1)} %get-tuple-element.81.blocks, s32[32,128]{1,0:T(8,128)S(1)} %get-tuple-element.82.piece, s32[32,128]{1,0:T(8,128)S(1)} %get-tuple-element.83.spot), custom_call_target="tpu_custom_call" | custom-call | bytes 5000000 | tf_op jit(solution)/shard_map/pallas_call | solution.py:598
  41.0 0.0 collective-permute-done.4.from_lat
  41.0 0.1 collective-permute-start.20
  41.0 0.5 %collective-permute-done.5.from_both = bf16[27,8,128]{2,1,0:T(8,128)(2,1)S(1)} collective-permute-done((bf16[27,8,128]{2,1,0:T(8,128)(2,1)S(1)}, bf16[27,8,128]{2,1,0:T(8,128)(2,1)S(1)}, u32[]{:S(2)}, u32[]{:S(2)}) %collective-permute-start.5) | collective-permute-done | bytes 55328 | tf_op jit(solution)/shard_map/ppermute | solution.py:527
  41.6 0.0 collective-permute-start.16
  41.6 0.0 collective-permute-done.15.refs_3_
  41.6 0.5 %collective-permute-start.19 = (bf16[19,8,128]{2,1,0:T(8,128)(2,1)S(1)}, bf16[19,8,128]{2,1,0:T(8,128)(2,1)S(1)}, u32[]{:S(2)}, u32[]{:S(2)}) collective-permute-start(bf16[19,8,128]{2,1,0:T(8,128)(2,1)S(1)} %collective-permute-done.15.refs_3_), channel_id=1, source_target_pairs={{0,1},{1,0},{2,3},{3,2},{4,5},{5,4},{6,7},{7,6},{8,9},{9,8},{10,11... | collective-permute-start | bytes 116744 | tf_op jit(solution)/shard_map/ppermute | solution.py:517
  42.1 0.0 collective-permute-done.14.refs_2_
  42.1 0.1 collective-permute-start.18
  42.1 0.0 collective-permute-done.13.refs_1_
  42.2 0.4 collective-permute-start.17
  42.6 0.8 %shard_map.138 = (bf16[6,12,4,192]{3,2,1,0:T(4,128)(2,1)}, bf16[6,12,4,192]{3,2,1,0:T(4,128)(2,1)}) custom-call(bf16[27,8,128]{2,1,0:T(8,128)(2,1)S(1)} %get-tuple-element.59.here, bf16[27,8,128]{2,1,0:T(8,128)(2,1)S(1)} %collective-permute-done.3.from_lon, bf16[27,8,128]{2,1,0:T(8,128)(2,1)S(1)} %collective-permute-done.4.from_lat, ...), custom_call_target="tpu_custom_call" | custom-call | bytes 2000000 | tf_op jit(solution)/shard_map/pallas_call | solution.py:605
  43.4 0.0 collective-permute-done.16.refs_4_
  43.4 0.0 collective-permute-done.20.refs_9_
  43.4 0.0 collective-permute-done.19.refs_7_
  43.4 0.0 collective-permute-done.18.refs_6_
  43.4 0.1 collective-permute-done.17.refs_5_
  43.5 1.0 %shard_map.144 = (f32[1,192]{1,0:T(1,128)}, f32[1,192]{1,0:T(1,128)}, f32[192,576]{1,0:T(8,128)}, f32[192,192]{1,0:T(8,128)}, f32[2,6,1,3312]{3,2,1,0:T(1,128)}) custom-call(bf16[19,8,128]{2,1,0:T(8,128)(2,1)S(1)} %get-tuple-element.80.refs_0_, bf16[19,8,128]{2,1,0:T(8,128)(2,1)S(1)} %collective-permute-done.13.refs_1_, ...), custom_call_target="tpu_custom_call" | custom-call | tf_op jit(solution)/shard_map/pallas_call | solution.py:610
  (3 shorter events, 0.1 us)
Async XLA Ops:
  2.1 11.3 %collective-permute-start = (bf16[2,3,6,4,192]{4,3,2,1,0:T(4,128)(2,1)S(1)}, bf16[2,3,6,4,192]{4,3,2,1,0:T(4,128)(2,1)S(1)}, u32[]{:S(2)}, u32[]{:S(2)}) collective-permute-start(bf16[2,3,6,4,192]{4,3,2,1,0:T(4,128)(2,1)S(1)} %get-tuple-element.49), channel_id=1, source_target_pairs={{0,7},{1,0},{2,1},{3,2},{4,3},{5,4},{6,5},{7,6},{8,15},{9,8},{10,9... | collective-permute-start | bytes 165896 | tf_op jit(solution)/shard_map/ppermute | solution.py:527
  6.6 6.7 %collective-permute-start.1 = (bf16[2,3,6,4,192]{4,3,2,1,0:T(4,128)(2,1)S(1)}, bf16[2,3,6,4,192]{4,3,2,1,0:T(4,128)(2,1)S(1)}, u32[]{:S(2)}, u32[]{:S(2)}) collective-permute-start(bf16[2,3,6,4,192]{4,3,2,1,0:T(4,128)(2,1)S(1)} %get-tuple-element.50), channel_id=1, source_target_pairs={{0,24},{1,25},{2,26},{3,27},{4,28},{5,29},{6,30},{7,31},{8,0},{9,1... | collective-permute-start | bytes 165896 | tf_op jit(solution)/shard_map/ppermute | solution.py:527
  9.0 4.3 %collective-permute-start.2 = (bf16[2,3,6,4,192]{4,3,2,1,0:T(4,128)(2,1)S(1)}, bf16[2,3,6,4,192]{4,3,2,1,0:T(4,128)(2,1)S(1)}, u32[]{:S(2)}, u32[]{:S(2)}) collective-permute-start(bf16[2,3,6,4,192]{4,3,2,1,0:T(4,128)(2,1)S(1)} %get-tuple-element.51), channel_id=1, source_target_pairs={{0,31},{1,24},{2,25},{3,26},{4,27},{5,28},{6,29},{7,30},{8,7},{9,0... | collective-permute-start | bytes 165896 | tf_op jit(solution)/shard_map/ppermute | solution.py:527
  18.4 1.5 %collective-permute-start.6 = (bf16[96,8,128]{2,1,0:T(8,128)(2,1)S(1)}, bf16[96,8,128]{2,1,0:T(8,128)(2,1)S(1)}, u32[]{:S(2)}, u32[]{:S(2)}) collective-permute-start(bf16[96,8,128]{2,1,0:T(8,128)(2,1)S(1)} %get-tuple-element.69), channel_id=1, source_target_pairs={{0,1},{1,0},{2,3},{3,2},{4,5},{5,4},{6,7},{7,6},{8,9},{9,8},{10,11... | collective-permute-start | bytes 589832 | tf_op jit(solution)/shard_map/ppermute | solution.py:517
  19.9 4.0 %collective-permute-start.7 = (bf16[19,8,128]{2,1,0:T(8,128)(2,1)S(1)}, bf16[19,8,128]{2,1,0:T(8,128)(2,1)S(1)}, u32[]{:S(2)}, u32[]{:S(2)}) collective-permute-start(bf16[19,8,128]{2,1,0:T(8,128)(2,1)S(1)} %get-tuple-element.76), channel_id=1, source_target_pairs={{0,8},{8,0},{16,24},{24,16},{1,9},{9,1},{17,25},{25,17},{2,10},{10... | collective-permute-start | bytes 116744 | tf_op jit(solution)/shard_map/ppermute | solution.py:517
  21.5 4.4 %collective-permute-start.8 = (bf16[19,8,128]{2,1,0:T(8,128)(2,1)S(1)}, bf16[19,8,128]{2,1,0:T(8,128)(2,1)S(1)}, u32[]{:S(2)}, u32[]{:S(2)}) collective-permute-start(bf16[19,8,128]{2,1,0:T(8,128)(2,1)S(1)} %get-tuple-element.77), channel_id=1, source_target_pairs={{0,16},{8,24},{16,0},{24,8},{1,17},{9,25},{17,1},{25,9},{2,18},{10... | collective-permute-start | bytes 116744 | tf_op jit(solution)/shard_map/ppermute | solution.py:517
  22.2 4.9 %collective-permute-start.9 = (bf16[19,8,128]{2,1,0:T(8,128)(2,1)S(1)}, bf16[19,8,128]{2,1,0:T(8,128)(2,1)S(1)}, u32[]{:S(2)}, u32[]{:S(2)}) collective-permute-start(bf16[19,8,128]{2,1,0:T(8,128)(2,1)S(1)} %get-tuple-element.78), channel_id=1, source_target_pairs={{0,24},{8,16},{16,8},{24,0},{1,25},{9,17},{17,9},{25,1},{2,26},{10... | collective-permute-start | bytes 116744 | tf_op jit(solution)/shard_map/ppermute | solution.py:517
  27.1 7.2 %collective-permute-start.12 = (bf16[39,8,128]{2,1,0:T(8,128)(2,1)S(1)}, bf16[39,8,128]{2,1,0:T(8,128)(2,1)S(1)}, u32[]{:S(2)}, u32[]{:S(2)}) collective-permute-start(bf16[39,8,128]{2,1,0:T(8,128)(2,1)S(1)} %shard_map.141.refs_0_), channel_id=1, source_target_pairs={{0,6},{1,7},{2,4},{3,5},{4,2},{5,3},{6,0},{7,1},{8,14},{9,15},{10,... | collective-permute-start | bytes 239624 | tf_op jit(solution)/shard_map/ppermute | solution.py:517
  29.5 6.3 %collective-permute-start.11 = (bf16[39,8,128]{2,1,0:T(8,128)(2,1)S(1)}, bf16[39,8,128]{2,1,0:T(8,128)(2,1)S(1)}, u32[]{:S(2)}, u32[]{:S(2)}) collective-permute-start(bf16[39,8,128]{2,1,0:T(8,128)(2,1)S(1)} %shard_map.141.refs_0_), channel_id=1, source_target_pairs={{0,4},{1,5},{2,6},{3,7},{4,0},{5,1},{6,2},{7,3},{8,12},{9,13},{10,... | collective-permute-start | bytes 239624 | tf_op jit(solution)/shard_map/ppermute | solution.py:517
  29.5 6.3 %collective-permute-start.10 = (bf16[39,8,128]{2,1,0:T(8,128)(2,1)S(1)}, bf16[39,8,128]{2,1,0:T(8,128)(2,1)S(1)}, u32[]{:S(2)}, u32[]{:S(2)}) collective-permute-start(bf16[39,8,128]{2,1,0:T(8,128)(2,1)S(1)} %shard_map.141.refs_0_), channel_id=1, source_target_pairs={{0,2},{1,3},{2,0},{3,1},{4,6},{5,7},{6,4},{7,5},{8,10},{9,11},{10,... | collective-permute-start | bytes 239624 | tf_op jit(solution)/shard_map/ppermute | solution.py:517
  31.6 6.1 %collective-permute-start.3 = (bf16[27,8,128]{2,1,0:T(8,128)(2,1)S(1)}, bf16[27,8,128]{2,1,0:T(8,128)(2,1)S(1)}, u32[]{:S(2)}, u32[]{:S(2)}) collective-permute-start(bf16[27,8,128]{2,1,0:T(8,128)(2,1)S(1)} %get-tuple-element.60), channel_id=1, source_target_pairs={{0,1},{1,2},{2,3},{3,4},{4,5},{5,6},{6,7},{7,0},{8,9},{9,10},{10,1... | collective-permute-start | bytes 165896 | tf_op jit(solution)/shard_map/ppermute | solution.py:527
  31.6 9.4 %collective-permute-start.4 = (bf16[27,8,128]{2,1,0:T(8,128)(2,1)S(1)}, bf16[27,8,128]{2,1,0:T(8,128)(2,1)S(1)}, u32[]{:S(2)}, u32[]{:S(2)}) collective-permute-start(bf16[27,8,128]{2,1,0:T(8,128)(2,1)S(1)} %get-tuple-element.61), channel_id=1, source_target_pairs={{0,8},{1,9},{2,10},{3,11},{4,12},{5,13},{6,14},{7,15},{8,16},{9,17... | collective-permute-start | bytes 165896 | tf_op jit(solution)/shard_map/ppermute | solution.py:527
  34.3 7.3 %collective-permute-start.5 = (bf16[27,8,128]{2,1,0:T(8,128)(2,1)S(1)}, bf16[27,8,128]{2,1,0:T(8,128)(2,1)S(1)}, u32[]{:S(2)}, u32[]{:S(2)}) collective-permute-start(bf16[27,8,128]{2,1,0:T(8,128)(2,1)S(1)} %get-tuple-element.62), channel_id=1, source_target_pairs={{0,9},{1,10},{2,11},{3,12},{4,13},{5,14},{6,15},{7,8},{8,17},{9,18... | collective-permute-start | bytes 165896 | tf_op jit(solution)/shard_map/ppermute | solution.py:527
  35.9 5.6 %collective-permute-start.15 = (bf16[19,8,128]{2,1,0:T(8,128)(2,1)S(1)}, bf16[19,8,128]{2,1,0:T(8,128)(2,1)S(1)}, u32[]{:S(2)}, u32[]{:S(2)}) collective-permute-start(bf16[19,8,128]{2,1,0:T(8,128)(2,1)S(1)} %get-tuple-element.80.refs_0_), channel_id=1, source_target_pairs={{0,24},{8,16},{16,8},{24,0},{1,25},{9,17},{17,9},{25,1},{2,26},{10... | collective-permute-start | bytes 116744 | tf_op jit(solution)/shard_map/ppermute | solution.py:517
  37.2 4.9 %collective-permute-start.14 = (bf16[19,8,128]{2,1,0:T(8,128)(2,1)S(1)}, bf16[19,8,128]{2,1,0:T(8,128)(2,1)S(1)}, u32[]{:S(2)}, u32[]{:S(2)}) collective-permute-start(bf16[19,8,128]{2,1,0:T(8,128)(2,1)S(1)} %get-tuple-element.80.refs_0_), channel_id=1, source_target_pairs={{0,16},{8,24},{16,0},{24,8},{1,17},{9,25},{17,1},{25,9},{2,18},{10... | collective-permute-start | bytes 116744 | tf_op jit(solution)/shard_map/ppermute | solution.py:517
  37.7 4.5 %collective-permute-start.13 = (bf16[19,8,128]{2,1,0:T(8,128)(2,1)S(1)}, bf16[19,8,128]{2,1,0:T(8,128)(2,1)S(1)}, u32[]{:S(2)}, u32[]{:S(2)}) collective-permute-start(bf16[19,8,128]{2,1,0:T(8,128)(2,1)S(1)} %get-tuple-element.80.refs_0_), channel_id=1, source_target_pairs={{0,8},{8,0},{16,24},{24,16},{1,9},{9,1},{17,25},{25,17},{2,10},{10... | collective-permute-start | bytes 116744 | tf_op jit(solution)/shard_map/ppermute | solution.py:517
  41.0 2.4 %collective-permute-start.20 = (bf16[8,3328]{1,0:T(8,128)(2,1)S(1)}, bf16[8,3328]{1,0:T(8,128)(2,1)S(1)}, u32[]{:S(2)}, u32[]{:S(2)}) collective-permute-start(bf16[8,3328]{1,0:T(8,128)(2,1)S(1)} %shard_map.143.refs_8_), channel_id=1, source_target_pairs={{0,1},{1,0},{2,3},{3,2},{4,5},{5,4},{6,7},{7,6},{8,9},{9,8},{10,11... | collective-permute-start | bytes 159752 | tf_op jit(solution)/shard_map/ppermute | solution.py:517
  41.6 1.8 %collective-permute-start.16 = (bf16[19,8,128]{2,1,0:T(8,128)(2,1)S(1)}, bf16[19,8,128]{2,1,0:T(8,128)(2,1)S(1)}, u32[]{:S(2)}, u32[]{:S(2)}) collective-permute-start(bf16[19,8,128]{2,1,0:T(8,128)(2,1)S(1)} %get-tuple-element.80.refs_0_), channel_id=1, source_target_pairs={{0,1},{1,0},{2,3},{3,2},{4,5},{5,4},{6,7},{7,6},{8,9},{9,8},{10,11... | collective-permute-start | bytes 116744 | tf_op jit(solution)/shard_map/ppermute | solution.py:517
  41.6 1.8 %collective-permute-start.19 = (bf16[19,8,128]{2,1,0:T(8,128)(2,1)S(1)}, bf16[19,8,128]{2,1,0:T(8,128)(2,1)S(1)}, u32[]{:S(2)}, u32[]{:S(2)}) collective-permute-start(bf16[19,8,128]{2,1,0:T(8,128)(2,1)S(1)} %collective-permute-done.15.refs_3_), channel_id=1, source_target_pairs={{0,1},{1,0},{2,3},{3,2},{4,5},{5,4},{6,7},{7,6},{8,9},{9,8},{10,11... | collective-permute-start | bytes 116744 | tf_op jit(solution)/shard_map/ppermute | solution.py:517
  42.1 1.3 %collective-permute-start.18 = (bf16[19,8,128]{2,1,0:T(8,128)(2,1)S(1)}, bf16[19,8,128]{2,1,0:T(8,128)(2,1)S(1)}, u32[]{:S(2)}, u32[]{:S(2)}) collective-permute-start(bf16[19,8,128]{2,1,0:T(8,128)(2,1)S(1)} %collective-permute-done.14.refs_2_), channel_id=1, source_target_pairs={{0,1},{1,0},{2,3},{3,2},{4,5},{5,4},{6,7},{7,6},{8,9},{9,8},{10,11... | collective-permute-start | bytes 116744 | tf_op jit(solution)/shard_map/ppermute | solution.py:517
  42.2 1.3 %collective-permute-start.17 = (bf16[19,8,128]{2,1,0:T(8,128)(2,1)S(1)}, bf16[19,8,128]{2,1,0:T(8,128)(2,1)S(1)}, u32[]{:S(2)}, u32[]{:S(2)}) collective-permute-start(bf16[19,8,128]{2,1,0:T(8,128)(2,1)S(1)} %collective-permute-done.13.refs_1_), channel_id=1, source_target_pairs={{0,1},{1,0},{2,3},{3,2},{4,5},{5,4},{6,7},{7,6},{8,9},{9,8},{10,11... | collective-permute-start | bytes 116744 | tf_op jit(solution)/shard_map/ppermute | solution.py:517

commit v5 on v4

--- a/solution.py
+++ b/solution.py
@@ -588,9 +588,10 @@
     came, piece, spot = lax.optimization_barrier((came, piece, spot))
     *pieces, tail = call(halves_body, (stack(blocks),) * lat_count + (stack(table_blocks),))(keep, came)
     pieces = [swap(p, "lat", at) if at else p for at, p in enumerate(pieces)]
+    returned = [shifted(b, lat, lon) for b, (lat, lon) in zip(backs, steps)]
+    tail, returned[0] = lax.optimization_barrier((tail, returned[0]))
     part = call(lats_body, stack(blocks + table_blocks))(*pieces, tail)
     parts = [part] + [swap(part, "lon", 2 * at) for at in range(1, lon_count // 2)]
-    returned = [shifted(b, lat, lon) for b, (lat, lon) in zip(backs, steps)]
     weights, tail = call(functools.partial(lons_body, len(parts)), (stack(blocks), stack(table_blocks)))(
         *parts
     )

time: 44.6 us -> 44.5 us (level)
  waiting for transfers between devices: 8.75 us -> 8.27 us
    ppermute x15, waiting for transfers between devices: 8.22 us -> 7.65 us  [swap(): lax.ppermute(value, axis, [(source, source ^ distance) for source in rang...]
  transfers between devices with their start and end apart: 21 -> 21, of which waited for: 8 -> 7; matrix products, arithmetic and copies ran while one was open for 0% -> 0% of each run, Pallas kernels for 15% -> 16%
where the time goes in v5:
time: 44.5 us; the launch traced here: 44.3 us
  starting transfers between devices  20.9 us (47%)
  Pallas kernels  14.3 us (32%)
  waiting for transfers between devices  8.27 us (19%)
  between operations  0.76 us (2%)
    ppermute x15, starting transfers between devices, swap(): lax.ppermute(value, axis, [(source, source ^ distance) for source in rang...  13.1 us
    ppermute x6, starting transfers between devices, shifted(): return lax.ppermute(value, ('lat', 'lon'), pairs)  7.88 us
    ppermute x15, waiting for transfers between devices, swap(): lax.ppermute(value, axis, [(source, source ^ distance) for source in rang...  7.65 us
    pallas_call x1, Pallas kernels, on_device(): call(window_body, (stack(quad_blocks),) * 4 + (half, half), [pltpu.VMEM((...  4.99 us
    pallas_call x1, Pallas kernels, on_device(): call(bias_body, (struct((level_win * heads, WIN, WIN), f32), spread, spre...  3.91 us
    pallas_call x1, Pallas kernels, on_device(): call(place_body, struct((SUBLANES, whole_lanes), bf16), moved=5 * 10 ** 6)  1.46 us
    pallas_call x1, Pallas kernels, on_device(): call(functools.partial(pack_body, len(plain)), (quad,) * 4 + tuple((struc...  1.42 us
    pallas_call x1, Pallas kernels, on_device(): call(functools.partial(finish_body, lat_count, factor), (row, row, struct...  1.02 us
  transfers between devices with their start and end apart: 21, of which 7 were waited for; matrix products, arithmetic and copies ran while one was open for 0% of the time, Pallas kernels for 16%

profile of v5, /device:TPU:0, one launch (start us, length us, event | category | flops | bytes accessed | tf_op | source)
XLA Modules:
  0.0 44.3 jit_solution(18431379160051682701)
XLA Ops:
  0.6 1.4 %shard_map.135 = (bf16[2,3,6,4,192]{4,3,2,1,0:T(4,128)(2,1)S(1)}, bf16[2,3,6,4,192]{4,3,2,1,0:T(4,128)(2,1)S(1)}, bf16[2,3,6,4,192]{4,3,2,1,0:T(4,128)(2,1)S(1)}...) custom-call(bf16[6,12,4,192]{3,2,1,0:T(4,128)(2,1)} %bitcast.11, ...), custom_call_target="tpu_custom_call" | custom-call | tf_op jit(solution)/shard_map/pallas_call | solution.py:541
  2.1 4.5 %collective-permute-start = (bf16[2,3,6,4,192]{4,3,2,1,0:T(4,128)(2,1)S(1)}, bf16[2,3,6,4,192]{4,3,2,1,0:T(4,128)(2,1)S(1)}, u32[]{:S(2)}, u32[]{:S(2)}) collective-permute-start(bf16[2,3,6,4,192]{4,3,2,1,0:T(4,128)(2,1)S(1)} %get-tuple-element.51), channel_id=1, source_target_pairs={{0,7},{1,0},{2,1},{3,2},{4,3},{5,4},{6,5},{7,6},{8,15},{9,8},{10,9... | collective-permute-start | bytes 165896 | tf_op jit(solution)/shard_map/ppermute | solution.py:527
  6.6 2.4 %collective-permute-start.1 = (bf16[2,3,6,4,192]{4,3,2,1,0:T(4,128)(2,1)S(1)}, bf16[2,3,6,4,192]{4,3,2,1,0:T(4,128)(2,1)S(1)}, u32[]{:S(2)}, u32[]{:S(2)}) collective-permute-start(bf16[2,3,6,4,192]{4,3,2,1,0:T(4,128)(2,1)S(1)} %get-tuple-element.52), channel_id=1, source_target_pairs={{0,24},{1,25},{2,26},{3,27},{4,28},{5,29},{6,30},{7,31},{8,0},{9,1... | collective-permute-start | bytes 165896 | tf_op jit(solution)/shard_map/ppermute | solution.py:527
  9.0 0.4 collective-permute-start.2
  9.4 3.9 %shard_map.136 = (f32[12,144,144]{2,1,0:T(8,128)S(1)}, s32[16,384]{1,0:T(8,128)S(1)}, s32[16,384]{1,0:T(8,128)S(1)}) custom-call(f32[2,6,1,3312]{3,2,1,0:T(1,128)S(1)} %get-tuple-element.58.bias_table, s32[144,144]{1,0:T(8,128)S(1)} %get-tuple-element.59.index_table), custom_call_target="tpu_custom_call" | custom-call | bytes 16000000 | tf_op jit(solution)/shard_map/pallas_call | solution.py:557
  13.3 0.0 collective-permute-done.from_lon
  13.3 0.0 collective-permute-done.1.from_lat
  13.3 0.0 collective-permute-done.2.from_both
  13.4 5.0 %shard_map.137 = (bf16[27,8,128]{2,1,0:T(8,128)(2,1)S(1)}, bf16[27,8,128]{2,1,0:T(8,128)(2,1)S(1)}, bf16[27,8,128]{2,1,0:T(8,128)(2,1)S(1)}, bf16[27,8,128]{2,1,...) custom-call(bf16[2,3,6,4,192]{4,3,2,1,0:T(4,128)(2,1)S(1)} %get-tuple-element.50.here, ...), custom_call_target="tpu_custom_call" | custom-call | bytes 25000000 | tf_op jit(solution)/shard_map/pallas_call | solution.py:572
  18.4 0.3 collective-permute-start.3
  18.7 0.2 collective-permute-start.4
  18.9 0.6 %shard_map.138 = (s32[32,128]{1,0:T(8,128)S(1)}, s32[32,128]{1,0:T(8,128)S(1)}) custom-call(s32[16,384]{1,0:T(8,128)S(1)} %get-tuple-element.67.chunk, s32[16,384]{1,0:T(8,128)S(1)} %get-tuple-element.68.lane), custom_call_target="tpu_custom_call" | custom-call | bytes 2000000 | tf_op jit(solution)/shard_map/pallas_call | solution.py:587
  19.6 0.3 collective-permute-done.3.came
  19.9 1.5 %collective-permute-start.7 = (bf16[19,8,128]{2,1,0:T(8,128)(2,1)S(1)}, bf16[19,8,128]{2,1,0:T(8,128)(2,1)S(1)}, u32[]{:S(2)}, u32[]{:S(2)}) collective-permute-start(bf16[19,8,128]{2,1,0:T(8,128)(2,1)S(1)} %get-tuple-element.80), channel_id=1, source_target_pairs={{0,8},{8,0},{16,24},{24,16},{1,9},{9,1},{17,25},{25,17},{2,10},{10... | collective-permute-start | bytes 116744 | tf_op jit(solution)/shard_map/ppermute | solution.py:517
  21.5 0.8 %collective-permute-start.8 = (bf16[19,8,128]{2,1,0:T(8,128)(2,1)S(1)}, bf16[19,8,128]{2,1,0:T(8,128)(2,1)S(1)}, u32[]{:S(2)}, u32[]{:S(2)}) collective-permute-start(bf16[19,8,128]{2,1,0:T(8,128)(2,1)S(1)} %get-tuple-element.81), channel_id=1, source_target_pairs={{0,16},{8,24},{16,0},{24,8},{1,17},{9,25},{17,1},{25,9},{2,18},{10... | collective-permute-start | bytes 116744 | tf_op jit(solution)/shard_map/ppermute | solution.py:517
  22.2 1.2 %collective-permute-start.9 = (bf16[19,8,128]{2,1,0:T(8,128)(2,1)S(1)}, bf16[19,8,128]{2,1,0:T(8,128)(2,1)S(1)}, u32[]{:S(2)}, u32[]{:S(2)}) collective-permute-start(bf16[19,8,128]{2,1,0:T(8,128)(2,1)S(1)} %get-tuple-element.82), channel_id=1, source_target_pairs={{0,24},{8,16},{16,8},{24,0},{1,25},{9,17},{17,9},{25,1},{2,26},{10... | collective-permute-start | bytes 116744 | tf_op jit(solution)/shard_map/ppermute | solution.py:517
  23.5 0.6 %collective-permute-done.4.from_lon = bf16[27,8,128]{2,1,0:T(8,128)(2,1)S(1)} collective-permute-done((bf16[27,8,128]{2,1,0:T(8,128)(2,1)S(1)}, bf16[27,8,128]{2,1,0:T(8,128)(2,1)S(1)}, u32[]{:S(2)}, u32[]{:S(2)}) %collective-permute-start.4) | collective-permute-done | bytes 55328 | tf_op jit(solution)/shard_map/ppermute | solution.py:527
  24.1 0.0 collective-permute-done.7.refs_1_
  24.1 1.8 %collective-permute-done.8.refs_2_ = bf16[19,8,128]{2,1,0:T(8,128)(2,1)S(1)} collective-permute-done((bf16[19,8,128]{2,1,0:T(8,128)(2,1)S(1)}, bf16[19,8,128]{2,1,0:T(8,128)(2,1)S(1)}, u32[]{:S(2)}, u32[]{:S(2)}) %collective-permute-start.8) | collective-permute-done | bytes 38944 | tf_op jit(solution)/shard_map/ppermute | solution.py:517
  25.9 1.2 %collective-permute-done.9.refs_3_ = bf16[19,8,128]{2,1,0:T(8,128)(2,1)S(1)} collective-permute-done((bf16[19,8,128]{2,1,0:T(8,128)(2,1)S(1)}, bf16[19,8,128]{2,1,0:T(8,128)(2,1)S(1)}, u32[]{:S(2)}, u32[]{:S(2)}) %collective-permute-start.9) | collective-permute-done | bytes 38944 | tf_op jit(solution)/shard_map/ppermute | solution.py:517
  27.1 2.4 %collective-permute-start.12 = (bf16[39,8,128]{2,1,0:T(8,128)(2,1)S(1)}, bf16[39,8,128]{2,1,0:T(8,128)(2,1)S(1)}, u32[]{:S(2)}, u32[]{:S(2)}) collective-permute-start(bf16[39,8,128]{2,1,0:T(8,128)(2,1)S(1)} %shard_map.141.refs_0_), channel_id=1, source_target_pairs={{0,6},{1,7},{2,4},{3,5},{4,2},{5,3},{6,0},{7,1},{8,14},{9,15},{10,... | collective-permute-start | bytes 239624 | tf_op jit(solution)/shard_map/ppermute | solution.py:517
  29.5 0.0 collective-permute-start.11
  29.5 2.1 %collective-permute-start.10 = (bf16[39,8,128]{2,1,0:T(8,128)(2,1)S(1)}, bf16[39,8,128]{2,1,0:T(8,128)(2,1)S(1)}, u32[]{:S(2)}, u32[]{:S(2)}) collective-permute-start(bf16[39,8,128]{2,1,0:T(8,128)(2,1)S(1)} %shard_map.141.refs_0_), channel_id=1, source_target_pairs={{0,2},{1,3},{2,0},{3,1},{4,6},{5,7},{6,4},{7,5},{8,10},{9,11},{10,... | collective-permute-start | bytes 239624 | tf_op jit(solution)/shard_map/ppermute | solution.py:517
  31.6 0.3 collective-permute-start.5
  31.9 0.0 collective-permute-start.6
  31.9 2.0 %collective-permute-done.12.refs_3_ = bf16[39,8,128]{2,1,0:T(8,128)(2,1)S(1)} collective-permute-done((bf16[39,8,128]{2,1,0:T(8,128)(2,1)S(1)}, bf16[39,8,128]{2,1,0:T(8,128)(2,1)S(1)}, u32[]{:S(2)}, u32[]{:S(2)}) %collective-permute-start.12) | collective-permute-done | bytes 79904 | tf_op jit(solution)/shard_map/ppermute | solution.py:517
  33.9 2.0 %collective-permute-done.11.refs_2_ = bf16[39,8,128]{2,1,0:T(8,128)(2,1)S(1)} collective-permute-done((bf16[39,8,128]{2,1,0:T(8,128)(2,1)S(1)}, bf16[39,8,128]{2,1,0:T(8,128)(2,1)S(1)}, u32[]{:S(2)}, u32[]{:S(2)}) %collective-permute-start.11) | collective-permute-done | bytes 79904 | tf_op jit(solution)/shard_map/ppermute | solution.py:517
  35.9 0.0 collective-permute-done.10.refs_1_
  35.9 1.4 %collective-permute-start.15 = (bf16[19,8,128]{2,1,0:T(8,128)(2,1)S(1)}, bf16[19,8,128]{2,1,0:T(8,128)(2,1)S(1)}, u32[]{:S(2)}, u32[]{:S(2)}) collective-permute-start(bf16[19,8,128]{2,1,0:T(8,128)(2,1)S(1)} %get-tuple-element.84.refs_0_), channel_id=1, source_target_pairs={{0,24},{8,16},{16,8},{24,0},{1,25},{9,17},{17,9},{25,1},{2,26},{10... | collective-permute-start | bytes 116744 | tf_op jit(solution)/shard_map/ppermute | solution.py:517
  37.3 0.6 %collective-permute-start.14 = (bf16[19,8,128]{2,1,0:T(8,128)(2,1)S(1)}, bf16[19,8,128]{2,1,0:T(8,128)(2,1)S(1)}, u32[]{:S(2)}, u32[]{:S(2)}) collective-permute-start(bf16[19,8,128]{2,1,0:T(8,128)(2,1)S(1)} %get-tuple-element.84.refs_0_), channel_id=1, source_target_pairs={{0,16},{8,24},{16,0},{24,8},{1,17},{9,25},{17,1},{25,9},{2,18},{10... | collective-permute-start | bytes 116744 | tf_op jit(solution)/shard_map/ppermute | solution.py:517
  37.9 1.6 %collective-permute-start.13 = (bf16[19,8,128]{2,1,0:T(8,128)(2,1)S(1)}, bf16[19,8,128]{2,1,0:T(8,128)(2,1)S(1)}, u32[]{:S(2)}, u32[]{:S(2)}) collective-permute-start(bf16[19,8,128]{2,1,0:T(8,128)(2,1)S(1)} %get-tuple-element.84.refs_0_), channel_id=1, source_target_pairs={{0,8},{8,0},{16,24},{24,16},{1,9},{9,1},{17,25},{25,17},{2,10},{10... | collective-permute-start | bytes 116744 | tf_op jit(solution)/shard_map/ppermute | solution.py:517
  39.5 1.5 %shard_map.143.refs_8_ = bf16[8,3328]{1,0:T(8,128)(2,1)S(1)} custom-call(bf16[20,8,128]{2,1,0:T(8,128)(2,1)S(1)} %get-tuple-element.85.blocks, s32[32,128]{1,0:T(8,128)S(1)} %get-tuple-element.86.piece, s32[32,128]{1,0:T(8,128)S(1)} %get-tuple-element.87.spot), custom_call_target="tpu_custom_call" | custom-call | bytes 5000000 | tf_op jit(solution)/shard_map/pallas_call | solution.py:599
  40.9 0.0 collective-permute-done.5.from_lat
  41.0 0.1 collective-permute-start.20
  41.0 0.0 collective-permute-done.6.from_both
  41.0 0.5 %collective-permute-start.16 = (bf16[19,8,128]{2,1,0:T(8,128)(2,1)S(1)}, bf16[19,8,128]{2,1,0:T(8,128)(2,1)S(1)}, u32[]{:S(2)}, u32[]{:S(2)}) collective-permute-start(bf16[19,8,128]{2,1,0:T(8,128)(2,1)S(1)} %get-tuple-element.84.refs_0_), channel_id=1, source_target_pairs={{0,1},{1,0},{2,3},{3,2},{4,5},{5,4},{6,7},{7,6},{8,9},{9,8},{10,11... | collective-permute-start | bytes 116744 | tf_op jit(solution)/shard_map/ppermute | solution.py:517
  41.5 0.0 collective-permute-done.15.refs_3_
  41.5 0.1 collective-permute-start.19
  41.6 0.0 collective-permute-done.14.refs_2_
  41.6 0.4 collective-permute-start.18
  42.1 0.0 collective-permute-done.13.refs_1_
  42.1 0.1 collective-permute-start.17
  42.1 0.8 %shard_map.140 = (bf16[6,12,4,192]{3,2,1,0:T(4,128)(2,1)}, bf16[6,12,4,192]{3,2,1,0:T(4,128)(2,1)}) custom-call(bf16[27,8,128]{2,1,0:T(8,128)(2,1)S(1)} %get-tuple-element.61.here, bf16[27,8,128]{2,1,0:T(8,128)(2,1)S(1)} %collective-permute-done.4.from_lon, bf16[27,8,128]{2,1,0:T(8,128)(2,1)S(1)} %collective-permute-done.5.from_lat, ...), custom_call_target="tpu_custom_call" | custom-call | bytes 2000000 | tf_op jit(solution)/shard_map/pallas_call | solution.py:606
  42.9 0.0 collective-permute-done.16.refs_4_
  42.9 0.0 collective-permute-done.20.refs_9_
  42.9 0.0 collective-permute-done.19.refs_7_
  42.9 0.0 collective-permute-done.18.refs_6_
  43.0 0.3 collective-permute-done.17.refs_5_
  43.3 1.0 %shard_map.144 = (f32[1,192]{1,0:T(1,128)}, f32[1,192]{1,0:T(1,128)}, f32[192,576]{1,0:T(8,128)}, f32[192,192]{1,0:T(8,128)}, f32[2,6,1,3312]{3,2,1,0:T(1,128)}) custom-call(bf16[19,8,128]{2,1,0:T(8,128)(2,1)S(1)} %get-tuple-element.84.refs_0_, bf16[19,8,128]{2,1,0:T(8,128)(2,1)S(1)} %collective-permute-done.13.refs_1_, ...), custom_call_target="tpu_custom_call" | custom-call | tf_op jit(solution)/shard_map/pallas_call | solution.py:611
  (3 shorter events, 0.1 us)
Async XLA Ops:
  2.1 11.3 %collective-permute-start = (bf16[2,3,6,4,192]{4,3,2,1,0:T(4,128)(2,1)S(1)}, bf16[2,3,6,4,192]{4,3,2,1,0:T(4,128)(2,1)S(1)}, u32[]{:S(2)}, u32[]{:S(2)}) collective-permute-start(bf16[2,3,6,4,192]{4,3,2,1,0:T(4,128)(2,1)S(1)} %get-tuple-element.51), channel_id=1, source_target_pairs={{0,7},{1,0},{2,1},{3,2},{4,3},{5,4},{6,5},{7,6},{8,15},{9,8},{10,9... | collective-permute-start | bytes 165896 | tf_op jit(solution)/shard_map/ppermute | solution.py:527
  6.6 6.7 %collective-permute-start.1 = (bf16[2,3,6,4,192]{4,3,2,1,0:T(4,128)(2,1)S(1)}, bf16[2,3,6,4,192]{4,3,2,1,0:T(4,128)(2,1)S(1)}, u32[]{:S(2)}, u32[]{:S(2)}) collective-permute-start(bf16[2,3,6,4,192]{4,3,2,1,0:T(4,128)(2,1)S(1)} %get-tuple-element.52), channel_id=1, source_target_pairs={{0,24},{1,25},{2,26},{3,27},{4,28},{5,29},{6,30},{7,31},{8,0},{9,1... | collective-permute-start | bytes 165896 | tf_op jit(solution)/shard_map/ppermute | solution.py:527
  9.0 4.3 %collective-permute-start.2 = (bf16[2,3,6,4,192]{4,3,2,1,0:T(4,128)(2,1)S(1)}, bf16[2,3,6,4,192]{4,3,2,1,0:T(4,128)(2,1)S(1)}, u32[]{:S(2)}, u32[]{:S(2)}) collective-permute-start(bf16[2,3,6,4,192]{4,3,2,1,0:T(4,128)(2,1)S(1)} %get-tuple-element.53), channel_id=1, source_target_pairs={{0,31},{1,24},{2,25},{3,26},{4,27},{5,28},{6,29},{7,30},{8,7},{9,0... | collective-permute-start | bytes 165896 | tf_op jit(solution)/shard_map/ppermute | solution.py:527
  18.4 1.5 %collective-permute-start.3 = (bf16[96,8,128]{2,1,0:T(8,128)(2,1)S(1)}, bf16[96,8,128]{2,1,0:T(8,128)(2,1)S(1)}, u32[]{:S(2)}, u32[]{:S(2)}) collective-permute-start(bf16[96,8,128]{2,1,0:T(8,128)(2,1)S(1)} %get-tuple-element.66), channel_id=1, source_target_pairs={{0,1},{1,0},{2,3},{3,2},{4,5},{5,4},{6,7},{7,6},{8,9},{9,8},{10,11... | collective-permute-start | bytes 589832 | tf_op jit(solution)/shard_map/ppermute | solution.py:517
  18.7 5.4 %collective-permute-start.4 = (bf16[27,8,128]{2,1,0:T(8,128)(2,1)S(1)}, bf16[27,8,128]{2,1,0:T(8,128)(2,1)S(1)}, u32[]{:S(2)}, u32[]{:S(2)}) collective-permute-start(bf16[27,8,128]{2,1,0:T(8,128)(2,1)S(1)} %get-tuple-element.73), channel_id=1, source_target_pairs={{0,1},{1,2},{2,3},{3,4},{4,5},{5,6},{6,7},{7,0},{8,9},{9,10},{10,1... | collective-permute-start | bytes 165896 | tf_op jit(solution)/shard_map/ppermute | solution.py:527
  19.9 4.2 %collective-permute-start.7 = (bf16[19,8,128]{2,1,0:T(8,128)(2,1)S(1)}, bf16[19,8,128]{2,1,0:T(8,128)(2,1)S(1)}, u32[]{:S(2)}, u32[]{:S(2)}) collective-permute-start(bf16[19,8,128]{2,1,0:T(8,128)(2,1)S(1)} %get-tuple-element.80), channel_id=1, source_target_pairs={{0,8},{8,0},{16,24},{24,16},{1,9},{9,1},{17,25},{25,17},{2,10},{10... | collective-permute-start | bytes 116744 | tf_op jit(solution)/shard_map/ppermute | solution.py:517
  21.5 4.4 %collective-permute-start.8 = (bf16[19,8,128]{2,1,0:T(8,128)(2,1)S(1)}, bf16[19,8,128]{2,1,0:T(8,128)(2,1)S(1)}, u32[]{:S(2)}, u32[]{:S(2)}) collective-permute-start(bf16[19,8,128]{2,1,0:T(8,128)(2,1)S(1)} %get-tuple-element.81), channel_id=1, source_target_pairs={{0,16},{8,24},{16,0},{24,8},{1,17},{9,25},{17,1},{25,9},{2,18},{10... | collective-permute-start | bytes 116744 | tf_op jit(solution)/shard_map/ppermute | solution.py:517
  22.2 4.9 %collective-permute-start.9 = (bf16[19,8,128]{2,1,0:T(8,128)(2,1)S(1)}, bf16[19,8,128]{2,1,0:T(8,128)(2,1)S(1)}, u32[]{:S(2)}, u32[]{:S(2)}) collective-permute-start(bf16[19,8,128]{2,1,0:T(8,128)(2,1)S(1)} %get-tuple-element.82), channel_id=1, source_target_pairs={{0,24},{8,16},{16,8},{24,0},{1,25},{9,17},{17,9},{25,1},{2,26},{10... | collective-permute-start | bytes 116744 | tf_op jit(solution)/shard_map/ppermute | solution.py:517
  27.1 6.7 %collective-permute-start.12 = (bf16[39,8,128]{2,1,0:T(8,128)(2,1)S(1)}, bf16[39,8,128]{2,1,0:T(8,128)(2,1)S(1)}, u32[]{:S(2)}, u32[]{:S(2)}) collective-permute-start(bf16[39,8,128]{2,1,0:T(8,128)(2,1)S(1)} %shard_map.141.refs_0_), channel_id=1, source_target_pairs={{0,6},{1,7},{2,4},{3,5},{4,2},{5,3},{6,0},{7,1},{8,14},{9,15},{10,... | collective-permute-start | bytes 239624 | tf_op jit(solution)/shard_map/ppermute | solution.py:517
  29.5 6.3 %collective-permute-start.11 = (bf16[39,8,128]{2,1,0:T(8,128)(2,1)S(1)}, bf16[39,8,128]{2,1,0:T(8,128)(2,1)S(1)}, u32[]{:S(2)}, u32[]{:S(2)}) collective-permute-start(bf16[39,8,128]{2,1,0:T(8,128)(2,1)S(1)} %shard_map.141.refs_0_), channel_id=1, source_target_pairs={{0,4},{1,5},{2,6},{3,7},{4,0},{5,1},{6,2},{7,3},{8,12},{9,13},{10,... | collective-permute-start | bytes 239624 | tf_op jit(solution)/shard_map/ppermute | solution.py:517
  29.5 6.3 %collective-permute-start.10 = (bf16[39,8,128]{2,1,0:T(8,128)(2,1)S(1)}, bf16[39,8,128]{2,1,0:T(8,128)(2,1)S(1)}, u32[]{:S(2)}, u32[]{:S(2)}) collective-permute-start(bf16[39,8,128]{2,1,0:T(8,128)(2,1)S(1)} %shard_map.141.refs_0_), channel_id=1, source_target_pairs={{0,2},{1,3},{2,0},{3,1},{4,6},{5,7},{6,4},{7,5},{8,10},{9,11},{10,... | collective-permute-start | bytes 239624 | tf_op jit(solution)/shard_map/ppermute | solution.py:517
  31.6 9.4 %collective-permute-start.5 = (bf16[27,8,128]{2,1,0:T(8,128)(2,1)S(1)}, bf16[27,8,128]{2,1,0:T(8,128)(2,1)S(1)}, u32[]{:S(2)}, u32[]{:S(2)}) collective-permute-start(bf16[27,8,128]{2,1,0:T(8,128)(2,1)S(1)} %get-tuple-element.75), channel_id=1, source_target_pairs={{0,8},{1,9},{2,10},{3,11},{4,12},{5,13},{6,14},{7,15},{8,16},{9,17... | collective-permute-start | bytes 165896 | tf_op jit(solution)/shard_map/ppermute | solution.py:527
  31.9 9.2 %collective-permute-start.6 = (bf16[27,8,128]{2,1,0:T(8,128)(2,1)S(1)}, bf16[27,8,128]{2,1,0:T(8,128)(2,1)S(1)}, u32[]{:S(2)}, u32[]{:S(2)}) collective-permute-start(bf16[27,8,128]{2,1,0:T(8,128)(2,1)S(1)} %get-tuple-element.76), channel_id=1, source_target_pairs={{0,9},{1,10},{2,11},{3,12},{4,13},{5,14},{6,15},{7,8},{8,17},{9,18... | collective-permute-start | bytes 165896 | tf_op jit(solution)/shard_map/ppermute | solution.py:527
  35.9 5.6 %collective-permute-start.15 = (bf16[19,8,128]{2,1,0:T(8,128)(2,1)S(1)}, bf16[19,8,128]{2,1,0:T(8,128)(2,1)S(1)}, u32[]{:S(2)}, u32[]{:S(2)}) collective-permute-start(bf16[19,8,128]{2,1,0:T(8,128)(2,1)S(1)} %get-tuple-element.84.refs_0_), channel_id=1, source_target_pairs={{0,24},{8,16},{16,8},{24,0},{1,25},{9,17},{17,9},{25,1},{2,26},{10... | collective-permute-start | bytes 116744 | tf_op jit(solution)/shard_map/ppermute | solution.py:517
  37.3 4.3 %collective-permute-start.14 = (bf16[19,8,128]{2,1,0:T(8,128)(2,1)S(1)}, bf16[19,8,128]{2,1,0:T(8,128)(2,1)S(1)}, u32[]{:S(2)}, u32[]{:S(2)}) collective-permute-start(bf16[19,8,128]{2,1,0:T(8,128)(2,1)S(1)} %get-tuple-element.84.refs_0_), channel_id=1, source_target_pairs={{0,16},{8,24},{16,0},{24,8},{1,17},{9,25},{17,1},{25,9},{2,18},{10... | collective-permute-start | bytes 116744 | tf_op jit(solution)/shard_map/ppermute | solution.py:517
  37.9 4.2 %collective-permute-start.13 = (bf16[19,8,128]{2,1,0:T(8,128)(2,1)S(1)}, bf16[19,8,128]{2,1,0:T(8,128)(2,1)S(1)}, u32[]{:S(2)}, u32[]{:S(2)}) collective-permute-start(bf16[19,8,128]{2,1,0:T(8,128)(2,1)S(1)} %get-tuple-element.84.refs_0_), channel_id=1, source_target_pairs={{0,8},{8,0},{16,24},{24,16},{1,9},{9,1},{17,25},{25,17},{2,10},{10... | collective-permute-start | bytes 116744 | tf_op jit(solution)/shard_map/ppermute | solution.py:517
  41.0 2.0 %collective-permute-start.20 = (bf16[8,3328]{1,0:T(8,128)(2,1)S(1)}, bf16[8,3328]{1,0:T(8,128)(2,1)S(1)}, u32[]{:S(2)}, u32[]{:S(2)}) collective-permute-start(bf16[8,3328]{1,0:T(8,128)(2,1)S(1)} %shard_map.143.refs_8_), channel_id=1, source_target_pairs={{0,1},{1,0},{2,3},{3,2},{4,5},{5,4},{6,7},{7,6},{8,9},{9,8},{10,11... | collective-permute-start | bytes 159752 | tf_op jit(solution)/shard_map/ppermute | solution.py:517
  41.0 1.9 %collective-permute-start.16 = (bf16[19,8,128]{2,1,0:T(8,128)(2,1)S(1)}, bf16[19,8,128]{2,1,0:T(8,128)(2,1)S(1)}, u32[]{:S(2)}, u32[]{:S(2)}) collective-permute-start(bf16[19,8,128]{2,1,0:T(8,128)(2,1)S(1)} %get-tuple-element.84.refs_0_), channel_id=1, source_target_pairs={{0,1},{1,0},{2,3},{3,2},{4,5},{5,4},{6,7},{7,6},{8,9},{9,8},{10,11... | collective-permute-start | bytes 116744 | tf_op jit(solution)/shard_map/ppermute | solution.py:517
  41.5 1.4 %collective-permute-start.19 = (bf16[19,8,128]{2,1,0:T(8,128)(2,1)S(1)}, bf16[19,8,128]{2,1,0:T(8,128)(2,1)S(1)}, u32[]{:S(2)}, u32[]{:S(2)}) collective-permute-start(bf16[19,8,128]{2,1,0:T(8,128)(2,1)S(1)} %collective-permute-done.15.refs_3_), channel_id=1, source_target_pairs={{0,1},{1,0},{2,3},{3,2},{4,5},{5,4},{6,7},{7,6},{8,9},{9,8},{10,11... | collective-permute-start | bytes 116744 | tf_op jit(solution)/shard_map/ppermute | solution.py:517
  41.6 1.3 %collective-permute-start.18 = (bf16[19,8,128]{2,1,0:T(8,128)(2,1)S(1)}, bf16[19,8,128]{2,1,0:T(8,128)(2,1)S(1)}, u32[]{:S(2)}, u32[]{:S(2)}) collective-permute-start(bf16[19,8,128]{2,1,0:T(8,128)(2,1)S(1)} %collective-permute-done.14.refs_2_), channel_id=1, source_target_pairs={{0,1},{1,0},{2,3},{3,2},{4,5},{5,4},{6,7},{7,6},{8,9},{9,8},{10,11... | collective-permute-start | bytes 116744 | tf_op jit(solution)/shard_map/ppermute | solution.py:517
  42.1 1.2 %collective-permute-start.17 = (bf16[19,8,128]{2,1,0:T(8,128)(2,1)S(1)}, bf16[19,8,128]{2,1,0:T(8,128)(2,1)S(1)}, u32[]{:S(2)}, u32[]{:S(2)}) collective-permute-start(bf16[19,8,128]{2,1,0:T(8,128)(2,1)S(1)} %collective-permute-done.13.refs_1_), channel_id=1, source_target_pairs={{0,1},{1,0},{2,3},{3,2},{4,5},{5,4},{6,7},{7,6},{8,9},{9,8},{10,11... | collective-permute-start | bytes 116744 | tf_op jit(solution)/shard_map/ppermute | solution.py:517
